TPU v7x, 128 devices: a whole 4x4x4 slice. The times are simulated.
128 devices in a mesh: row: 16 (over z, y), col: 8 (over x, core).
Axes of the slice: x: 4, y: 4, z: 4, core: 2. Of those that a mesh axis runs over, the one named last changes fastest.
Arguments:
- slc: float32 [2, 16, 1536, 6144], P(None, 'row', None, 'col'), may hold values from -6 to 6
- valid_rows: int32 [16, 2], replicated, may hold values from 0 to 1536, as said below
Outputs:
- linked: float32 [2, 16, 256, 2048], P(None, None, 'row', 'col')
Inputs may be any that keep to these rules, and one draw needn't show every extreme that they name: valid_rows[t, 0] is below 192 and valid_rows[t, 1] is above 1344; some date starts at row 0 and some date ends at row 1536.
All inputs are finite; a program needn't handle non-finite values.
Results may differ from a plain program's by a relative error of at most 0.00029.
Values sent between devices are 32-bit elements; how exact they have to be, the bound alone decides.
No kernel may reach another device: no remote copies, remote signals or barrier semaphores. Data moves between devices by JAX's collectives and lax.ppermute only.
A program may use at most 128 MiB of HBM per device.

v0:
```python
import jax
import jax.numpy as jnp
from jax import lax
from jax.sharding import PartitionSpec as P

ITERS = 10


coherence_floor = 20.0


def with_halo(shard, sides, width):
    for axis, dim in sides:
        size, length = (lax.axis_size(axis), shard.shape[dim])
        up = [(i, (i + 1) % size) for i in range(size - 1)]
        down = [(j, i) for i, j in up]
        last = lax.slice_in_dim(shard, length - width, length, axis=dim)
        leading = lax.slice_in_dim(shard, 0, width, axis=dim)
        before = lax.ppermute(last, axis, up)
        after = lax.ppermute(leading, axis, down)
        shard = jnp.concatenate([before, shard, after], axis=dim)
    return shard


def column_table(col_count):
    out_cols = (col_count - 2) // 3
    source = jnp.arange(col_count, dtype=jnp.int32)[:, None]
    target = jnp.arange(out_cols, dtype=jnp.int32)[None, :] * 3
    inside = (source >= target) & (source <= target + 4)
    return inside.astype(jnp.float32)


def pool_window(field, table):
    row_count = field.shape[-2]
    col_count = field.shape[-1]
    blocks = row_count // 6
    grouped = field.reshape(field.shape[:-2] + (blocks, 6, col_count))
    whole_block = jnp.sum(grouped, axis=-2)
    first_five = jnp.sum(grouped[..., 0:5, :], axis=-2)
    row_sum = whole_block[..., 0 : blocks - 1, :] + first_five[..., 1:, :]
    return jnp.dot(
        row_sum, table, precision=lax.Precision.HIGHEST, preferred_element_type=jnp.float32
    )


def covariance(padded):
    real_part = padded[0]
    imag_part = padded[1]
    table = column_table(padded.shape[-1])

    def one_date(pair):
        date_real, date_imag = pair
        prod_real = date_real[None] * real_part + date_imag[None] * imag_part
        prod_imag = date_imag[None] * real_part - date_real[None] * imag_part
        return (pool_window(prod_real, table), pool_window(prod_imag, table))

    return lax.map(one_date, (real_part, imag_part))


def phase_link(cov_real, cov_imag):
    count = cov_real.shape[0]
    index_all = jnp.arange(count)
    power = jnp.maximum(cov_real[index_all, index_all], coherence_floor)
    inv_root = 1.0 / jnp.sqrt(power)
    factor = inv_root[:, None] * inv_root[None, :]
    coh_real = cov_real * factor
    coh_imag = cov_imag * factor
    vec_real = jnp.full(cov_real.shape[1:], 0.25, jnp.float32)
    vec_imag = jnp.zeros(cov_real.shape[1:], jnp.float32)
    for iteration in range(ITERS):
        new_real = jnp.sum(coh_real * vec_real[None] - coh_imag * vec_imag[None], axis=1) + vec_real
        new_imag = jnp.sum(coh_real * vec_imag[None] + coh_imag * vec_real[None], axis=1) + vec_imag
        length = jnp.sqrt(jnp.sum(new_real * new_real + new_imag * new_imag, axis=0))
        vec_real = new_real / length[None]
        vec_imag = new_imag / length[None]
    return jnp.stack([vec_real, vec_imag])


def local(slc, valid_rows):
    num_parts, dates_here, full_rows, col_count = slc.shape
    first_date = lax.axis_index("row") * dates_here
    bounds = lax.dynamic_slice_in_dim(valid_rows, first_date, dates_here, 0)
    row_index = jnp.arange(full_rows, dtype=jnp.int32)[None, :]
    keep_mask = (row_index >= bounds[:, 0:1]) & (row_index < bounds[:, 1:2])
    masked = slc * keep_mask[None, :, :, None].astype(jnp.float32)
    tile_data = lax.all_to_all(masked, "row", split_axis=2, concat_axis=1, tiled=True)
    tile_data = with_halo(tile_data, (("row", 2),), 3)
    padded = with_halo(tile_data, (("col", 3),), 1)
    cov_real, cov_imag = covariance(padded)
    return phase_link(cov_real, cov_imag)


def solution(mesh):
    return jax.shard_map(
        local,
        mesh=mesh,
        in_specs=(P(None, "row", None, "col"), P()),
        out_specs=P(None, None, "row", "col"),
        check_vma=False,
    )
```

profile of v0, /device:TPU:1, one launch (start us, length us, event | category | flops | bytes accessed | tf_op | source)
XLA Modules:
  0.0 500.4 jit_solution(15684050967178603140)
XLA Ops:
  7.1 29.1 %copy.43 = f32[2,1,1536,768]{3,0,1,2:T(2,128)S(1)} copy(f32[2,1,1536,768]{3,2,1,0:T(8,128)S(1)} %broadcast_multiply_fusion) | data formatting | bytes 18874368 | tf_op jit(solution)/shard_map/mul | solution.py:85
  36.2 114.4 %all_to_all.12 = f32[2,1,1536,768]{3,0,1,2:T(2,128)S(1)} all-to-all(f32[2,1,1536,768]{3,0,1,2:T(2,128)S(1)} %copy.43), channel_id=1, replica_groups=mesh['row'=16,'col'=8] {'row'}, dimensions={2} | all-to-all | bytes 18874368 | tf_op jit(solution)/shard_map/all_to_all | solution.py:86
  155.0 5.0 %collective-permute-done = f32[2,16,3,768]{3,2,1,0:T(4,128)S(1)} collective-permute-done((f32[2,16,3,768]{3,2,1,0:T(4,128)S(1)}, f32[2,16,3,768]{3,2,1,0:T(4,128)S(1)}, u32[]{:S(2)}, u32[]{:S(2)}) %collective-permute-start) | collective-permute-done | bytes 294944 | tf_op jit(solution)/shard_map/ppermute | solution.py:19
  165.2 6.3 %collective-permute-start.2 = (f32[2,16,102,1]{2,1,3,0:T(8,128)S(1)}, f32[2,16,102,1]{2,1,3,0:T(8,128)S(1)}, u32[]{:S(2)}, u32[]{:S(2)}) collective-permute-start(f32[2,16,102,1]{2,1,3,0:T(8,128)S(1)} %copy.45), channel_id=1, source_target_pairs={{0,1},{1,2},{2,3},{3,4},{4,5},{5,6},{6,7},{8,9},{9,10},{10,11},{11... | collective-permute-start | bytes 39176 | tf_op jit(solution)/shard_map/ppermute | solution.py:19
  177.7 11.7 %pad_maximum_fusion = f32[2,16,102,770]{3,2,1,0:T(8,128)} fusion(f32[2,16,102,1]{3,2,1,0:T(8,128)S(1)} %copy.48, f32[2,16,3,768]{3,2,1,0:T(4,128)} %copy-done.4, f32[2,16,96,768]{3,2,1,0:T(8,128)} %bitcast.194, f32[2,16,3,768]{3,2,1,0:T(4,128)} %copy-done.3, f32[2,16,102,1]{3,2,1,0:T(8,128)S(1)} %copy.47), kind=kLoop, calls=%fused_computation.27 | loop fusion | flops 10053120 | bytes 20106240 | tf_op jit(solution)/shard_map/concatenate | solution.py:21
  189.4 7.7 %slice_bitcast_fusion = (f32[16,102,770]{2,1,0:T(8,128)S(1)}, f32[16,102,770]{2,1,0:T(8,128)}) fusion(f32[2,16,102,770]{3,2,1,0:T(8,128)} %pad_maximum_fusion), kind=kLoop, calls=%fused_computation.30 | loop fusion | bytes 20106240 | tf_op jit(solution)/shard_map/squeeze | solution.py:48
  197.1 6.3 %copy.49 = f32[16,102,770]{2,0,1:T(8,128)} copy(f32[16,102,770]{2,1,0:T(8,128)} %get-tuple-element.174) | data formatting | bytes 10053120
  207.1 242.0 %while.15 = (s32[]{:T(128)}, f32[16,16,16,256]{3,1,2,0:T(8,128)}, f32[16,16,16,256]{3,1,2,0:T(8,128)}, f32[16,102,770]{2,0,1:T(8,128)}, f32[16,102,770]{2,0,1:T(8,128)}, /*index=5*/s32[256]{0:T(256)S(1)}, s32[256]{0:T(256)S(1)}) while((s32[]{:T(128)}, f32[16,16,16,256]{3,1,2,0:T(8,128)}, ...), condition=%wide.region_5.6_spmd.clone.clone.clone, body=%wide.region_0.5_spmd.clone.clone.sunk.clone | while | flops 1224386304 | bytes 39175984 | solution.py:57
  207.1 4.8 dynamic-slice_reduce_fusion.4
  212.0 5.8 %fusion.59 = (f32[16,17,770]{2,0,1:T(8,128)S(1)}, f32[16,17,6,770]{3,0,2,1:T(8,128)S(1)}, f32[16,17,770]{2,0,1:T(8,128)S(1)}, f32[16,17,6,770]{3,0,2,1:T(8,128)S(1)}) fusion(f32[16,17,6,770]{3,0,2,1:T(8,128)} %bitcast.191, f32[17,6,770]{2,1,0:T(8,128)S(1)} %mul.646, f32[16,17,6,770]{3,0,2,1:T(8,128)} %bitcast.190, f32[17,6,770]{2,1,0:T(8,128)S(1)} %mul.647), kind=kLoop, calls=%fused_computation.126.clone.1.clone | loop fusion | flops 9634240 | bytes 22410080 | tf_op jit(solution)/shard_map/while/body/eval_jaxpr/reduce_sum | solution.py:38
  222.2 4.8 dynamic-slice_reduce_fusion.4
  227.2 5.8 %fusion.59 = (f32[16,17,770]{2,0,1:T(8,128)S(1)}, f32[16,17,6,770]{3,0,2,1:T(8,128)S(1)}, f32[16,17,770]{2,0,1:T(8,128)S(1)}, f32[16,17,6,770]{3,0,2,1:T(8,128)S(1)}) fusion(f32[16,17,6,770]{3,0,2,1:T(8,128)} %bitcast.191, f32[17,6,770]{2,1,0:T(8,128)S(1)} %mul.646, f32[16,17,6,770]{3,0,2,1:T(8,128)} %bitcast.190, f32[17,6,770]{2,1,0:T(8,128)S(1)} %mul.647), kind=kLoop, calls=%fused_computation.126.clone.1.clone | loop fusion | flops 9634240 | bytes 22410080 | tf_op jit(solution)/shard_map/while/body/eval_jaxpr/reduce_sum | solution.py:38
  242.3 5.8 %fusion.59 = (f32[16,17,770]{2,0,1:T(8,128)S(1)}, f32[16,17,6,770]{3,0,2,1:T(8,128)S(1)}, f32[16,17,770]{2,0,1:T(8,128)S(1)}, f32[16,17,6,770]{3,0,2,1:T(8,128)S(1)}) fusion(f32[16,17,6,770]{3,0,2,1:T(8,128)} %bitcast.191, f32[17,6,770]{2,1,0:T(8,128)S(1)} %mul.646, f32[16,17,6,770]{3,0,2,1:T(8,128)} %bitcast.190, f32[17,6,770]{2,1,0:T(8,128)S(1)} %mul.647), kind=kLoop, calls=%fused_computation.126.clone.1.clone | loop fusion | flops 9634240 | bytes 22410080 | tf_op jit(solution)/shard_map/while/body/eval_jaxpr/reduce_sum | solution.py:38
  257.4 5.8 %fusion.59 = (f32[16,17,770]{2,0,1:T(8,128)S(1)}, f32[16,17,6,770]{3,0,2,1:T(8,128)S(1)}, f32[16,17,770]{2,0,1:T(8,128)S(1)}, f32[16,17,6,770]{3,0,2,1:T(8,128)S(1)}) fusion(f32[16,17,6,770]{3,0,2,1:T(8,128)} %bitcast.191, f32[17,6,770]{2,1,0:T(8,128)S(1)} %mul.646, f32[16,17,6,770]{3,0,2,1:T(8,128)} %bitcast.190, f32[17,6,770]{2,1,0:T(8,128)S(1)} %mul.647), kind=kLoop, calls=%fused_computation.126.clone.1.clone | loop fusion | flops 9634240 | bytes 22410080 | tf_op jit(solution)/shard_map/while/body/eval_jaxpr/reduce_sum | solution.py:38
  267.6 4.8 dynamic-slice_reduce_fusion.4
  272.5 5.8 %fusion.59 = (f32[16,17,770]{2,0,1:T(8,128)S(1)}, f32[16,17,6,770]{3,0,2,1:T(8,128)S(1)}, f32[16,17,770]{2,0,1:T(8,128)S(1)}, f32[16,17,6,770]{3,0,2,1:T(8,128)S(1)}) fusion(f32[16,17,6,770]{3,0,2,1:T(8,128)} %bitcast.191, f32[17,6,770]{2,1,0:T(8,128)S(1)} %mul.646, f32[16,17,6,770]{3,0,2,1:T(8,128)} %bitcast.190, f32[17,6,770]{2,1,0:T(8,128)S(1)} %mul.647), kind=kLoop, calls=%fused_computation.126.clone.1.clone | loop fusion | flops 9634240 | bytes 22410080 | tf_op jit(solution)/shard_map/while/body/eval_jaxpr/reduce_sum | solution.py:38
  287.6 5.8 %fusion.59 = (f32[16,17,770]{2,0,1:T(8,128)S(1)}, f32[16,17,6,770]{3,0,2,1:T(8,128)S(1)}, f32[16,17,770]{2,0,1:T(8,128)S(1)}, f32[16,17,6,770]{3,0,2,1:T(8,128)S(1)}) fusion(f32[16,17,6,770]{3,0,2,1:T(8,128)} %bitcast.191, f32[17,6,770]{2,1,0:T(8,128)S(1)} %mul.646, f32[16,17,6,770]{3,0,2,1:T(8,128)} %bitcast.190, f32[17,6,770]{2,1,0:T(8,128)S(1)} %mul.647), kind=kLoop, calls=%fused_computation.126.clone.1.clone | loop fusion | flops 9634240 | bytes 22410080 | tf_op jit(solution)/shard_map/while/body/eval_jaxpr/reduce_sum | solution.py:38
  302.7 5.8 %fusion.59 = (f32[16,17,770]{2,0,1:T(8,128)S(1)}, f32[16,17,6,770]{3,0,2,1:T(8,128)S(1)}, f32[16,17,770]{2,0,1:T(8,128)S(1)}, f32[16,17,6,770]{3,0,2,1:T(8,128)S(1)}) fusion(f32[16,17,6,770]{3,0,2,1:T(8,128)} %bitcast.191, f32[17,6,770]{2,1,0:T(8,128)S(1)} %mul.646, f32[16,17,6,770]{3,0,2,1:T(8,128)} %bitcast.190, f32[17,6,770]{2,1,0:T(8,128)S(1)} %mul.647), kind=kLoop, calls=%fused_computation.126.clone.1.clone | loop fusion | flops 9634240 | bytes 22410080 | tf_op jit(solution)/shard_map/while/body/eval_jaxpr/reduce_sum | solution.py:38
  312.9 4.8 dynamic-slice_reduce_fusion.4
  317.8 5.8 %fusion.59 = (f32[16,17,770]{2,0,1:T(8,128)S(1)}, f32[16,17,6,770]{3,0,2,1:T(8,128)S(1)}, f32[16,17,770]{2,0,1:T(8,128)S(1)}, f32[16,17,6,770]{3,0,2,1:T(8,128)S(1)}) fusion(f32[16,17,6,770]{3,0,2,1:T(8,128)} %bitcast.191, f32[17,6,770]{2,1,0:T(8,128)S(1)} %mul.646, f32[16,17,6,770]{3,0,2,1:T(8,128)} %bitcast.190, f32[17,6,770]{2,1,0:T(8,128)S(1)} %mul.647), kind=kLoop, calls=%fused_computation.126.clone.1.clone | loop fusion | flops 9634240 | bytes 22410080 | tf_op jit(solution)/shard_map/while/body/eval_jaxpr/reduce_sum | solution.py:38
  328.0 4.8 dynamic-slice_reduce_fusion.4
  332.9 5.8 %fusion.59 = (f32[16,17,770]{2,0,1:T(8,128)S(1)}, f32[16,17,6,770]{3,0,2,1:T(8,128)S(1)}, f32[16,17,770]{2,0,1:T(8,128)S(1)}, f32[16,17,6,770]{3,0,2,1:T(8,128)S(1)}) fusion(f32[16,17,6,770]{3,0,2,1:T(8,128)} %bitcast.191, f32[17,6,770]{2,1,0:T(8,128)S(1)} %mul.646, f32[16,17,6,770]{3,0,2,1:T(8,128)} %bitcast.190, f32[17,6,770]{2,1,0:T(8,128)S(1)} %mul.647), kind=kLoop, calls=%fused_computation.126.clone.1.clone | loop fusion | flops 9634240 | bytes 22410080 | tf_op jit(solution)/shard_map/while/body/eval_jaxpr/reduce_sum | solution.py:38
  348.0 5.8 %fusion.59 = (f32[16,17,770]{2,0,1:T(8,128)S(1)}, f32[16,17,6,770]{3,0,2,1:T(8,128)S(1)}, f32[16,17,770]{2,0,1:T(8,128)S(1)}, f32[16,17,6,770]{3,0,2,1:T(8,128)S(1)}) fusion(f32[16,17,6,770]{3,0,2,1:T(8,128)} %bitcast.191, f32[17,6,770]{2,1,0:T(8,128)S(1)} %mul.646, f32[16,17,6,770]{3,0,2,1:T(8,128)} %bitcast.190, f32[17,6,770]{2,1,0:T(8,128)S(1)} %mul.647), kind=kLoop, calls=%fused_computation.126.clone.1.clone | loop fusion | flops 9634240 | bytes 22410080 | tf_op jit(solution)/shard_map/while/body/eval_jaxpr/reduce_sum | solution.py:38
  363.2 5.8 %fusion.59 = (f32[16,17,770]{2,0,1:T(8,128)S(1)}, f32[16,17,6,770]{3,0,2,1:T(8,128)S(1)}, f32[16,17,770]{2,0,1:T(8,128)S(1)}, f32[16,17,6,770]{3,0,2,1:T(8,128)S(1)}) fusion(f32[16,17,6,770]{3,0,2,1:T(8,128)} %bitcast.191, f32[17,6,770]{2,1,0:T(8,128)S(1)} %mul.646, f32[16,17,6,770]{3,0,2,1:T(8,128)} %bitcast.190, f32[17,6,770]{2,1,0:T(8,128)S(1)} %mul.647), kind=kLoop, calls=%fused_computation.126.clone.1.clone | loop fusion | flops 9634240 | bytes 22410080 | tf_op jit(solution)/shard_map/while/body/eval_jaxpr/reduce_sum | solution.py:38
  378.3 5.8 %fusion.59 = (f32[16,17,770]{2,0,1:T(8,128)S(1)}, f32[16,17,6,770]{3,0,2,1:T(8,128)S(1)}, f32[16,17,770]{2,0,1:T(8,128)S(1)}, f32[16,17,6,770]{3,0,2,1:T(8,128)S(1)}) fusion(f32[16,17,6,770]{3,0,2,1:T(8,128)} %bitcast.191, f32[17,6,770]{2,1,0:T(8,128)S(1)} %mul.646, f32[16,17,6,770]{3,0,2,1:T(8,128)} %bitcast.190, f32[17,6,770]{2,1,0:T(8,128)S(1)} %mul.647), kind=kLoop, calls=%fused_computation.126.clone.1.clone | loop fusion | flops 9634240 | bytes 22410080 | tf_op jit(solution)/shard_map/while/body/eval_jaxpr/reduce_sum | solution.py:38
  393.4 5.8 %fusion.59 = (f32[16,17,770]{2,0,1:T(8,128)S(1)}, f32[16,17,6,770]{3,0,2,1:T(8,128)S(1)}, f32[16,17,770]{2,0,1:T(8,128)S(1)}, f32[16,17,6,770]{3,0,2,1:T(8,128)S(1)}) fusion(f32[16,17,6,770]{3,0,2,1:T(8,128)} %bitcast.191, f32[17,6,770]{2,1,0:T(8,128)S(1)} %mul.646, f32[16,17,6,770]{3,0,2,1:T(8,128)} %bitcast.190, f32[17,6,770]{2,1,0:T(8,128)S(1)} %mul.647), kind=kLoop, calls=%fused_computation.126.clone.1.clone | loop fusion | flops 9634240 | bytes 22410080 | tf_op jit(solution)/shard_map/while/body/eval_jaxpr/reduce_sum | solution.py:38
  403.5 4.8 dynamic-slice_reduce_fusion.4
  408.5 5.8 %fusion.59 = (f32[16,17,770]{2,0,1:T(8,128)S(1)}, f32[16,17,6,770]{3,0,2,1:T(8,128)S(1)}, f32[16,17,770]{2,0,1:T(8,128)S(1)}, f32[16,17,6,770]{3,0,2,1:T(8,128)S(1)}) fusion(f32[16,17,6,770]{3,0,2,1:T(8,128)} %bitcast.191, f32[17,6,770]{2,1,0:T(8,128)S(1)} %mul.646, f32[16,17,6,770]{3,0,2,1:T(8,128)} %bitcast.190, f32[17,6,770]{2,1,0:T(8,128)S(1)} %mul.647), kind=kLoop, calls=%fused_computation.126.clone.1.clone | loop fusion | flops 9634240 | bytes 22410080 | tf_op jit(solution)/shard_map/while/body/eval_jaxpr/reduce_sum | solution.py:38
  423.6 5.8 %fusion.59 = (f32[16,17,770]{2,0,1:T(8,128)S(1)}, f32[16,17,6,770]{3,0,2,1:T(8,128)S(1)}, f32[16,17,770]{2,0,1:T(8,128)S(1)}, f32[16,17,6,770]{3,0,2,1:T(8,128)S(1)}) fusion(f32[16,17,6,770]{3,0,2,1:T(8,128)} %bitcast.191, f32[17,6,770]{2,1,0:T(8,128)S(1)} %mul.646, f32[16,17,6,770]{3,0,2,1:T(8,128)} %bitcast.190, f32[17,6,770]{2,1,0:T(8,128)S(1)} %mul.647), kind=kLoop, calls=%fused_computation.126.clone.1.clone | loop fusion | flops 9634240 | bytes 22410080 | tf_op jit(solution)/shard_map/while/body/eval_jaxpr/reduce_sum | solution.py:38
  438.7 5.8 %fusion.59 = (f32[16,17,770]{2,0,1:T(8,128)S(1)}, f32[16,17,6,770]{3,0,2,1:T(8,128)S(1)}, f32[16,17,770]{2,0,1:T(8,128)S(1)}, f32[16,17,6,770]{3,0,2,1:T(8,128)S(1)}) fusion(f32[16,17,6,770]{3,0,2,1:T(8,128)} %bitcast.191, f32[17,6,770]{2,1,0:T(8,128)S(1)} %mul.646, f32[16,17,6,770]{3,0,2,1:T(8,128)} %bitcast.190, f32[17,6,770]{2,1,0:T(8,128)S(1)} %mul.647), kind=kLoop, calls=%fused_computation.126.clone.1.clone | loop fusion | flops 9634240 | bytes 22410080 | tf_op jit(solution)/shard_map/while/body/eval_jaxpr/reduce_sum | solution.py:38
  449.1 7.4 %copy.51 = f32[16,16,16,256]{3,2,1,0:T(8,128)} copy(f32[16,16,16,256]{3,1,2,0:T(8,128)} %get-tuple-element.41) | data formatting | bytes 8388608 | tf_op jit(solution)/shard_map/while | solution.py:57
  459.4 5.6 %subtract_reduce_fusion.9 = (f32[16,16,256]{2,1,0:T(8,128)S(1)}, f32[16,16,256]{2,1,0:T(8,128)S(1)}, f32[16,16,16,256]{3,1,2,0:T(8,128)S(1)}, f32[16,16,16,256]{3,1,2,0:T(8,128)S(1)}) fusion(f32[16,16,16,256]{3,1,2,0:T(8,128)} %get-tuple-element.41, f32[16,16,256]{2,0,1:T(8,128)S(1)} %copy.52, f32[16,16,256]{2,1,0:T(8,128)S(1)} %maximum_rsqrt_fusion, ...), kind=kLoop, calls=%fused_computation.52 | loop fusion | flops 11403264 | bytes 17825792 | tf_op jit(solution)/shard_map/reduce_sum | solution.py:71
  (200 shorter events, 183.2 us)
Async XLA Ops:
  0.0 0.7 copy-start
  151.4 12.5 %copy-start.2 = (f32[2,1,1536,768]{3,2,0,1:T(8,128)}, f32[2,1,1536,768]{3,2,0,1:T(8,128)S(1)}, u32[]{:S(2)}) copy-start(f32[2,1,1536,768]{3,2,0,1:T(8,128)S(1)} %copy.44) | copy-start | bytes 28311556
  151.5 8.5 %collective-permute-start = (f32[2,16,3,768]{3,2,1,0:T(4,128)S(1)}, f32[2,16,3,768]{3,2,1,0:T(4,128)S(1)}, u32[]{:S(2)}, u32[]{:S(2)}) collective-permute-start(f32[2,16,3,768]{3,2,1,0:T(4,128)S(1)} %get-tuple-element.177), channel_id=1, source_target_pairs={{0,8},{8,16},{16,24},{24,32},{32,40},{40,48},{48,56},{56,64},{64,7... | collective-permute-start | bytes 884744 | tf_op jit(solution)/shard_map/ppermute | solution.py:19
  153.7 10.2 %collective-permute-start.1 = (f32[2,16,3,768]{3,2,1,0:T(4,128)S(1)}, f32[2,16,3,768]{3,2,1,0:T(4,128)S(1)}, u32[]{:S(2)}, u32[]{:S(2)}) collective-permute-start(f32[2,16,3,768]{3,2,1,0:T(4,128)S(1)} %get-tuple-element.178), channel_id=1, source_target_pairs={{8,0},{16,8},{24,16},{32,24},{40,32},{48,40},{56,48},{64,56},{72,6... | collective-permute-start | bytes 884744 | tf_op jit(solution)/shard_map/ppermute | solution.py:20
  160.0 4.5 copy-start.3
  163.9 0.7 copy-start.4
  165.2 9.3 %collective-permute-start.2 = (f32[2,16,102,1]{2,1,3,0:T(8,128)S(1)}, f32[2,16,102,1]{2,1,3,0:T(8,128)S(1)}, u32[]{:S(2)}, u32[]{:S(2)}) collective-permute-start(f32[2,16,102,1]{2,1,3,0:T(8,128)S(1)} %copy.45), channel_id=1, source_target_pairs={{0,1},{1,2},{2,3},{3,4},{4,5},{5,6},{6,7},{8,9},{9,10},{10,11},{11... | collective-permute-start | bytes 39176 | tf_op jit(solution)/shard_map/ppermute | solution.py:19
  172.0 5.1 %collective-permute-start.3 = (f32[2,16,102,1]{2,1,3,0:T(8,128)S(1)}, f32[2,16,102,1]{2,1,3,0:T(8,128)S(1)}, u32[]{:S(2)}, u32[]{:S(2)}) collective-permute-start(f32[2,16,102,1]{2,1,3,0:T(8,128)S(1)} %copy.46), channel_id=1, source_target_pairs={{1,0},{2,1},{3,2},{4,3},{5,4},{6,5},{7,6},{9,8},{10,9},{11,10},{12... | collective-permute-start | bytes 39176 | tf_op jit(solution)/shard_map/ppermute | solution.py:20
  495.4 4.8 copy-start.1
where the time goes:
time: 504 us; the launch traced here: 500 us
  other arithmetic  159 us (32%)
  local copies, waits for them, and re-layouts  144 us (29%)
  blocking collectives  114 us (23%)
  matrix products  58.7 us (12%)
  starting transfers between devices  12.1 us (2%)
  waiting for transfers between devices  10.8 us (2%)
    all_to_all x1, blocking collectives, local(): lax.all_to_all(masked, 'row', split_axis=2, concat_axis=1, tiled=True)  114 us
    reduce_sum x16, other arithmetic, pool_window(): whole_block = jnp.sum(grouped, axis=-2)  93.2 us
    dynamic_slice x16, local copies, waits for them, and re-layouts, covariance(): return lax.map(one_date, (real_part, imag_part))  77.2 us
    dot_general x32, matrix products, pool_window(): jnp.dot(row_sum, table, precision=lax.Precision.HIGHEST, preferred_elemen...  58.7 us
    reduce_sum x10, other arithmetic, phase_link(): jnp.sum(coh_real * vec_real[None] - coh_imag * vec_imag[None], axis=1)  34.3 us
    mul x1, local copies, waits for them, and re-layouts, local(): masked = slc * keep_mask[None, :, :, None].astype(jnp.float32)  29.1 us
    concatenate x1, other arithmetic, with_halo(): shard = jnp.concatenate([before, shard, after], axis=dim)  11.7 us
    unnamed x12, local copies, waits for them, and re-layouts  10.7 us
  transfers between devices with their start and end apart: 4, of which 3 were waited for; matrix products, arithmetic and copies ran while one was open for 0% of the time, Pallas kernels for 0%

commit v1 on v0

v1 whole, which is shorter than its diff:
```python
import functools

import jax
import jax.numpy as jnp
import numpy as np
from jax import lax
from jax.experimental import pallas as pl
from jax.experimental.pallas import tpu as pltpu
from jax.sharding import PartitionSpec as P

ITERS = 10
FLOOR = 20.0
DATES = 16
TILES = 16
COLS = 768
OUT_COLS = 256
BLOCKS = 16
TILE_ROWS = 6 * BLOCKS
MSG_ROWS = 208
HALO_ROW = 192
EDGE_ROW = 202
GROUP = 4
PAIRS = [(t, u) for t in range(DATES) for u in range(t + 1, DATES)]
PAIR_AT = {pair: i for i, pair in enumerate(PAIRS)}
FIELDS = DATES + 2 * len(PAIRS)
CHUNK = 512
VMEM_LIMIT = 56 * 1024 * 1024


def column_tables():
    source = np.arange(COLS)[:, None]
    target = 3 * np.arange(OUT_COLS)[None, :]
    main = ((source >= target - 1) & (source <= target + 3)).astype(np.float32)
    row = np.arange(128)[:, None]
    lane = np.arange(128)[None, :]
    pool = np.zeros((2, 128, 128), np.float32)
    for side in range(2):
        block = lane - 16 * side
        inside = (block >= 0) & (block < 16) & (row >= 6 * block) & (row <= 6 * block + 10)
        pool[side] = inside
    edge = np.zeros((128, OUT_COLS), np.float32)
    edge[0:16, 0] = 1.0
    edge[16:32, OUT_COLS - 1] = 1.0
    return main, pool, edge


def edge_kernel(valid_ref, left_ref, right_ref, first_ref, last_ref):
    me = lax.axis_index("row")
    low, high = valid_ref[me, 0], valid_ref[me, 1]
    lane = lax.broadcasted_iota(jnp.int32, (8, 128), 1)
    row = lax.broadcasted_iota(jnp.int32, (1, 1536), 1)
    keep = (row >= low) & (row < high)
    for ref, pick, out in ((left_ref, 0, first_ref), (right_ref, 127, last_ref)):
        one = jnp.where(lane == pick, 1.0, 0.0)
        for part in range(2):
            column = lax.dot_general(
                one, ref[part, 0], (((1,), (1,)), ((), ())),
                precision=lax.Precision.HIGHEST, preferred_element_type=jnp.float32,
            )
            out[part : part + 1, :] = jnp.where(keep, column[0:1, :], 0.0)


def edge_columns(slc, valid_rows):
    shape = jax.ShapeDtypeStruct((2, 1536), jnp.float32)
    return pl.pallas_call(
        edge_kernel,
        grid=(1,),
        in_specs=[
            pl.BlockSpec(memory_space=pltpu.SMEM),
            pl.BlockSpec((2, 1, 1536, 128), lambda i: (0, 0, 0, 0)),
            pl.BlockSpec((2, 1, 1536, 128), lambda i: (0, 0, 0, COLS // 128 - 1)),
        ],
        out_specs=[pl.BlockSpec((2, 1536), lambda i: (0, 0))] * 2,
        out_shape=[shape, shape],
        compiler_params=pltpu.CompilerParams(vmem_limit_bytes=VMEM_LIMIT),
        name="edge_columns",
    )(valid_rows, slc, slc)


def pack_kernel(valid_ref, before_ref, tile_ref, after_ref, out_ref, rows_ref):
    me = lax.axis_index("row")
    step = pl.program_id(0)
    low, high = valid_ref[me, 0], valid_ref[me, 1]
    span = GROUP * TILE_ROWS

    def masked(ref, start, count):
        row = lax.broadcasted_iota(jnp.int32, (count, COLS), 0) + (step * span + start)
        keep = (row >= low) & (row < high)
        for part in range(2):
            value = jnp.where(keep, ref[part, 0], 0.0)
            for lt in range(COLS // 128):
                rows_ref[part, lt, pl.ds(start + 8, count), :] = value[:, lt * 128 : lt * 128 + 128]

    masked(before_ref, -8, 8)
    masked(tile_ref, 0, span)
    masked(after_ref, span, 8)
    for tile in range(GROUP):
        base = 5 + tile * TILE_ROWS
        for part in range(2):
            for phase in range(6):
                for half in range(2):
                    at = part * 96 + phase * 16 + half * 8
                    for lt in range(COLS // 128):
                        lanes = pl.ds(lt * 128, 128)
                        out_ref[tile, pl.ds(at, 8), lanes] = rows_ref[
                            part, lt, pl.ds(base + 6 * half + phase, 8, stride=12), :
                        ]
            for lt in range(COLS // 128):
                out_ref[tile, pl.ds(HALO_ROW + 5 * part, 5), pl.ds(lt * 128, 128)] = rows_ref[
                    part, lt, pl.ds(base + TILE_ROWS, 5), :
                ]
        out_ref[tile, pl.ds(EDGE_ROW, 6), :] = jnp.zeros((6, COLS), jnp.float32)


def pack(slc, valid_rows):
    span = GROUP * TILE_ROWS // 8
    return pl.pallas_call(
        pack_kernel,
        grid=(TILES // GROUP,),
        in_specs=[
            pl.BlockSpec(memory_space=pltpu.SMEM),
            pl.BlockSpec((2, 1, 8, COLS), lambda i: (0, 0, jnp.maximum(i * span - 1, 0), 0)),
            pl.BlockSpec((2, 1, GROUP * TILE_ROWS, COLS), lambda i: (0, 0, i, 0)),
            pl.BlockSpec((2, 1, 8, COLS), lambda i: (0, 0, jnp.minimum(i * span + span, 191), 0)),
        ],
        out_specs=pl.BlockSpec((GROUP, MSG_ROWS, COLS), lambda i: (i, 0, 0)),
        out_shape=jax.ShapeDtypeStruct((TILES, MSG_ROWS, COLS), jnp.float32),
        scratch_shapes=[pltpu.VMEM((2, COLS // 128, GROUP * TILE_ROWS + 16, 128), jnp.float32)],
        compiler_params=pltpu.CompilerParams(vmem_limit_bytes=VMEM_LIMIT),
        cost_estimate=pl.CostEstimate(flops=10**6, bytes_accessed=2 * 10**7, transcendentals=0),
        name="pack",
    )(valid_rows, slc, slc, slc)


def insert_kernel(left_ref, right_ref, in_ref, out_ref, wide_ref):
    out_ref[...] = in_ref[...]
    wide_ref[...] = jnp.zeros_like(wide_ref)
    for side, ref in enumerate((left_ref, right_ref)):
        wide_ref[2 * side : 2 * side + 2, 128 : 128 + 1536] = ref[...]
    for tile in range(TILES):
        start = 128 + tile * TILE_ROWS - 3
        for row in range(4):
            out_ref[tile, EDGE_ROW % 8 : EDGE_ROW % 8 + 1, row * 128 : row * 128 + 128] = wide_ref[
                row : row + 1, start : start + 128
            ]


def insert_edges(left, right, message):
    spec = pl.BlockSpec((TILES, 8, COLS), lambda i: (0, EDGE_ROW // 8, 0))
    column = pl.BlockSpec((2, 1536), lambda i: (0, 0))
    return pl.pallas_call(
        insert_kernel,
        grid=(1,),
        in_specs=[column, column, spec],
        out_specs=spec,
        out_shape=jax.ShapeDtypeStruct(message.shape, message.dtype),
        input_output_aliases={2: 0},
        scratch_shapes=[pltpu.VMEM((8, 1920), jnp.float32)],
        compiler_params=pltpu.CompilerParams(vmem_limit_bytes=VMEM_LIMIT),
        name="insert_edges",
    )(left, right, message)


def split(x):
    high = x.astype(jnp.bfloat16)
    return high, (x - high.astype(jnp.float32)).astype(jnp.bfloat16)


def field_of(t, u):
    return t if t == u else DATES + 2 * PAIR_AT[t, u]


def cross_products(data, t_part, u_tile, lanes, rows):
    real = imag = None
    for re_row, im_row in rows:
        a_t = data[re_row, pl.ds(t_part, 1), lanes]
        b_t = data[im_row, pl.ds(t_part, 1), lanes]
        a_u = data[re_row, pl.ds(u_tile * 8, 8), lanes]
        b_u = data[im_row, pl.ds(u_tile * 8, 8), lanes]
        re = a_t * a_u + b_t * b_u
        im = b_t * a_u - a_t * b_u
        real = re if real is None else real + re
        imag = im if imag is None else imag + im
    return real, imag


def main_products(msg, sums, lhs, lt):
    lanes = pl.ds(pl.multiple_of(lt * 128, 128), 128)
    last = lax.broadcasted_iota(jnp.int32, (8, 128), 0) == 7

    def rows_at(phase, half):
        return pl.ds(phase * 16 + half * 8, 8)

    def load(kind, date, phase, half):
        if kind == "a":
            return msg[date, pl.ds(phase * 16 + half * 8, 8), lanes]
        if kind == "b":
            return msg[date, pl.ds(96 + phase * 16 + half * 8, 8), lanes]
        base = 0 if kind == "s" else 96
        return sums[date, pl.ds(base + phase * 16 + half * 8, 8), lanes]

    def emit(field, first, whole):
        out0 = whole[0] + first[1]
        rolled = jnp.where(last, 0.0, pltpu.roll(first[0], 7, 0))
        out1 = whole[1] + rolled
        high, low = split(jnp.concatenate([out0, out1], axis=0))
        lhs[0, pl.ds(field * 16, 16), lanes] = high
        lhs[1, pl.ds(field * 16, 16), lanes] = low

    for t in range(DATES):
        first, whole = [], []
        for half in range(2):
            total = None
            for phase in range(6):
                a, b = load("a", t, phase, half), load("b", t, phase, half)
                term = a * a + b * b
                if phase == 5:
                    first.append(total)
                total = term if total is None else total + term
            whole.append(total)
        emit(t, first, whole)

    groups = []
    for i in range(0, DATES, 2):
        groups.append(([i], [i + 1]))
        rest = list(range(i + 2, DATES))
        for j in range(0, len(rest), 4):
            groups.append(([i, i + 1], rest[j : j + 4]))
    for ts, us in groups:
        pairs = [(t, u) for t in ts for u in us]
        first = {pair: ([], []) for pair in pairs}
        whole = {pair: ([], []) for pair in pairs}
        for half in range(2):
            acc = {}
            for phase in range(6):
                s_t = {t: load("s", t, phase, half) for t in ts}
                a_t = {t: load("a", t, phase, half) for t in ts}
                b_t = {t: load("b", t, phase, half) for t in ts}
                a_u = {u: load("a", u, phase, half) for u in us}
                s_u = {u: load("s", u, phase, half) for u in us}
                d_u = {u: load("d", u, phase, half) for u in us}
                for t, u in pairs:
                    p = a_u[u] * s_t[t]
                    q = d_u[u] * b_t[t]
                    r = s_u[u] * a_t[t]
                    if phase == 0:
                        acc[t, u] = (p, q, r)
                    elif phase < 5:
                        p0, q0, r0 = acc[t, u]
                        acc[t, u] = (p0 + p, q0 + q, r0 + r)
                    else:
                        p0, q0, r0 = acc[t, u]
                        re5, im5 = p0 - q0, p0 - r0
                        first[t, u][0].append(re5)
                        first[t, u][1].append(im5)
                        whole[t, u][0].append(re5 + (p - q))
                        whole[t, u][1].append(im5 + (p - r))
        for pair in pairs:
            for part in range(2):
                emit(field_of(*pair) + part, first[pair][part], whole[pair][part])


def dot(a, b):
    return jnp.dot(a, b, preferred_element_type=jnp.float32)


def link_kernel(
    msg, table, pool, edge_table, out, sums, lhs, acc, small, side_lhs, halo, edge, coh, vec, weight,
    rows,
):
    step = pl.program_id(0)
    steps = COLS // 256

    @pl.when(step == 0)
    def _():
        edge[...] = jnp.zeros_like(edge)
        halo[...] = jnp.zeros_like(halo)
        side_lhs[...] = jnp.zeros_like(side_lhs)

    def fill(date, carry):
        a = msg[date, pl.ds(0, 96), :]
        b = msg[date, pl.ds(96, 96), :]
        sums[date, pl.ds(0, 96), :] = a + b
        sums[date, pl.ds(96, 96), :] = a - b
        return carry

    lax.fori_loop(0, DATES, fill, 0)

    def products(lt, carry):
        main_products(msg, sums, lhs, lt)
        return carry

    lax.fori_loop(0, 2, products, 0)

    for date in range(DATES):
        for row in range(11):
            small[row, date : date + 1, :] = msg[date, HALO_ROW + row : HALO_ROW + row + 1, :]
    halo_rows = [(p, 5 + p) for p in range(5)]
    for t in range(DATES):
        for u_tile in range(t // 8, 2):
            for lt in range(2):
                lanes = pl.ds(lt * 128, 128)
                values = cross_products(small, t, u_tile, lanes, halo_rows)
                for part in range(2):
                    at = part * 256 + t * 16 + u_tile * 8
                    side_lhs[pl.ds(at, 8), lanes] = values[part]
    high, low = split(side_lhs[...])
    halo[...] += dot(high, table[...]) + dot(low, table[...])

    @pl.when(step < 2)
    def _():
        for t in range(DATES):
            for u_tile in range(t // 8, 2):
                a_t = small[10, t : t + 1, 0:128]
                b_t = small[10, t : t + 1, 128:256]
                a_u = small[10, u_tile * 8 : u_tile * 8 + 8, 0:128]
                b_u = small[10, u_tile * 8 : u_tile * 8 + 8, 128:256]
                at = t * 16 + u_tile * 8
                side_lhs[pl.ds(at, 8), 0:128] = a_t * a_u + b_t * b_u
                side_lhs[pl.ds(256 + at, 8), 0:128] = b_t * a_u - a_t * b_u
        high, low = split(side_lhs[:, 0:128])
        edge[...] += dot(high, pool[0]) + dot(low, pool[0])

    def pooled(chunk, carry):
        at = pl.ds(pl.multiple_of(chunk * CHUNK, CHUNK), CHUNK)
        value = dot(lhs[0, at, :], table[...]) + dot(lhs[1, at, :], table[...])

        @pl.when(step == 0)
        def _():
            acc[at, :] = value

        @pl.when(step > 0)
        def _():
            acc[at, :] += value

        return carry

    lax.fori_loop(0, FIELDS * 16 // CHUNK, pooled, 0)

    @pl.when(step == steps - 1)
    def _():
        finish(acc, edge_table, halo, edge, lhs, coh, vec, weight, rows, out)


def finish(acc, edge_table, halo, edge, lhs, coh, vec, weight, rows, out):
    row = lax.broadcasted_iota(jnp.int32, (16, 128), 0)
    lane = lax.broadcasted_iota(jnp.int32, (16, 128), 1)
    block = jnp.where(row < 8, 2 * row, 2 * (row - 8) + 1)
    mine = ((lane == block) | (lane == block + 16))
    for t in range(DATES):
        for u in range(t, DATES):
            for part in range(1 if t == u else 2):
                field = field_of(t, u) + part
                at = part * 256 + t * 16 + u
                value = jnp.where(mine, edge[at : at + 1, :], 0.0)
                high, low = split(value)
                lhs[0, pl.ds(field * 16, 16), 0:128] = high
                lhs[1, pl.ds(field * 16, 16), 0:128] = low

    def pooled(chunk, carry):
        at = pl.ds(pl.multiple_of(chunk * CHUNK, CHUNK), CHUNK)
        acc[at, :] += dot(lhs[0, at, 0:128], edge_table[...]) + dot(
            lhs[1, at, 0:128], edge_table[...]
        )
        return carry

    lax.fori_loop(0, FIELDS * 16 // CHUNK, pooled, 0)

    last = lax.broadcasted_iota(jnp.int32, (8, 128), 0) == 7
    for half in range(2):
        for mt in range(2):
            lanes = pl.ds(mt * 128, 128)

            def cov(t, u, part):
                field = field_of(t, u) + part
                value = acc[pl.ds(field * 16 + half * 8, 8), lanes]
                if half == 1:
                    at = part * 256 + t * 16 + u
                    value = value + jnp.where(last, halo[pl.ds(at, 1), lanes], 0.0)
                return value

            solve(cov, coh, vec, weight)
            for date in range(DATES):
                for part in range(2):
                    rows[part, date, mt, pl.ds(half, 8, stride=2), :] = vec[part, date]
    for mt in range(2):
        out[:, :, :, mt * 128 : mt * 128 + 128] = rows[:, :, mt]


def solve(cov, coh, vec, weight):
    inv = []
    for t in range(DATES):
        diag = cov(t, t, 0)
        root = lax.rsqrt(jnp.maximum(diag, FLOOR))
        inv.append(root)
        weight[t] = diag * (root * root) + 1.0
    for i, (t, u) in enumerate(PAIRS):
        factor = inv[t] * inv[u]
        real = cov(t, u, 0) * factor
        imag = cov(t, u, 1) * factor
        coh[i, 0] = real
        coh[i, 1] = real + imag
        coh[i, 2] = imag - real
    for t in range(DATES):
        vec[0, t] = jnp.full((8, 128), 0.25, jnp.float32)
        vec[1, t] = jnp.zeros((8, 128), jnp.float32)
        vec[2, t] = jnp.full((8, 128), 0.25, jnp.float32)

    def iterate(_, carry):
        new_real, new_imag = [None] * DATES, [None] * DATES
        sums = [[None, None, None] for _ in range(DATES)]

        def add(t, which, value, minus=False):
            if sums[t][which] is None:
                sums[t][which] = -value if minus else value
            elif minus:
                sums[t][which] = sums[t][which] - value
            else:
                sums[t][which] = sums[t][which] + value

        def pair(t, u, v):
            i = PAIR_AT[t, u]
            real, plus, minus = coh[i, 0], coh[i, 1], coh[i, 2]
            add(t, 0, real * v[u][2])
            add(t, 1, plus * v[u][1])
            add(t, 2, minus * v[u][0])
            add(u, 0, real * v[t][2])
            add(u, 1, minus * v[t][1], True)
            add(u, 2, plus * v[t][0], True)

        for first in range(0, DATES, 4):
            for second in range(first, DATES, 4):
                dates = sorted(set(range(first, first + 4)) | set(range(second, second + 4)))
                v = {t: (vec[0, t], vec[1, t], vec[2, t]) for t in dates}
                for t in range(first, first + 4):
                    for u in range(second, second + 4):
                        if t < u:
                            pair(t, u, v)
        norm = None
        for t in range(DATES):
            own = weight[t]
            new_real[t] = (sums[t][0] - sums[t][1]) + own * vec[0, t]
            new_imag[t] = (sums[t][0] + sums[t][2]) + own * vec[1, t]
            square = new_real[t] * new_real[t] + new_imag[t] * new_imag[t]
            norm = square if norm is None else norm + square
        scale = lax.rsqrt(norm)
        for t in range(DATES):
            real, imag = new_real[t] * scale, new_imag[t] * scale
            vec[0, t] = real
            vec[1, t] = imag
            vec[2, t] = real + imag
        return carry

    lax.fori_loop(0, ITERS, iterate, 0)


def link(message, table, pool, edge_table):
    whole = lambda *shape: pl.BlockSpec(shape, lambda i: (0,) * len(shape))
    return pl.pallas_call(
        link_kernel,
        grid=(COLS // 256,),
        in_specs=[
            pl.BlockSpec((DATES, MSG_ROWS, 256), lambda i: (0, 0, i)),
            pl.BlockSpec((256, OUT_COLS), lambda i: (i, 0)),
            pl.BlockSpec((1, 128, 128), lambda i: (jnp.minimum(i, 1), 0, 0)),
            whole(128, OUT_COLS),
        ],
        out_specs=whole(2, DATES, BLOCKS, OUT_COLS),
        out_shape=jax.ShapeDtypeStruct((2, DATES, BLOCKS, OUT_COLS), jnp.float32),
        scratch_shapes=[
            pltpu.VMEM((DATES, 192, 256), jnp.float32),
            pltpu.VMEM((2, FIELDS * 16, 256), jnp.bfloat16),
            pltpu.VMEM((FIELDS * 16, OUT_COLS), jnp.float32),
            pltpu.VMEM((11, DATES, 256), jnp.float32),
            pltpu.VMEM((512, 256), jnp.float32),
            pltpu.VMEM((512, 256), jnp.float32),
            pltpu.VMEM((512, 128), jnp.float32),
            pltpu.VMEM((len(PAIRS), 3, 8, 128), jnp.float32),
            pltpu.VMEM((3, DATES, 8, 128), jnp.float32),
            pltpu.VMEM((DATES, 8, 128), jnp.float32),
            pltpu.VMEM((2, DATES, 2, BLOCKS, 128), jnp.float32),
        ],
        compiler_params=pltpu.CompilerParams(vmem_limit_bytes=VMEM_LIMIT),
        cost_estimate=pl.CostEstimate(flops=10**9, bytes_accessed=10**7, transcendentals=0),
        name="link",
    )(message, table, pool, edge_table)


def local(slc, valid_rows):
    size = lax.axis_size("col")
    up = [(i, i + 1) for i in range(size - 1)]
    down = [(i + 1, i) for i in range(size - 1)]
    first, last = edge_columns(slc, valid_rows)
    left = lax.ppermute(last, "col", up)
    right = lax.ppermute(first, "col", down)
    message = pack(slc, valid_rows)
    message = insert_edges(left, right, message)
    received = lax.all_to_all(message, "row", 0, 0, tiled=True)
    main, pool, edge = (jnp.asarray(x, jnp.bfloat16) for x in column_tables())
    return link(received, main, pool, edge)


def solution(mesh):
    return jax.shard_map(
        local,
        mesh=mesh,
        in_specs=(P(None, "row", None, "col"), P()),
        out_specs=P(None, None, "row", "col"),
        check_vma=False,
    )
```

time: 504 us -> 188 us (0.37)
  other arithmetic: 159 us -> 0 us
  local copies, waits for them, and re-layouts: 144 us -> 2.53 us
  matrix products: 58.7 us -> 0 us
  Pallas kernels: 0 us -> 55.2 us
  waiting for transfers between devices: 10.8 us -> 0.01 us
  blocking collectives: 114 us -> 122 us
  starting transfers between devices: 12.1 us -> 6.42 us
    reduce_sum x68 -> x0, other arithmetic: 139 us -> none  [the longest x16 93.2 us: pool_window(): whole_block = jnp.sum(grouped, axis=-2)]
    dynamic_slice x17 -> x0, local copies, waits for them, and re-layouts: 77.2 us -> none  [the longest x16 77.2 us: covariance(): return lax.map(one_date, (real_part, imag_part))]
    dot_general x32 -> x0, matrix products: 58.7 us -> none  [pool_window(): jnp.dot(row_sum, table, precision=lax.Precision.HIGHEST, preferred_elemen...]
    pallas_call x0 -> x4, Pallas kernels: none -> 55.2 us  [the longest x1 39.5 us: link(): pl.pallas_call(link_kernel, grid=(COLS // 256,), in_specs=[pl.BlockSpec((...]
    mul x33 -> x0, local copies, waits for them, and re-layouts: 30.6 us -> none  [the longest x1 29.1 us: local(): masked = slc * keep_mask[None, :, :, None].astype(jnp.float32)]
    concatenate x2 -> x0, other arithmetic: 11.7 us -> none  [the longest x1 11.7 us: with_halo(): shard = jnp.concatenate([before, shard, after], axis=dim)]
    ppermute x4 -> x2, waiting for transfers between devices: 10.8 us -> 0.01 us  [the longest x1 0.01 us: local(): right = lax.ppermute(first, 'col', down)]
    unnamed x12 -> x5, local copies, waits for them, and re-layouts: 10.7 us -> 2.53 us
  transfers between devices with their start and end apart: 4 -> 2, of which waited for: 3 -> 0; matrix products, arithmetic and copies ran while one was open for 0% -> 0% of each run, Pallas kernels for 0% -> 5%
where the time goes in v1:
time: 188 us; the launch traced here: 187 us
  blocking collectives  122 us (65%)
  Pallas kernels  55.2 us (29%)
  starting transfers between devices  6.42 us (3%)
  local copies, waits for them, and re-layouts  2.53 us (1%)
    all_to_all x1, blocking collectives, local(): received = lax.all_to_all(message, 'row', 0, 0, tiled=True)  122 us
    pallas_call x1, Pallas kernels, link(): pl.pallas_call(link_kernel, grid=(COLS // 256,), in_specs=[pl.BlockSpec((...  39.5 us
    pallas_call x1, Pallas kernels, pack(): pl.pallas_call(pack_kernel, grid=(TILES // GROUP,), in_specs=[pl.BlockSpe...  8.46 us
    pallas_call x1, Pallas kernels, edge_columns(): pl.pallas_call(edge_kernel, grid=(1,), in_specs=[pl.BlockSpec(memory_spac...  5.12 us
    ppermute x1, starting transfers between devices, local(): left = lax.ppermute(last, 'col', up)  4.5 us
  transfers between devices with their start and end apart: 2, of which 0 were waited for; matrix products, arithmetic and copies ran while one was open for 0% of the time, Pallas kernels for 5%

profile of v1, /device:TPU:1, one launch (start us, length us, event | category | flops | bytes accessed | tf_op | source)
XLA Modules:
  0.0 186.6 jit_solution(1366954009273558372)
XLA Ops:
  0.0 1.4 copy.7.valid_ref
  1.4 5.1 %edge_columns.1 = (f32[2,1536]{1,0:T(2,128)}, f32[2,1536]{1,0:T(2,128)}) custom-call(s32[16,2]{1,0:T(8,128)} %copy.7.valid_ref, f32[2,1,1536,768]{3,2,1,0:T(8,128)} %after_ref.1, f32[2,1,1536,768]{3,2,1,0:T(8,128)} %after_ref.1), custom_call_target="tpu_custom_call" | custom-call | tf_op jit(solution)/shard_map/edge_columns/pallas_call | solution.py:65
  6.5 4.5 %collective-permute-start = (f32[2,1536]{1,0:T(2,128)}, f32[2,1536]{1,0:T(2,128)S(1)}, u32[]{:S(2)}, u32[]{:S(2)}) collective-permute-start(f32[2,1536]{1,0:T(2,128)} %get-tuple-element.7), channel_id=1, source_target_pairs={{0,1},{1,2},{2,3},{3,4},{4,5},{5,6},{6,7},{8,9},{9,10},{10,11},{11... | collective-permute-start | bytes 36872 | tf_op jit(solution)/shard_map/ppermute | solution.py:494
  11.0 1.9 %collective-permute-start.1 = (f32[2,1536]{1,0:T(2,128)}, f32[2,1536]{1,0:T(2,128)S(1)}, u32[]{:S(2)}, u32[]{:S(2)}) collective-permute-start(f32[2,1536]{1,0:T(2,128)} %get-tuple-element.8), channel_id=1, source_target_pairs={{1,0},{2,1},{3,2},{4,3},{5,4},{6,5},{7,6},{9,8},{10,9},{11,10},{12... | collective-permute-start | bytes 36872 | tf_op jit(solution)/shard_map/ppermute | solution.py:495
  12.9 8.5 %pack.1.in_ref = f32[16,208,768]{2,1,0:T(8,128)} custom-call(s32[16,2]{1,0:T(8,128)} %copy.7.valid_ref, f32[2,1,1536,768]{3,2,1,0:T(8,128)} %after_ref.1, f32[2,1,1536,768]{3,2,1,0:T(8,128)} %after_ref.1, f32[2,1,1536,768]{3,2,1,0:T(8,128)} %after_ref.1), custom_call_target="tpu_custom_call" | custom-call | flops 1000000 | bytes 20000000 | tf_op jit(solution)/shard_map/pack/pallas_call | solution.py:117
  21.4 0.0 collective-permute-done.left_ref
  21.4 0.0 copy-start
  21.4 0.0 collective-permute-done.1.right_ref
  21.4 0.6 copy-done
  22.0 0.0 copy-start.1
  22.0 0.6 copy-done.1
  22.6 2.1 %insert_edges.1 = f32[16,208,768]{2,1,0:T(8,128)} custom-call(f32[2,1536]{1,0:T(2,128)} %copy-done, f32[2,1536]{1,0:T(2,128)} %copy-done.1, f32[16,208,768]{2,1,0:T(8,128)} %pack.1.in_ref), custom_call_target="tpu_custom_call", output_to_operand_aliasing={{}: (2, {})} | custom-call | tf_op jit(solution)/shard_map/insert_edges/pallas_call | solution.py:151
  24.6 122.4 %all_to_all.5.msg = f32[16,208,768]{2,1,0:T(8,128)} all-to-all(f32[16,208,768]{2,1,0:T(8,128)} %insert_edges.1), channel_id=1, replica_groups=mesh['row'=16,'col'=8] {'row'}, dimensions={0} | all-to-all | bytes 20447232 | tf_op jit(solution)/shard_map/all_to_all | solution.py:498
  147.1 39.5 %link.1 = f32[2,16,16,256]{3,2,1,0:T(8,128)} custom-call(f32[16,208,768]{2,1,0:T(8,128)} %all_to_all.5.msg, bf16[768,256]{1,0:T(8,128)(2,1)} %constant.6.clone.table, bf16[2,128,128]{2,1,0:T(8,128)(2,1)} %constant.7.clone.pool, bf16[128,256]{1,0:T(8,128)(2,1)} %constant.8.clone.edge_table), custom_call_target="tpu_custom_call" | custom-call | flops 1000000000 | bytes 10000000 | tf_op jit(solution)/shard_map/link/pallas_call | solution.py:459
Async XLA Ops:
  6.5 14.9 %collective-permute-start = (f32[2,1536]{1,0:T(2,128)}, f32[2,1536]{1,0:T(2,128)S(1)}, u32[]{:S(2)}, u32[]{:S(2)}) collective-permute-start(f32[2,1536]{1,0:T(2,128)} %get-tuple-element.7), channel_id=1, source_target_pairs={{0,1},{1,2},{2,3},{3,4},{4,5},{5,6},{6,7},{8,9},{9,10},{10,11},{11... | collective-permute-start | bytes 36872 | tf_op jit(solution)/shard_map/ppermute | solution.py:494
  11.0 10.4 %collective-permute-start.1 = (f32[2,1536]{1,0:T(2,128)}, f32[2,1536]{1,0:T(2,128)S(1)}, u32[]{:S(2)}, u32[]{:S(2)}) collective-permute-start(f32[2,1536]{1,0:T(2,128)} %get-tuple-element.8), channel_id=1, source_target_pairs={{1,0},{2,1},{3,2},{4,3},{5,4},{6,5},{7,6},{9,8},{10,9},{11,10},{12... | collective-permute-start | bytes 36872 | tf_op jit(solution)/shard_map/ppermute | solution.py:495
  21.4 0.6 copy-start
  22.0 0.6 copy-start.1

commit v2 on v1

v2 whole, which is shorter than its diff:
```python
import functools

import jax
import jax.numpy as jnp
import numpy as np
from jax import lax
from jax.experimental import pallas as pl
from jax.experimental.pallas import tpu as pltpu
from jax.sharding import PartitionSpec as P

ITERS = 10
FLOOR = 20.0
DATES = 16
TILES = 16
COLS = 768
LANE_TILES = 6
FIRST = 5
OUT_COLS = 256
BLOCKS = 16
TILE_ROWS = 6 * BLOCKS
MSG_ROWS = 208
HALO_ROW = 192
EDGE_ROW = 202
GROUP = 4
PAIRS = [(t, u) for t in range(DATES) for u in range(t + 1, DATES)]
PAIR_AT = {pair: i for i, pair in enumerate(PAIRS)}
FIELDS = DATES + 2 * len(PAIRS)
CHUNK = 512
SIDE = 512
VMEM_LIMIT = 56 * 1024 * 1024
FEEDS = ((0, 2), (0,), (0,), (0, 1), (1, 2), (2,))


def lane_columns():
    lane = np.arange(128)
    group_a = np.where(lane < 32, 128 + lane, lane)
    group_b = np.where((lane >= 32) & (lane < 96), 128 + lane, 128 + (lane + 64) % 128)
    own = np.where(lane < 32, lane, 128 + lane)
    other = (lane + 64) % 128
    far = np.where(other < 32, other, 128 + other)
    group_c = np.where((lane < 32) | (lane >= 96), own, far)
    return group_a, group_b, group_c


def column_tables():
    groups = lane_columns()
    tables = np.zeros((LANE_TILES, 256, 256), np.float32)
    for lt in range(LANE_TILES):
        column = (lt * 128 + np.arange(128) + 64) % COLS
        for place, group in enumerate(FEEDS[lt]):
            target = 3 * groups[group][None, :]
            inside = (column[:, None] >= target - 1) & (column[:, None] <= target + 3)
            for copy in range(2):
                tables[lt, copy * 128 : copy * 128 + 128, place * 128 : place * 128 + 128] = inside
    row = np.arange(128)
    pool = np.zeros((2, 8, 128), np.float32)
    for half in range(2):
        for s in range(8):
            block = 2 * s + half
            pool[half, s] = (row >= 6 * block) & (row <= 6 * block + 10)
    return tables, pool


def pack_kernel(
    valid_ref, before_ref, tile_ref, after_ref, out1_ref, out2_ref, first_ref, last_ref, rows_ref
):
    me = lax.axis_index("row")
    step = pl.program_id(0)
    low, high = valid_ref[0, me], valid_ref[1, me]
    span = GROUP * TILE_ROWS
    lane = lax.broadcasted_iota(jnp.int32, (8, 128), 1)

    def masked(ref, start, count):
        row = lax.broadcasted_iota(jnp.int32, (count, 128), 0) + (step * span + start)
        keep = (row >= low) & (row < high)
        left = lax.broadcasted_iota(jnp.int32, (count, 128), 1) < 64
        for part in range(2):
            value = [
                jnp.where(keep, ref[part, 0, :, lt * 128 : lt * 128 + 128], 0.0)
                for lt in range(LANE_TILES)
            ]
            if count == span:
                for at, pick, out in ((0, 0, first_ref), (LANE_TILES - 1, 127, last_ref)):
                    column = lax.dot_general(
                        jnp.where(lane == pick, 1.0, 0.0), value[at], (((1,), (1,)), ((), ())),
                        precision=lax.Precision.HIGHEST, preferred_element_type=jnp.float32,
                    )
                    out[part : part + 1, :] = column[0:1, :]
            turned = [pltpu.roll(v, 64, 1) for v in value]
            for lt in range(LANE_TILES):
                rows_ref[part, lt, pl.ds(start + 8, count), :] = jnp.where(
                    left, turned[lt], turned[(lt + 1) % LANE_TILES]
                )

    masked(before_ref, -8, 8)
    masked(tile_ref, 0, span)
    masked(after_ref, span, 8)
    for tile in range(GROUP):
        base = 5 + tile * TILE_ROWS
        for lt in range(LANE_TILES):
            out = out1_ref if lt < FIRST else out2_ref
            lanes = pl.ds((lt if lt < FIRST else 0) * 128, 128)
            for part in range(2):
                for phase in range(6):
                    for half in range(2):
                        out[tile, pl.ds(part * 96 + phase * 16 + half * 8, 8), lanes] = rows_ref[
                            part, lt, pl.ds(base + 6 * half + phase, 8, stride=12), :
                        ]
                out[tile, pl.ds(HALO_ROW + 5 * part, 5), lanes] = rows_ref[
                    part, lt, pl.ds(base + TILE_ROWS, 5), :
                ]
        out1_ref[tile, pl.ds(EDGE_ROW, 6), :] = jnp.zeros((6, FIRST * 128), jnp.float32)
        out2_ref[tile, pl.ds(EDGE_ROW, 6), :] = jnp.zeros((6, 128), jnp.float32)


def pack(slc, valid_rows):
    span = GROUP * TILE_ROWS
    eight = span // 8
    column = jax.ShapeDtypeStruct((2, 1536), jnp.float32)
    return pl.pallas_call(
        pack_kernel,
        grid=(TILES // GROUP,),
        in_specs=[
            pl.BlockSpec(memory_space=pltpu.SMEM),
            pl.BlockSpec((2, 1, 8, COLS), lambda i: (0, 0, jnp.maximum(i * eight - 1, 0), 0)),
            pl.BlockSpec((2, 1, span, COLS), lambda i: (0, 0, i, 0)),
            pl.BlockSpec((2, 1, 8, COLS), lambda i: (0, 0, jnp.minimum(i * eight + eight, 191), 0)),
        ],
        out_specs=[
            pl.BlockSpec((GROUP, MSG_ROWS, FIRST * 128), lambda i: (i, 0, 0)),
            pl.BlockSpec((GROUP, MSG_ROWS, 128), lambda i: (i, 0, 0)),
            pl.BlockSpec((2, span), lambda i: (0, i)),
            pl.BlockSpec((2, span), lambda i: (0, i)),
        ],
        out_shape=[
            jax.ShapeDtypeStruct((TILES, MSG_ROWS, FIRST * 128), jnp.float32),
            jax.ShapeDtypeStruct((TILES, MSG_ROWS, 128), jnp.float32),
            column,
            column,
        ],
        scratch_shapes=[pltpu.VMEM((2, LANE_TILES, span + 16, 128), jnp.float32)],
        compiler_params=pltpu.CompilerParams(vmem_limit_bytes=VMEM_LIMIT),
        cost_estimate=pl.CostEstimate(flops=10**6, bytes_accessed=2 * 10**7, transcendentals=0),
        name="pack",
    )(valid_rows.T, slc, slc, slc)


def insert_kernel(left_ref, right_ref, in_ref, out_ref, wide_ref):
    out_ref[...] = in_ref[...]
    wide_ref[...] = jnp.zeros_like(wide_ref)
    for side, ref in enumerate((left_ref, right_ref)):
        wide_ref[2 * side : 2 * side + 2, 128 : 128 + 1536] = ref[...]
    for tile in range(TILES):
        start = 128 + tile * TILE_ROWS - 3
        at = EDGE_ROW % 8
        out_ref[tile, at : at + 4, :] = wide_ref[0:4, start : start + 128]


def insert_edges(left, right, message):
    spec = pl.BlockSpec((TILES, 8, 128), lambda i: (0, EDGE_ROW // 8, 0))
    column = pl.BlockSpec((2, 1536), lambda i: (0, 0))
    return pl.pallas_call(
        insert_kernel,
        grid=(1,),
        in_specs=[column, column, spec],
        out_specs=spec,
        out_shape=jax.ShapeDtypeStruct(message.shape, message.dtype),
        input_output_aliases={2: 0},
        scratch_shapes=[pltpu.VMEM((8, 1920), jnp.float32)],
        name="insert_edges",
    )(left, right, message)


def split(x):
    high = x.astype(jnp.bfloat16)
    return high, (x - high.astype(jnp.float32)).astype(jnp.bfloat16)


def field_of(t, u):
    return t if t == u else DATES + 2 * PAIR_AT[t, u]


def cross_products(data, t_part, u_tile, lanes, rows):
    real = imag = None
    for re_row, im_row in rows:
        a_t = data[re_row, pl.ds(t_part, 1), lanes]
        b_t = data[im_row, pl.ds(t_part, 1), lanes]
        a_u = data[re_row, pl.ds(u_tile * 8, 8), lanes]
        b_u = data[im_row, pl.ds(u_tile * 8, 8), lanes]
        re = a_t * a_u + b_t * b_u
        im = b_t * a_u - a_t * b_u
        real = re if real is None else real + re
        imag = im if imag is None else imag + im
    return real, imag


def main_products(msg, sums, lhs):
    lanes = pl.ds(0, 128)
    last = lax.broadcasted_iota(jnp.int32, (8, 128), 0) == 7

    def rows_at(phase, half):
        return pl.ds(phase * 16 + half * 8, 8)

    def load(kind, date, phase, half):
        if kind == "a":
            return msg[date, pl.ds(phase * 16 + half * 8, 8), lanes]
        if kind == "b":
            return msg[date, pl.ds(96 + phase * 16 + half * 8, 8), lanes]
        base = 0 if kind == "s" else 96
        return sums[date, pl.ds(base + phase * 16 + half * 8, 8), lanes]

    def emit(field, first, whole):
        out0 = whole[0] + first[1]
        rolled = jnp.where(last, 0.0, pltpu.roll(first[0], 7, 0))
        out1 = whole[1] + rolled
        high, low = split(jnp.concatenate([out0, out1], axis=0))
        lhs[pl.ds(field * 16, 16), 0:128] = high
        lhs[pl.ds(field * 16, 16), 128:256] = low

    for t in range(DATES):
        first, whole = [], []
        for half in range(2):
            total = None
            for phase in range(6):
                a, b = load("a", t, phase, half), load("b", t, phase, half)
                term = a * a + b * b
                if phase == 5:
                    first.append(total)
                total = term if total is None else total + term
            whole.append(total)
        emit(t, first, whole)

    groups = []
    for i in range(0, DATES, 2):
        groups.append(([i], [i + 1]))
        rest = list(range(i + 2, DATES))
        for j in range(0, len(rest), 4):
            groups.append(([i, i + 1], rest[j : j + 4]))
    for ts, us in groups:
        pairs = [(t, u) for t in ts for u in us]
        first = {pair: ([], []) for pair in pairs}
        whole = {pair: ([], []) for pair in pairs}
        for half in range(2):
            acc = {}
            for phase in range(6):
                s_t = {t: load("s", t, phase, half) for t in ts}
                a_t = {t: load("a", t, phase, half) for t in ts}
                b_t = {t: load("b", t, phase, half) for t in ts}
                a_u = {u: load("a", u, phase, half) for u in us}
                s_u = {u: load("s", u, phase, half) for u in us}
                d_u = {u: load("d", u, phase, half) for u in us}
                for t, u in pairs:
                    p = a_u[u] * s_t[t]
                    q = d_u[u] * b_t[t]
                    r = s_u[u] * a_t[t]
                    if phase == 0:
                        acc[t, u] = (p, q, r)
                    elif phase < 5:
                        p0, q0, r0 = acc[t, u]
                        acc[t, u] = (p0 + p, q0 + q, r0 + r)
                    else:
                        p0, q0, r0 = acc[t, u]
                        re5, im5 = p0 - q0, p0 - r0
                        first[t, u][0].append(re5)
                        first[t, u][1].append(im5)
                        whole[t, u][0].append(re5 + (p - q))
                        whole[t, u][1].append(im5 + (p - r))
        for pair in pairs:
            for part in range(2):
                emit(field_of(*pair) + part, first[pair][part], whole[pair][part])


def dot(a, b):
    return jnp.dot(a, b, preferred_element_type=jnp.float32)


def lane_tile(msg, sums, lhs, small, side_lhs):
    def fill(date, carry):
        a = msg[date, pl.ds(0, 96), :]
        b = msg[date, pl.ds(96, 96), :]
        sums[date, pl.ds(0, 96), :] = a + b
        sums[date, pl.ds(96, 96), :] = a - b
        return carry

    lax.fori_loop(0, DATES, fill, 0)
    main_products(msg, sums, lhs)
    for date in range(DATES):
        for row in range(small.shape[0]):
            small[row, date : date + 1, :] = msg[date, HALO_ROW + row : HALO_ROW + row + 1, :]
    for t in range(DATES):
        for u_tile in range(2):
            if u_tile < t // 8:
                values = (jnp.zeros((8, 128), jnp.float32),) * 2
            else:
                rows = [(p, 5 + p) for p in range(5)]
                values = cross_products(small, t, u_tile, pl.ds(0, 128), rows)
            for part in range(2):
                at = pl.ds(part * 256 + t * 16 + u_tile * 8, 8)
                side_lhs[at, 0:128] = values[part]


def pool_columns(lhs, side_lhs, table, width, put, put_side):
    def pooled(chunk, carry):
        at = pl.ds(pl.multiple_of(chunk * CHUNK, CHUNK), CHUNK)
        put(at, dot(lhs[at, :], table[0, :, 0:width]))
        return carry

    lax.fori_loop(0, FIELDS * 16 // CHUNK, pooled, 0)
    high, low = split(side_lhs[...])
    put_side(dot(high, table[0, 0:128, 0:width]) + dot(low, table[0, 0:128, 0:width]))


def first_kernel(
    msg, table, part_out, out, sums, lhs, small, side_lhs, acc, halo, coh, vec, weight, rows
):
    step = pl.program_id(0)
    lane_tile(msg, sums, lhs, small, side_lhs)
    for lt in range(FIRST):

        @pl.when(step == lt)
        def _():
            def put(at, value):
                for place, group in enumerate(FEEDS[lt]):
                    own = value[:, place * 128 : place * 128 + 128]
                    if group == 2:
                        if lt == 0:
                            part_out[at, :] = own
                        else:
                            part_out[at, :] += own
                    elif lt == min(i for i in range(FIRST) if group in FEEDS[i]):
                        acc[group, at, :] = own
                    else:
                        acc[group, at, :] += own

            def put_side(value):
                for place, group in enumerate(FEEDS[lt]):
                    own = value[:, place * 128 : place * 128 + 128]
                    if group == 2:
                        at = pl.ds(FIELDS * 16, SIDE)
                        if lt == 0:
                            part_out[at, :] = own
                        else:
                            part_out[at, :] += own
                    elif lt == min(i for i in range(FIRST) if group in FEEDS[i]):
                        halo[group] = own
                    else:
                        halo[group] += own

            pool_columns(lhs, side_lhs, table, 128 * len(FEEDS[lt]), put, put_side)

    @pl.when(step == FIRST - 1)
    def _():
        lane = lax.broadcasted_iota(jnp.int32, (8, 128), 1)
        last = lax.broadcasted_iota(jnp.int32, (8, 128), 0) == 7

        def below(group, t, u, part):
            return halo[group, pl.ds(part * 256 + t * 16 + u, 1), :]

        for half in range(2):

            def cov(t, u, part):
                value = acc[0, pl.ds((field_of(t, u) + part) * 16 + half * 8, 8), :]
                if half == 1:
                    value = value + jnp.where(last, below(0, t, u, part), 0.0)
                return value

            solve(cov, coh, vec, weight)
            for date in range(DATES):
                for part in range(2):
                    rows[part, date, 0, pl.ds(half, 8, stride=2), :] = vec[part, date]

        even = (lane >= 32) & (lane < 96)

        def cov_b(t, u, part):
            at = (field_of(t, u) + part) * 16
            value = jnp.where(even, acc[1, pl.ds(at, 8), :], acc[1, pl.ds(at + 8, 8), :])
            return value + jnp.where(last & ~even, below(1, t, u, part), 0.0)

        solve(cov_b, coh, vec, weight)
        for date in range(DATES):
            for part in range(2):
                value = vec[part, date]
                rows[part, date, 1, pl.ds(0, 8, stride=2), :] = value
                rows[part, date, 1, pl.ds(1, 8, stride=2), :] = pltpu.roll(value, 64, 1)
        out[:, :, :, 0:128] = rows[:, :, 0]
        left = lax.broadcasted_iota(jnp.int32, (2, DATES, BLOCKS, 128), 3) < 32
        out[:, :, :, 128:256] = jnp.where(left, rows[:, :, 0], rows[:, :, 1])


def last_kernel(
    msg, table, pool, partial, done, out, sums, lhs, small, side_lhs, acc, halo, edge, coh, vec,
    weight, rows,
):
    lane_tile(msg, sums, lhs, small, side_lhs)

    def put(at, value):
        acc[at, :] = value + partial[at, :]

    def put_side(value):
        halo[...] = value + partial[pl.ds(FIELDS * 16, SIDE), :]

    pool_columns(lhs, side_lhs, table, 128, put, put_side)
    for side in range(2):
        for t in range(DATES):
            for u_tile in range(t // 8, 2):
                row = 10 + 2 * side
                value = cross_products(small, t, u_tile, pl.ds(0, 128), [(row, row + 1)])
                for part in range(2):
                    at = part * 256 + t * 16 + u_tile * 8
                    side_lhs[pl.ds(at, 8), :] = value[part]
        high, low = split(side_lhs[...])
        for half in range(2):
            dims = (((1,), (1,)), ((), ()))
            weights = pool[half].astype(jnp.bfloat16)
            edge[side, half] = lax.dot_general(
                weights, high, dims, preferred_element_type=jnp.float32
            ) + lax.dot_general(weights, low, dims, preferred_element_type=jnp.float32)

    lane = lax.broadcasted_iota(jnp.int32, (8, 128), 1)
    last = lax.broadcasted_iota(jnp.int32, (8, 128), 0) == 7
    even = (lane < 32) | (lane >= 96)
    places = ((0, 0, 0), (0, 1, 64), (1, 0, 127), (1, 1, 63))

    def cov(t, u, part):
        at = (field_of(t, u) + part) * 16
        value = jnp.where(even, acc[pl.ds(at, 8), :], acc[pl.ds(at + 8, 8), :])
        index = part * 256 + t * 16 + u
        beside = jnp.where(last & ~even, halo[pl.ds(index, 1), :], 0.0)
        for side, half, target in places:
            source = edge[side, half, :, pl.ds(index // 128 * 128, 128)]
            turned = pltpu.roll(source, (target - index) % 128, 1)
            beside = beside + jnp.where(lane == target, turned, 0.0)
        return value + beside

    solve(cov, coh, vec, weight)
    for date in range(DATES):
        for part in range(2):
            value = vec[part, date]
            rows[part, date, 0, pl.ds(0, 8, stride=2), :] = value
            rows[part, date, 0, pl.ds(1, 8, stride=2), :] = pltpu.roll(value, 64, 1)
    place = lax.broadcasted_iota(jnp.int32, (2, DATES, BLOCKS, 128), 3)
    out[:, :, :, 0:128] = jnp.where(place < 32, rows[:, :, 0], done[:, :, :, 0:128])
    out[:, :, :, 128:256] = jnp.where(place >= 96, rows[:, :, 0], done[:, :, :, 128:256])


def solve(cov, coh, vec, weight):
    inv = []
    for t in range(DATES):
        diag = cov(t, t, 0)
        root = lax.rsqrt(jnp.maximum(diag, FLOOR))
        inv.append(root)
        weight[t] = diag * (root * root) + 1.0
    for i, (t, u) in enumerate(PAIRS):
        factor = inv[t] * inv[u]
        real = cov(t, u, 0) * factor
        imag = cov(t, u, 1) * factor
        coh[i, 0] = real
        coh[i, 1] = real + imag
        coh[i, 2] = imag - real
    for t in range(DATES):
        vec[0, t] = jnp.full((8, 128), 0.25, jnp.float32)
        vec[1, t] = jnp.zeros((8, 128), jnp.float32)
        vec[2, t] = jnp.full((8, 128), 0.25, jnp.float32)

    def iterate(_, carry):
        new_real, new_imag = [None] * DATES, [None] * DATES
        sums = [[None, None, None] for _ in range(DATES)]

        def add(t, which, value, minus=False):
            if sums[t][which] is None:
                sums[t][which] = -value if minus else value
            elif minus:
                sums[t][which] = sums[t][which] - value
            else:
                sums[t][which] = sums[t][which] + value

        def pair(t, u, v):
            i = PAIR_AT[t, u]
            real, plus, minus = coh[i, 0], coh[i, 1], coh[i, 2]
            add(t, 0, real * v[u][2])
            add(t, 1, plus * v[u][1])
            add(t, 2, minus * v[u][0])
            add(u, 0, real * v[t][2])
            add(u, 1, minus * v[t][1], True)
            add(u, 2, plus * v[t][0], True)

        for first in range(0, DATES, 4):
            for second in range(first, DATES, 4):
                dates = sorted(set(range(first, first + 4)) | set(range(second, second + 4)))
                v = {t: (vec[0, t], vec[1, t], vec[2, t]) for t in dates}
                for t in range(first, first + 4):
                    for u in range(second, second + 4):
                        if t < u:
                            pair(t, u, v)
        norm = None
        for t in range(DATES):
            own = weight[t]
            new_real[t] = (sums[t][0] - sums[t][1]) + own * vec[0, t]
            new_imag[t] = (sums[t][0] + sums[t][2]) + own * vec[1, t]
            square = new_real[t] * new_real[t] + new_imag[t] * new_imag[t]
            norm = square if norm is None else norm + square
        scale = lax.rsqrt(norm)
        for t in range(DATES):
            real, imag = new_real[t] * scale, new_imag[t] * scale
            vec[0, t] = real
            vec[1, t] = imag
            vec[2, t] = real + imag
        return carry

    lax.fori_loop(0, ITERS, iterate, 0)


def whole(*shape):
    return pl.BlockSpec(shape, lambda i: (0,) * len(shape))


def common_scratch(small_rows):
    return [
        pltpu.VMEM((DATES, 192, 128), jnp.float32),
        pltpu.VMEM((FIELDS * 16, 256), jnp.bfloat16),
        pltpu.VMEM((small_rows, DATES, 128), jnp.float32),
        pltpu.VMEM((SIDE, 128), jnp.float32),
    ]


SOLVE_SCRATCH = [
    pltpu.VMEM((len(PAIRS), 3, 8, 128), jnp.float32),
    pltpu.VMEM((3, DATES, 8, 128), jnp.float32),
    pltpu.VMEM((DATES, 8, 128), jnp.float32),
]
LINKED = (2, DATES, BLOCKS, OUT_COLS)


def link_first(message, tables):
    rows = FIELDS * 16 + SIDE
    return pl.pallas_call(
        first_kernel,
        grid=(FIRST,),
        in_specs=[
            pl.BlockSpec((DATES, MSG_ROWS, 128), lambda i: (0, 0, i)),
            pl.BlockSpec((1, 256, 256), lambda i: (i, 0, 0)),
        ],
        out_specs=[whole(rows, 128), whole(*LINKED)],
        out_shape=[
            jax.ShapeDtypeStruct((rows, 128), jnp.float32),
            jax.ShapeDtypeStruct(LINKED, jnp.float32),
        ],
        scratch_shapes=common_scratch(10)
        + [
            pltpu.VMEM((2, FIELDS * 16, 128), jnp.float32),
            pltpu.VMEM((2, SIDE, 128), jnp.float32),
        ]
        + SOLVE_SCRATCH
        + [pltpu.VMEM((2, DATES, 2, BLOCKS, 128), jnp.float32)],
        compiler_params=pltpu.CompilerParams(vmem_limit_bytes=VMEM_LIMIT),
        cost_estimate=pl.CostEstimate(flops=10**9, bytes_accessed=10**7, transcendentals=0),
        name="link_first",
    )(message, tables)


def link_last(message, tables, pool, partial, done):
    rows = FIELDS * 16 + SIDE
    return pl.pallas_call(
        last_kernel,
        grid=(1,),
        in_specs=[
            whole(DATES, MSG_ROWS, 128),
            pl.BlockSpec((1, 256, 128), lambda i: (FIRST, 0, 0)),
            whole(2, 8, 128),
            whole(rows, 128),
            whole(*LINKED),
        ],
        out_specs=whole(*LINKED),
        out_shape=jax.ShapeDtypeStruct(LINKED, jnp.float32),
        scratch_shapes=common_scratch(14)
        + [
            pltpu.VMEM((FIELDS * 16, 128), jnp.float32),
            pltpu.VMEM((SIDE, 128), jnp.float32),
            pltpu.VMEM((2, 2, 8, SIDE), jnp.float32),
        ]
        + SOLVE_SCRATCH
        + [pltpu.VMEM((2, DATES, 1, BLOCKS, 128), jnp.float32)],
        compiler_params=pltpu.CompilerParams(vmem_limit_bytes=VMEM_LIMIT),
        cost_estimate=pl.CostEstimate(flops=10**8, bytes_accessed=10**7, transcendentals=0),
        name="link_last",
    )(message, tables, pool, partial, done)


def local(slc, valid_rows):
    size = lax.axis_size("col")
    up = [(i, i + 1) for i in range(size - 1)]
    down = [(i + 1, i) for i in range(size - 1)]
    message1, message2, first, last = pack(slc, valid_rows)
    left = lax.ppermute(last, "col", up)
    right = lax.ppermute(first, "col", down)
    received1 = lax.all_to_all(message1, "row", 0, 0, tiled=True)
    left, right, received1 = lax.optimization_barrier((left, right, received1))
    message2 = insert_edges(left, right, message2)
    received2 = lax.all_to_all(message2, "row", 0, 0, tiled=True)
    tables, pool = column_tables()
    tables = jnp.asarray(tables, jnp.bfloat16)
    partial, done = link_first(received1, tables)
    return link_last(received2, tables, jnp.asarray(pool), partial, done)


def solution(mesh):
    return jax.shard_map(
        local,
        mesh=mesh,
        in_specs=(P(None, "row", None, "col"), P()),
        out_specs=P(None, None, "row", "col"),
        check_vma=False,
    )
```

time: 188 us -> 196 us (1.043)
  blocking collectives: 122 us -> 0 us
  waiting for transfers between devices: 0.01 us -> 119 us
  starting transfers between devices: 6.42 us -> 19.9 us
    all_to_all x1 -> x0, blocking collectives: 122 us -> none  [local(): received = lax.all_to_all(message, 'row', 0, 0, tiled=True)]
    all_to_all x0 -> x2, waiting for transfers between devices: none -> 116 us  [the longest x1 116 us: local(): received1 = lax.all_to_all(message1, 'row', 0, 0, tiled=True)]
    all_to_all x0 -> x2, starting transfers between devices: none -> 14.1 us  [the longest x1 8.65 us: local(): received1 = lax.all_to_all(message1, 'row', 0, 0, tiled=True)]
    ppermute x1, waiting for transfers between devices: 0.01 us -> 3.46 us  [local(): right = lax.ppermute(first, 'col', down)]
  transfers between devices with their start and end apart: 2 -> 4, of which waited for: 0 -> 2; matrix products, arithmetic and copies ran while one was open for 0% -> 0% of each run, Pallas kernels for 5% -> 16%
where the time goes in v2:
time: 196 us; the launch traced here: 195 us
  waiting for transfers between devices  119 us (61%)
  Pallas kernels  54.3 us (28%)
  starting transfers between devices  19.9 us (10%)
    all_to_all x1, waiting for transfers between devices, local(): received1 = lax.all_to_all(message1, 'row', 0, 0, tiled=True)  116 us
    pallas_call x1, Pallas kernels, link_first(): pl.pallas_call(first_kernel, grid=(FIRST,), in_specs=[pl.BlockSpec((DATES...  31.7 us
    pallas_call x1, Pallas kernels, link_last(): pl.pallas_call(last_kernel, grid=(1,), in_specs=[whole(DATES, MSG_ROWS, 1...  11 us
    pallas_call x1, Pallas kernels, pack(): pl.pallas_call(pack_kernel, grid=(TILES // GROUP,), in_specs=[pl.BlockSpe...  9.92 us
    all_to_all x1, starting transfers between devices, local(): received1 = lax.all_to_all(message1, 'row', 0, 0, tiled=True)  8.65 us
    all_to_all x1, starting transfers between devices, local(): received2 = lax.all_to_all(message2, 'row', 0, 0, tiled=True)  5.4 us
    ppermute x1, starting transfers between devices, local(): left = lax.ppermute(last, 'col', up)  3.96 us
  transfers between devices with their start and end apart: 4, of which 2 were waited for; matrix products, arithmetic and copies ran while one was open for 0% of the time, Pallas kernels for 16%

profile of v2, /device:TPU:1, one launch (start us, length us, event | category | flops | bytes accessed | tf_op | source)
XLA Modules:
  0.0 194.7 jit_solution(10746808838099211758)
XLA Ops:
  0.0 9.9 %pack.1 = (f32[16,208,640]{2,1,0:T(8,128)}, f32[16,208,128]{2,1,0:T(8,128)}, f32[2,1536]{1,0:T(2,128)}, f32[2,1536]{1,0:T(2,128)}) custom-call(s32[2,16]{1,0:T(2,128)} %bitcast.1, f32[2,1,1536,768]{3,2,1,0:T(8,128)} %after_ref.1, f32[2,1,1536,768]{3,2,1,0:T(8,128)} %after_ref.1, f32[2,1,1536,768]{3,2,1,0:T(8,128)} %after_ref.1), custom_call_target="tpu_custom_call" | custom-call | flops 1000000 | bytes 20000000 | tf_op jit(solution)/shard_map/pack/pallas_call | solution.py:120
  9.9 0.0 copy-start.4
  9.9 0.0 copy-start.3
  9.9 8.7 %all-to-all-start = ((f32[16,208,640]{2,1,0:T(8,128)}), f32[16,208,640]{2,1,0:T(8,128)}, u32[]{:S(2)}, u32[]{:S(2)}) async-start(f32[16,208,640]{2,1,0:T(8,128)} %get-tuple-element.16), calls=%async_computation | async-start | bytes 17039360 | tf_op jit(solution)/shard_map/all_to_all | solution.py:596
  18.6 0.0 copy-done.4
  18.6 4.0 %collective-permute-start = (f32[2,1536]{1,0:T(2,128)S(1)}, f32[2,1536]{1,0:T(2,128)S(1)}, u32[]{:S(2)}, u32[]{:S(2)}) collective-permute-start(f32[2,1536]{1,0:T(2,128)S(1)} %copy-done.4), channel_id=1, source_target_pairs={{0,1},{1,2},{2,3},{3,4},{4,5},{5,6},{6,7},{8,9},{9,10},{10,11},{11... | collective-permute-start | bytes 36872 | tf_op jit(solution)/shard_map/ppermute | solution.py:594
  22.6 0.0 copy-done.3
  22.6 1.9 collective-permute-start.1
  24.5 0.0 collective-permute-done.left_ref
  24.5 0.0 copy-start.1
  24.6 3.5 %collective-permute-done.1.right_ref = f32[2,1536]{1,0:T(2,128)S(1)} collective-permute-done((f32[2,1536]{1,0:T(2,128)S(1)}, f32[2,1536]{1,0:T(2,128)S(1)}, u32[]{:S(2)}, u32[]{:S(2)}) %collective-permute-start.1) | collective-permute-done | bytes 12320 | tf_op jit(solution)/shard_map/ppermute | solution.py:595
  28.0 0.0 copy-start.2
  28.0 115.7 %all-to-all-done.msg = f32[16,208,640]{2,1,0:T(8,128)} async-done(((f32[16,208,640]{2,1,0:T(8,128)}), f32[16,208,640]{2,1,0:T(8,128)}, u32[]{:S(2)}, u32[]{:S(2)}) %all-to-all-start) | async-done | bytes 8519712 | tf_op jit(solution)/shard_map/all_to_all | solution.py:596
  143.7 0.0 copy-done.1
  143.7 0.0 copy-done.2
  143.7 1.6 insert_edges.1
  145.3 5.4 %all-to-all-start.1 = ((f32[16,208,128]{2,1,0:T(8,128)}), f32[16,208,128]{2,1,0:T(8,128)S(1)}, u32[]{:S(2)}, u32[]{:S(2)}) async-start(f32[16,208,128]{2,1,0:T(8,128)} %insert_edges.1), calls=%async_computation.1 | async-start | bytes 3407872 | tf_op jit(solution)/shard_map/all_to_all | solution.py:599
  150.7 31.7 %link_first.1 = (f32[4608,128]{1,0:T(8,128)}, f32[2,16,16,256]{3,2,1,0:T(8,128)}) custom-call(f32[16,208,640]{2,1,0:T(8,128)} %all-to-all-done.msg, bf16[6,256,256]{2,1,0:T(8,128)(2,1)} %constant.4.clone.table), custom_call_target="tpu_custom_call" | custom-call | flops 1000000000 | bytes 10000000 | tf_op jit(solution)/shard_map/link_first/pallas_call | solution.py:536
  182.4 0.0 all-to-all-done.1.msg
  182.4 0.0 copy-start
  182.4 1.2 copy-done
  183.6 11.0 %link_last.1 = f32[2,16,16,256]{3,2,1,0:T(8,128)} custom-call(f32[16,208,128]{2,1,0:T(8,128)} %copy-done, bf16[6,256,256]{2,1,0:T(8,128)(2,1)} %constant.4.clone.table, f32[2,8,128]{2,1,0:T(8,128)} %constant.5.clone.pool, f32[4608,128]{1,0:T(8,128)} %get-tuple-element.21.partial, f32[2,16,16,256]{3,2,1,0:T(8,128)} %get-tuple-element.22.done), custom_call_target="tpu_custom_call" | custom-call | flops 100000000 | bytes 10000000 | tf_op jit(solution)/shard_map/link_last/pallas_call | solution.py:563
Async XLA Ops:
  9.9 8.7 %copy-start.4 = (f32[2,1536]{1,0:T(2,128)S(1)}, f32[2,1536]{1,0:T(2,128)}, u32[]{:S(2)}) copy-start(f32[2,1536]{1,0:T(2,128)} %get-tuple-element.14) | copy-start | bytes 36868
  9.9 12.7 %copy-start.3 = (f32[2,1536]{1,0:T(2,128)S(1)}, f32[2,1536]{1,0:T(2,128)}, u32[]{:S(2)}) copy-start(f32[2,1536]{1,0:T(2,128)} %get-tuple-element.15) | copy-start | bytes 36868
  9.9 133.7 %all-to-all-start = ((f32[16,208,640]{2,1,0:T(8,128)}), f32[16,208,640]{2,1,0:T(8,128)}, u32[]{:S(2)}, u32[]{:S(2)}) async-start(f32[16,208,640]{2,1,0:T(8,128)} %get-tuple-element.16), calls=%async_computation | async-start | bytes 17039360 | tf_op jit(solution)/shard_map/all_to_all | solution.py:596
  18.6 5.9 %collective-permute-start = (f32[2,1536]{1,0:T(2,128)S(1)}, f32[2,1536]{1,0:T(2,128)S(1)}, u32[]{:S(2)}, u32[]{:S(2)}) collective-permute-start(f32[2,1536]{1,0:T(2,128)S(1)} %copy-done.4), channel_id=1, source_target_pairs={{0,1},{1,2},{2,3},{3,4},{4,5},{5,6},{6,7},{8,9},{9,10},{10,11},{11... | collective-permute-start | bytes 36872 | tf_op jit(solution)/shard_map/ppermute | solution.py:594
  22.6 5.4 %collective-permute-start.1 = (f32[2,1536]{1,0:T(2,128)S(1)}, f32[2,1536]{1,0:T(2,128)S(1)}, u32[]{:S(2)}, u32[]{:S(2)}) collective-permute-start(f32[2,1536]{1,0:T(2,128)S(1)} %copy-done.3), channel_id=1, source_target_pairs={{1,0},{2,1},{3,2},{4,3},{5,4},{6,5},{7,6},{9,8},{10,9},{11,10},{12... | collective-permute-start | bytes 36872 | tf_op jit(solution)/shard_map/ppermute | solution.py:595
  24.5 119.2 %copy-start.1 = (f32[2,1536]{1,0:T(2,128)}, f32[2,1536]{1,0:T(2,128)S(1)}, u32[]{:S(2)}) copy-start(f32[2,1536]{1,0:T(2,128)S(1)} %collective-permute-done.left_ref) | copy-start | bytes 36868
  28.0 115.7 %copy-start.2 = (f32[2,1536]{1,0:T(2,128)}, f32[2,1536]{1,0:T(2,128)S(1)}, u32[]{:S(2)}) copy-start(f32[2,1536]{1,0:T(2,128)S(1)} %collective-permute-done.1.right_ref) | copy-start | bytes 36868
  145.3 37.1 %all-to-all-start.1 = ((f32[16,208,128]{2,1,0:T(8,128)}), f32[16,208,128]{2,1,0:T(8,128)S(1)}, u32[]{:S(2)}, u32[]{:S(2)}) async-start(f32[16,208,128]{2,1,0:T(8,128)} %insert_edges.1), calls=%async_computation.1 | async-start | bytes 3407872 | tf_op jit(solution)/shard_map/all_to_all | solution.py:599
  182.4 1.2 copy-start

commit v3 on v2

v3 whole, which is shorter than its diff:
```python
import functools

import jax
import jax.numpy as jnp
import numpy as np
from jax import lax
from jax.experimental import pallas as pl
from jax.experimental.pallas import tpu as pltpu
from jax.sharding import PartitionSpec as P

ITERS = 10
FLOOR = 20.0
DATES = 16
TILES = 16
COLS = 768
LANE_TILES = 6
FIRST = 5
OUT_COLS = 256
BLOCKS = 16
TILE_ROWS = 6 * BLOCKS
TILE_LANES = 192
ROWS1 = 1024
HALO1 = FIRST * TILE_LANES
ROWS2 = 208
HALO2 = TILE_LANES
EDGE_ROW = 202
GROUP1 = 4
GROUP2 = 8


def pair_groups():
    groups = []
    for i in range(0, DATES, 2):
        groups.append(([i], [i + 1]))
        rest = list(range(i + 2, DATES))
        for j in range(0, len(rest), 4):
            groups.append(([i, i + 1], rest[j : j + 4]))
    return groups


GROUPS = pair_groups()
PAIRS = [(t, u) for ts, us in GROUPS for t in ts for u in us]
PAIR_AT = {pair: i for i, pair in enumerate(PAIRS)}
FIELDS = DATES + 2 * len(PAIRS)
CHUNK = 512
SIDE = 512
VMEM_LIMIT = 56 * 1024 * 1024
FEEDS = ((0, 2), (0,), (0,), (0, 1), (1, 2), (2,))


def lane_columns():
    lane = np.arange(128)
    group_a = np.where(lane < 32, 128 + lane, lane)
    group_b = np.where((lane >= 32) & (lane < 96), 128 + lane, 128 + (lane + 64) % 128)
    own = np.where(lane < 32, lane, 128 + lane)
    other = (lane + 64) % 128
    far = np.where(other < 32, other, 128 + other)
    group_c = np.where((lane < 32) | (lane >= 96), own, far)
    return group_a, group_b, group_c


def column_tables():
    groups = lane_columns()
    tables = np.zeros((LANE_TILES, 256, 256), np.float32)
    for lt in range(LANE_TILES):
        column = (lt * 128 + np.arange(128) + 64) % COLS
        for place, group in enumerate(FEEDS[lt]):
            target = 3 * groups[group][None, :]
            inside = (column[:, None] >= target - 1) & (column[:, None] <= target + 3)
            for copy in range(2):
                tables[lt, copy * 128 : copy * 128 + 128, place * 128 : place * 128 + 128] = inside
    row = np.arange(128)
    pool = np.zeros((2, 8, 128), np.float32)
    for half in range(2):
        for s in range(8):
            block = 2 * s + half
            pool[half, s] = (row >= 6 * block) & (row <= 6 * block + 10)
    return tables, pool.reshape(16, 128)


def masked_rows(valid_ref, parts, step, span, rows_ref):
    me = lax.axis_index("row")
    low, high = valid_ref[0, me], valid_ref[1, me]
    count_out = rows_ref.shape[1]
    kept = []
    for which, (start, count) in enumerate(((-8, 8), (0, span), (span, 8))):
        row = lax.broadcasted_iota(jnp.int32, (count, 128), 0) + (step * span + start)
        keep = (row >= low) & (row < high)
        left = lax.broadcasted_iota(jnp.int32, (count, 128), 1) < 64
        for part in range(2):
            value = [jnp.where(keep, v, 0.0) for v in parts(which, part)]
            if which == 1:
                kept.append(value)
            turned = [pltpu.roll(v, 64, 1) for v in value]
            for lt in range(count_out):
                rows_ref[part, lt, pl.ds(start + 8, count), :] = jnp.where(
                    left, turned[lt], turned[(lt + 1) % len(turned)]
                )
    return kept


def spread(out, tile, base, first_row, rows_ref, lt):
    for part in range(2):
        for phase in range(6):
            for half in range(2):
                at = first_row + part * 96 + phase * 16 + half * 8
                out[tile, pl.ds(at, 8), :] = rows_ref[
                    part, lt, pl.ds(base + 6 * half + phase, 8, stride=12), :
                ]


def pack_first_kernel(valid_ref, before_ref, tile_ref, after_ref, out_ref, rows_ref):
    refs = (before_ref, tile_ref, after_ref)

    def parts(which, part):
        return [refs[which][part, 0, :, lt * 128 : lt * 128 + 128] for lt in range(LANE_TILES)]

    masked_rows(valid_ref, parts, pl.program_id(0), GROUP1 * TILE_ROWS, rows_ref)
    for tile in range(GROUP1):
        base = 5 + tile * TILE_ROWS
        out_ref[tile, pl.ds(ROWS1 - 16, 16), :] = jnp.zeros((16, 128), jnp.float32)
        for lt in range(FIRST):
            spread(out_ref, tile, base, lt * TILE_LANES, rows_ref, lt)
            for part in range(2):
                out_ref[tile, pl.ds(HALO1 + lt * 10 + 5 * part, 5), :] = rows_ref[
                    part, lt, pl.ds(base + TILE_ROWS, 5), :
                ]


def pack_last_kernel(
    valid_ref, l_before, l_tile, l_after, r_before, r_tile, r_after, out_ref, first_ref, last_ref,
    rows_ref,
):
    refs = ((r_before, l_before), (r_tile, l_tile), (r_after, l_after))

    def parts(which, part):
        return [ref[part, 0] for ref in refs[which]]

    kept = masked_rows(valid_ref, parts, pl.program_id(0), GROUP2 * TILE_ROWS, rows_ref)
    lane = lax.broadcasted_iota(jnp.int32, (8, 128), 1)
    for at, pick, out in ((1, 0, first_ref), (0, 127, last_ref)):
        for part in range(2):
            column = lax.dot_general(
                jnp.where(lane == pick, 1.0, 0.0), kept[part][at], (((1,), (1,)), ((), ())),
                precision=lax.Precision.HIGHEST, preferred_element_type=jnp.float32,
            )
            out[part : part + 1, :] = column[0:1, :]
    for tile in range(GROUP2):
        base = 5 + tile * TILE_ROWS
        spread(out_ref, tile, base, 0, rows_ref, 0)
        for part in range(2):
            out_ref[tile, pl.ds(HALO2 + 5 * part, 5), :] = rows_ref[
                part, 0, pl.ds(base + TILE_ROWS, 5), :
            ]
        out_ref[tile, pl.ds(EDGE_ROW, 6), :] = jnp.zeros((6, 128), jnp.float32)


def row_specs(span, width, column):
    eight = span // 8
    return [
        pl.BlockSpec((2, 1, 8, width), lambda i: (0, 0, jnp.maximum(i * eight - 1, 0), column)),
        pl.BlockSpec((2, 1, span, width), lambda i: (0, 0, i, column)),
        pl.BlockSpec(
            (2, 1, 8, width), lambda i: (0, 0, jnp.minimum(i * eight + eight, 191), column)
        ),
    ]


def pack_first(slc, valid):
    span = GROUP1 * TILE_ROWS
    return pl.pallas_call(
        pack_first_kernel,
        grid=(TILES // GROUP1,),
        in_specs=[pl.BlockSpec(memory_space=pltpu.SMEM)] + row_specs(span, COLS, 0),
        out_specs=pl.BlockSpec((GROUP1, ROWS1, 128), lambda i: (i, 0, 0)),
        out_shape=jax.ShapeDtypeStruct((TILES, ROWS1, 128), jnp.float32),
        scratch_shapes=[pltpu.VMEM((2, LANE_TILES, span + 16, 128), jnp.float32)],
        compiler_params=pltpu.CompilerParams(vmem_limit_bytes=VMEM_LIMIT),
        cost_estimate=pl.CostEstimate(flops=10**6, bytes_accessed=2 * 10**7, transcendentals=0),
        name="pack_first",
    )(valid, slc, slc, slc)


def pack_last(slc, valid):
    span = GROUP2 * TILE_ROWS
    column = jax.ShapeDtypeStruct((2, 1536), jnp.float32)
    return pl.pallas_call(
        pack_last_kernel,
        grid=(TILES // GROUP2,),
        in_specs=[pl.BlockSpec(memory_space=pltpu.SMEM)]
        + row_specs(span, 128, 0)
        + row_specs(span, 128, LANE_TILES - 1),
        out_specs=[
            pl.BlockSpec((GROUP2, ROWS2, 128), lambda i: (i, 0, 0)),
            pl.BlockSpec((2, span), lambda i: (0, i)),
            pl.BlockSpec((2, span), lambda i: (0, i)),
        ],
        out_shape=[jax.ShapeDtypeStruct((TILES, ROWS2, 128), jnp.float32), column, column],
        scratch_shapes=[pltpu.VMEM((2, 1, span + 16, 128), jnp.float32)],
        compiler_params=pltpu.CompilerParams(vmem_limit_bytes=VMEM_LIMIT),
        cost_estimate=pl.CostEstimate(flops=10**6, bytes_accessed=5 * 10**6, transcendentals=0),
        name="pack_last",
    )(valid, *([slc] * 6))


def insert_kernel(left_ref, right_ref, in_ref, out_ref, wide_ref):
    out_ref[...] = in_ref[...]
    wide_ref[...] = jnp.zeros_like(wide_ref)
    for side, ref in enumerate((left_ref, right_ref)):
        wide_ref[2 * side : 2 * side + 2, 128 : 128 + 1536] = ref[...]
    for tile in range(TILES):
        start = 128 + tile * TILE_ROWS - 3
        at = EDGE_ROW % 8
        out_ref[tile, at : at + 4, :] = wide_ref[0:4, start : start + 128]


def insert_edges(left, right, message):
    spec = pl.BlockSpec((TILES, 8, 128), lambda i: (0, EDGE_ROW // 8, 0))
    column = pl.BlockSpec((2, 1536), lambda i: (0, 0))
    return pl.pallas_call(
        insert_kernel,
        grid=(1,),
        in_specs=[column, column, spec],
        out_specs=spec,
        out_shape=jax.ShapeDtypeStruct(message.shape, message.dtype),
        input_output_aliases={2: 0},
        scratch_shapes=[pltpu.VMEM((8, 1920), jnp.float32)],
        name="insert_edges",
    )(left, right, message)


def split(x):
    high = x.astype(jnp.bfloat16)
    return high, (x - high.astype(jnp.float32)).astype(jnp.bfloat16)


def field_of(t, u):
    return t if t == u else DATES + 2 * PAIR_AT[t, u]


def cross_products(data, t_part, u_tile, lanes, rows):
    real = imag = None
    for re_row, im_row in rows:
        a_t = data[re_row, pl.ds(t_part, 1), lanes]
        b_t = data[im_row, pl.ds(t_part, 1), lanes]
        a_u = data[re_row, pl.ds(u_tile * 8, 8), lanes]
        b_u = data[im_row, pl.ds(u_tile * 8, 8), lanes]
        re = a_t * a_u + b_t * b_u
        im = b_t * a_u - a_t * b_u
        real = re if real is None else real + re
        imag = im if imag is None else imag + im
    return real, imag


def dot(a, b):
    return jnp.dot(a, b, preferred_element_type=jnp.float32)


def main_products(msg, sums, lhs, pooled):
    last = lax.broadcasted_iota(jnp.int32, (8, 128), 0) == 7
    state = {"fields": 0, "chunks": 0}

    def load(kind, date, phase, half):
        source = msg if kind in "ab" else sums
        base = 0 if kind in "as" else 96
        return source[date, pl.ds(base + phase * 16 + half * 8, 8), :]

    def emit(field, first, whole):
        out0 = whole[0] + first[1]
        rolled = jnp.where(last, 0.0, pltpu.roll(first[0], 7, 0))
        out1 = whole[1] + rolled
        high, low = split(jnp.concatenate([out0, out1], axis=0))
        lhs[pl.ds(field * 16, 16), 0:128] = high
        lhs[pl.ds(field * 16, 16), 128:256] = low
        state["fields"] += 1

    def drain():
        while (state["chunks"] + 1) * CHUNK <= state["fields"] * 16:
            pooled(state["chunks"])
            state["chunks"] += 1

    for t in range(DATES):
        first, whole = [], []
        for half in range(2):
            total = None
            for phase in range(6):
                a, b = load("a", t, phase, half), load("b", t, phase, half)
                term = a * a + b * b
                if phase == 5:
                    first.append(total)
                total = term if total is None else total + term
            whole.append(total)
        emit(t, first, whole)

    for ts, us in GROUPS:
        pairs = [(t, u) for t in ts for u in us]
        first = {pair: ([], []) for pair in pairs}
        whole = {pair: ([], []) for pair in pairs}
        for half in range(2):
            acc = {}
            for phase in range(6):
                s_t = {t: load("s", t, phase, half) for t in ts}
                a_t = {t: load("a", t, phase, half) for t in ts}
                b_t = {t: load("b", t, phase, half) for t in ts}
                a_u = {u: load("a", u, phase, half) for u in us}
                s_u = {u: load("s", u, phase, half) for u in us}
                d_u = {u: load("d", u, phase, half) for u in us}
                for t, u in pairs:
                    p = a_u[u] * s_t[t]
                    q = d_u[u] * b_t[t]
                    r = s_u[u] * a_t[t]
                    if phase == 0:
                        acc[t, u] = (p, q, r)
                    elif phase < 5:
                        p0, q0, r0 = acc[t, u]
                        acc[t, u] = (p0 + p, q0 + q, r0 + r)
                    else:
                        p0, q0, r0 = acc[t, u]
                        re5, im5 = p0 - q0, p0 - r0
                        first[t, u][0].append(re5)
                        first[t, u][1].append(im5)
                        whole[t, u][0].append(re5 + (p - q))
                        whole[t, u][1].append(im5 + (p - r))
        for pair in pairs:
            for part in range(2):
                emit(field_of(*pair) + part, first[pair][part], whole[pair][part])
        drain()


def dot(a, b):
    return jnp.dot(a, b, preferred_element_type=jnp.float32)


def side_products(small, t, rows, put):
    for u_tile in range(2):
        if u_tile < t // 8:
            values = (jnp.zeros((8, 128), jnp.float32),) * 2
        else:
            values = cross_products(small, t, u_tile, pl.ds(0, 128), rows)
        for part in range(2):
            put(part * 256 + t * 16 + u_tile * 8, values[part])


def fill_sums(msg, sums):
    def fill(date, carry):
        a = msg[date, pl.ds(0, 96), :]
        b = msg[date, pl.ds(96, 96), :]
        sums[date, pl.ds(0, 96), :] = a + b
        sums[date, pl.ds(96, 96), :] = a - b
        return carry

    lax.fori_loop(0, DATES, fill, 0, unroll=2)


def halo_products(small, side_lhs):
    def put(at, value):
        side_lhs[pl.ds(at, 8), :] = value

    for t in range(DATES):
        side_products(small, t, [(p, 5 + p) for p in range(5)], put)


def pool_side(side_lhs, table):
    high, low = split(side_lhs[...])
    return dot(jnp.concatenate([high, low], axis=1), table[0])


def chunk_rows(chunk):
    return pl.ds(chunk * CHUNK, CHUNK)


def first_kernel(
    msg, below_msg, table, part_out, out, sums, lhs, small, side_lhs, res, halo, coh, vec, weight,
    rows,
):
    step = pl.program_id(0)
    fill_sums(msg, sums)
    for date in range(DATES):
        for row in range(10):
            small[row, date : date + 1, :] = below_msg[date, pl.ds(step * 10 + row, 1), :]
    halo_products(small, side_lhs)
    halo[step] = pool_side(side_lhs, table)

    def pooled(chunk):
        res[step, chunk_rows(chunk), :] = dot(lhs[chunk_rows(chunk), :], table[0])

    main_products(msg, sums, lhs, pooled)

    @pl.when(step == FIRST - 1)
    def _():
        lane = lax.broadcasted_iota(jnp.int32, (8, 128), 1)
        last = lax.broadcasted_iota(jnp.int32, (8, 128), 0) == 7

        def total(ref, group, at, count):
            value = None
            for lt in range(FIRST):
                if group in FEEDS[lt]:
                    place = FEEDS[lt].index(group) * 128
                    own = ref[lt, pl.ds(at, count), place : place + 128]
                    value = own if value is None else value + own
            return value

        def below(group, t, u, part):
            return total(halo, group, part * 256 + t * 16 + u, 1)

        def paired(group, even, t, u, part):
            at = (field_of(t, u) + part) * 16
            value = jnp.where(even, total(res, group, at, 8), total(res, group, at + 8, 8))
            return value + jnp.where(last & ~even, below(group, t, u, part), 0.0)

        even = (lane < 32) | (lane >= 96)
        for t in range(DATES):
            for u in range(t, DATES):
                for part in range(1 if t == u else 2):
                    at = (field_of(t, u) + part) * 8
                    part_out[pl.ds(at, 8), :] = paired(2, even, t, u, part)

        for half in range(2):

            def cov(t, u, part):
                value = total(res, 0, (field_of(t, u) + part) * 16 + half * 8, 8)
                if half == 1:
                    value = value + jnp.where(last, below(0, t, u, part), 0.0)
                return value

            solve(cov, coh, vec, weight)
            for date in range(DATES):
                for part in range(2):
                    rows[part, date, 0, pl.ds(half, 8, stride=2), :] = vec[part, date]

        even_b = (lane >= 32) & (lane < 96)
        solve(functools.partial(paired, 1, even_b), coh, vec, weight)
        for date in range(DATES):
            for part in range(2):
                value = vec[part, date]
                rows[part, date, 1, pl.ds(0, 8, stride=2), :] = value
                rows[part, date, 1, pl.ds(1, 8, stride=2), :] = pltpu.roll(value, 64, 1)
        out[:, :, :, 0:128] = rows[:, :, 0]
        left = lax.broadcasted_iota(jnp.int32, (2, DATES, BLOCKS, 128), 3) < 32
        out[:, :, :, 128:256] = jnp.where(left, rows[:, :, 0], rows[:, :, 1])


def last_kernel(
    msg, table, pool, partial_hbm, done_hbm, out, sums, lhs, small, side_lhs, res, halo,
    pairs, edge, coh, vec, weight, rows, partial, done, sems,
):
    copies = [
        pltpu.make_async_copy(partial_hbm, partial, sems.at[0]),
        pltpu.make_async_copy(done_hbm, done, sems.at[1]),
    ]
    for copy in copies:
        copy.start()
    fill_sums(msg, sums)
    for date in range(DATES):
        for row in range(14):
            small[row, date : date + 1, :] = msg[date, HALO2 + row : HALO2 + row + 1, :]
    halo_products(small, side_lhs)
    high, low = split(side_lhs[...])
    halo[...] = dot(jnp.concatenate([high, low], axis=1), table[0])
    for side in range(2):
        row = 10 + 2 * side

        def put(at, value):
            pairs[pl.ds(2 * at + 1 - side, 8, stride=2), :] = value

        for t in range(DATES):
            side_products(small, t, [(row, row + 1)], put)
    dims = (((1,), (1,)), ((), ()))
    high, low = split(pairs[...])
    pool2 = pool[...].astype(jnp.bfloat16)
    sides = lax.dot_general(
        pool2, high, dims, preferred_element_type=jnp.float32
    ) + lax.dot_general(pool2, low, dims, preferred_element_type=jnp.float32)
    lower = lax.broadcasted_iota(jnp.int32, (8, 128), 1) < 64
    for group in range(SIDE // 64):
        tile = slice(group * 128, group * 128 + 128)
        even_rows, odd_rows = sides[0:8, tile], sides[8:16, tile]
        edge[2 * group] = jnp.where(lower, even_rows, pltpu.roll(odd_rows, 64, 1))
        edge[2 * group + 1] = jnp.where(lower, pltpu.roll(even_rows, 64, 1), odd_rows)

    def pooled(chunk):
        res[chunk_rows(chunk), :] = dot(lhs[chunk_rows(chunk), :], table[0])

    main_products(msg, sums, lhs, pooled)

    lane = lax.broadcasted_iota(jnp.int32, (8, 128), 1)
    last = lax.broadcasted_iota(jnp.int32, (8, 128), 0) == 7
    even = (lane < 32) | (lane >= 96)
    beside = (lane == 0) | (lane == 127) | (lane == 63) | (lane == 64)
    for copy in copies:
        copy.wait()

    def cov(t, u, part):
        field = field_of(t, u) + part
        at = field * 16
        value = jnp.where(even, res[pl.ds(at, 8), :], res[pl.ds(at + 8, 8), :])
        index = part * 256 + t * 16 + u
        value = value + jnp.where(last & ~even, halo[pl.ds(index, 1), :], 0.0)
        turned = pltpu.roll(edge[index // 32], (127 - 2 * (index % 32)) % 128, 1)
        return value + partial[pl.ds(field * 8, 8), :] + jnp.where(beside, turned, 0.0)

    solve(cov, coh, vec, weight)
    for date in range(DATES):
        for part in range(2):
            value = vec[part, date]
            rows[part, date, 0, pl.ds(0, 8, stride=2), :] = value
            rows[part, date, 0, pl.ds(1, 8, stride=2), :] = pltpu.roll(value, 64, 1)
    place = lax.broadcasted_iota(jnp.int32, (2, DATES, BLOCKS, 128), 3)
    out[:, :, :, 0:128] = jnp.where(place < 32, rows[:, :, 0], done[:, :, :, 0:128])
    out[:, :, :, 128:256] = jnp.where(place >= 96, rows[:, :, 0], done[:, :, :, 128:256])


def inverse_norm(vec):
    terms = [vec[part, t] * vec[part, t] for t in range(DATES) for part in range(2)]
    while len(terms) > 1:
        terms = [terms[i] + terms[i + 1] for i in range(0, len(terms), 2)]
    return lax.rsqrt(terms[0])


def solve(cov, coh, vec, weight):
    inv = []
    for t in range(DATES):
        diag = cov(t, t, 0)
        root = lax.rsqrt(jnp.maximum(diag, FLOOR))
        inv.append(root)
        weight[t] = diag * (root * root) + 1.0
    for i, (t, u) in enumerate(PAIRS):
        factor = inv[t] * inv[u]
        real = cov(t, u, 0) * factor
        imag = cov(t, u, 1) * factor
        coh[i, 0] = real
        coh[i, 1] = real + imag
        coh[i, 2] = imag - real
    for t in range(DATES):
        vec[0, t] = jnp.full((8, 128), 0.25, jnp.float32)
        vec[1, t] = jnp.zeros((8, 128), jnp.float32)
        vec[2, t] = jnp.full((8, 128), 0.25, jnp.float32)

    def iterate(_, carry):
        scale = inverse_norm(vec)
        new_real, new_imag = [None] * DATES, [None] * DATES
        sums = [[None, None, None] for _ in range(DATES)]

        def add(t, which, value, minus=False):
            if sums[t][which] is None:
                sums[t][which] = -value if minus else value
            elif minus:
                sums[t][which] = sums[t][which] - value
            else:
                sums[t][which] = sums[t][which] + value

        def pair(t, u, v):
            i = PAIR_AT[t, u]
            real, plus, minus = coh[i, 0], coh[i, 1], coh[i, 2]
            add(t, 0, real * v[u][2])
            add(t, 1, plus * v[u][1])
            add(t, 2, minus * v[u][0])
            add(u, 0, real * v[t][2])
            add(u, 1, minus * v[t][1], True)
            add(u, 2, plus * v[t][0], True)

        for first in range(0, DATES, 4):
            for second in range(first, DATES, 4):
                dates = sorted(set(range(first, first + 4)) | set(range(second, second + 4)))
                v = {t: (vec[0, t], vec[1, t], vec[2, t]) for t in dates}
                for t in range(first, first + 4):
                    for u in range(second, second + 4):
                        if t < u:
                            pair(t, u, v)
        for t in range(DATES):
            own = weight[t]
            new_real[t] = (sums[t][0] - sums[t][1]) + own * vec[0, t]
            new_imag[t] = (sums[t][0] + sums[t][2]) + own * vec[1, t]
        for t in range(DATES):
            real, imag = new_real[t] * scale, new_imag[t] * scale
            vec[0, t] = real
            vec[1, t] = imag
            vec[2, t] = real + imag
        return carry

    lax.fori_loop(0, ITERS, iterate, 0)
    scale = inverse_norm(vec)
    for t in range(DATES):
        for part in range(2):
            vec[part, t] = vec[part, t] * scale


def whole(*shape):
    return pl.BlockSpec(shape, lambda i: (0,) * len(shape))


def common_scratch(small_rows):
    return [
        pltpu.VMEM((DATES, TILE_LANES, 128), jnp.float32),
        pltpu.VMEM((FIELDS * 16, 256), jnp.bfloat16),
        pltpu.VMEM((small_rows, DATES, 128), jnp.float32),
        pltpu.VMEM((SIDE, 128), jnp.float32),
    ]


SOLVE_SCRATCH = [
    pltpu.VMEM((len(PAIRS), 3, 8, 128), jnp.float32),
    pltpu.VMEM((3, DATES, 8, 128), jnp.float32),
    pltpu.VMEM((DATES, 8, 128), jnp.float32),
]
LINKED = (2, DATES, BLOCKS, OUT_COLS)
PARTIAL = (FIELDS * 8, 128)


def link_first(message, tables):
    return pl.pallas_call(
        first_kernel,
        grid=(FIRST,),
        in_specs=[
            pl.BlockSpec((DATES, TILE_LANES, 128), lambda i: (0, i, 0)),
            pl.BlockSpec((DATES, 64, 128), lambda i: (0, HALO1 // 64, 0)),
            pl.BlockSpec((1, 256, 256), lambda i: (i, 0, 0)),
        ],
        out_specs=[whole(*PARTIAL), whole(*LINKED)],
        out_shape=[
            jax.ShapeDtypeStruct(PARTIAL, jnp.float32),
            jax.ShapeDtypeStruct(LINKED, jnp.float32),
        ],
        scratch_shapes=common_scratch(10)
        + [
            pltpu.VMEM((FIRST, FIELDS * 16, 256), jnp.float32),
            pltpu.VMEM((FIRST, SIDE, 256), jnp.float32),
        ]
        + SOLVE_SCRATCH
        + [pltpu.VMEM((2, DATES, 2, BLOCKS, 128), jnp.float32)],
        compiler_params=pltpu.CompilerParams(vmem_limit_bytes=VMEM_LIMIT),
        cost_estimate=pl.CostEstimate(flops=10**9, bytes_accessed=10**7, transcendentals=0),
        name="link_first",
    )(message, message, tables)


def link_last(message, tables, pool, partial, done):
    return pl.pallas_call(
        last_kernel,
        grid=(1,),
        in_specs=[
            whole(DATES, ROWS2, 128),
            pl.BlockSpec((1, 256, 128), lambda i: (FIRST, 0, 0)),
            whole(16, 128),
            pl.BlockSpec(memory_space=pl.ANY),
            pl.BlockSpec(memory_space=pl.ANY),
        ],
        out_specs=whole(*LINKED),
        out_shape=jax.ShapeDtypeStruct(LINKED, jnp.float32),
        scratch_shapes=common_scratch(14)
        + [
            pltpu.VMEM((FIELDS * 16, 128), jnp.float32),
            pltpu.VMEM((SIDE, 128), jnp.float32),
            pltpu.VMEM((2 * SIDE, 128), jnp.float32),
            pltpu.VMEM((SIDE // 32, 8, 128), jnp.float32),
        ]
        + SOLVE_SCRATCH
        + [
            pltpu.VMEM((2, DATES, 1, BLOCKS, 128), jnp.float32),
            pltpu.VMEM(PARTIAL, jnp.float32),
            pltpu.VMEM(LINKED, jnp.float32),
            pltpu.SemaphoreType.DMA((2,)),
        ],
        compiler_params=pltpu.CompilerParams(vmem_limit_bytes=VMEM_LIMIT),
        cost_estimate=pl.CostEstimate(flops=10**8, bytes_accessed=10**7, transcendentals=0),
        name="link_last",
    )(message, tables, pool, partial, done)


def local(slc, valid_rows):
    size = lax.axis_size("col")
    up = [(i, i + 1) for i in range(size - 1)]
    down = [(i + 1, i) for i in range(size - 1)]
    valid = valid_rows.T
    message2, first, last = pack_last(slc, valid)
    left = lax.ppermute(last, "col", up)
    right = lax.ppermute(first, "col", down)
    slc, message2 = lax.optimization_barrier((slc, message2))
    message1 = pack_first(slc, valid)
    message2 = insert_edges(left, right, message2)
    message1, message2 = lax.optimization_barrier((message1, message2))
    received1 = lax.all_to_all(message1, "row", 0, 0, tiled=True)
    received1, message2 = lax.optimization_barrier((received1, message2))
    received2 = lax.all_to_all(message2, "row", 0, 0, tiled=True)
    tables, pool = column_tables()
    tables = jnp.asarray(tables, jnp.bfloat16)
    partial, done = link_first(received1, tables)
    return link_last(received2, tables, jnp.asarray(pool), partial, done)


def solution(mesh):
    return jax.shard_map(
        local,
        mesh=mesh,
        in_specs=(P(None, "row", None, "col"), P()),
        out_specs=P(None, None, "row", "col"),
        check_vma=False,
    )
```

time: 196 us -> 168 us (0.86)
  waiting for transfers between devices: 119 us -> 6.02 us
  blocking collectives: 0 us -> 103 us
  starting transfers between devices: 19.9 us -> 10.1 us
  Pallas kernels: 54.3 us -> 45.9 us
    all_to_all x1 -> x0, waiting for transfers between devices: 116 us -> none  [local(): received1 = lax.all_to_all(message1, 'row', 0, 0, tiled=True)]
    all_to_all x0 -> x1, blocking collectives: none -> 103 us  [local(): received1 = lax.all_to_all(message1, 'row', 0, 0, tiled=True)]
    pallas_call x1, Pallas kernels: 31.7 us -> 22.7 us  [link_first(): pl.pallas_call(first_kernel, grid=(FIRST,), in_specs=[pl.BlockSpec((DATES...]
    all_to_all x1 -> x0, starting transfers between devices: 8.65 us -> none  [local(): received1 = lax.all_to_all(message1, 'row', 0, 0, tiled=True)]
    all_to_all x1, waiting for transfers between devices: 0.01 us -> 6.01 us  [local(): received2 = lax.all_to_all(message2, 'row', 0, 0, tiled=True)]
    ppermute x1, waiting for transfers between devices: 3.46 us -> 0.01 us  [local(): right = lax.ppermute(first, 'col', down)]
    pallas_call x2 -> x3, Pallas kernels: 21 us -> 21.5 us  [the longest x1 8.82 us: pack_first(): pl.pallas_call(pack_first_kernel, grid=(TILES // GROUP1,), in_specs=[pl.B...]
  transfers between devices with their start and end apart: 4 -> 3, of which waited for: 2 -> 1; matrix products, arithmetic and copies ran while one was open for 0% -> 0% of each run, Pallas kernels for 16% -> 19%
where the time goes in v3:
time: 168 us; the launch traced here: 167 us
  blocking collectives  103 us (61%)
  Pallas kernels  45.9 us (27%)
  starting transfers between devices  10.1 us (6%)
  waiting for transfers between devices  6.02 us (4%)
  local copies, waits for them, and re-layouts  2.4 us (1%)
    all_to_all x1, blocking collectives, local(): received1 = lax.all_to_all(message1, 'row', 0, 0, tiled=True)  103 us
    pallas_call x1, Pallas kernels, link_first(): pl.pallas_call(first_kernel, grid=(FIRST,), in_specs=[pl.BlockSpec((DATES...  22.7 us
    pallas_call x1, Pallas kernels, pack_first(): pl.pallas_call(pack_first_kernel, grid=(TILES // GROUP1,), in_specs=[pl.B...  8.82 us
    pallas_call x1, Pallas kernels, link_last(): pl.pallas_call(last_kernel, grid=(1,), in_specs=[whole(DATES, ROWS2, 128)...  7.45 us
    all_to_all x1, waiting for transfers between devices, local(): received2 = lax.all_to_all(message2, 'row', 0, 0, tiled=True)  6.01 us
    pallas_call x1, Pallas kernels, pack_last(): pl.pallas_call(pack_last_kernel, grid=(TILES // GROUP2,), in_specs=[pl.Bl...  5.27 us
    ppermute x1, starting transfers between devices, local(): left = lax.ppermute(last, 'col', up)  4.51 us
    all_to_all x1, starting transfers between devices, local(): received2 = lax.all_to_all(message2, 'row', 0, 0, tiled=True)  3.71 us
  transfers between devices with their start and end apart: 3, of which 1 were waited for; matrix products, arithmetic and copies ran while one was open for 0% of the time, Pallas kernels for 19%

profile of v3, /device:TPU:1, one launch (start us, length us, event | category | flops | bytes accessed | tf_op | source)
XLA Modules:
  0.0 167.3 jit_solution(8300645848159832449)
XLA Ops:
  0.0 5.3 %pack_last.1 = (f32[16,208,128]{2,1,0:T(8,128)}, f32[2,1536]{1,0:T(2,128)}, f32[2,1536]{1,0:T(2,128)}) custom-call(s32[2,16]{1,0:T(2,128)} %bitcast.1, f32[2,1,1536,768]{3,2,1,0:T(8,128)} %after_ref, f32[2,1,1536,768]{3,2,1,0:T(8,128)} %after_ref, f32[2,1,1536,768]{3,2,1,0:T(8,128)} %after_ref, f32[2,1,1536,768]{3,2,1,0:T(8,128)} %after_ref, ...), custom_call_target="tpu_custom_call" | custom-call | flops 1000000 | bytes 5000000 | tf_op jit(solution)/shard_map/pack_last/pallas_call | solution.py:187
  5.3 4.5 %collective-permute-start = (f32[2,1536]{1,0:T(2,128)}, f32[2,1536]{1,0:T(2,128)S(1)}, u32[]{:S(2)}, u32[]{:S(2)}) collective-permute-start(f32[2,1536]{1,0:T(2,128)} %get-tuple-element.18), channel_id=1, source_target_pairs={{0,1},{1,2},{2,3},{3,4},{4,5},{5,6},{6,7},{8,9},{9,10},{10,11},{11... | collective-permute-start | bytes 36872 | tf_op jit(solution)/shard_map/ppermute | solution.py:676
  9.8 1.9 %collective-permute-start.1 = (f32[2,1536]{1,0:T(2,128)}, f32[2,1536]{1,0:T(2,128)S(1)}, u32[]{:S(2)}, u32[]{:S(2)}) collective-permute-start(f32[2,1536]{1,0:T(2,128)} %get-tuple-element.19), channel_id=1, source_target_pairs={{1,0},{2,1},{3,2},{4,3},{5,4},{6,5},{7,6},{9,8},{10,9},{11,10},{12... | collective-permute-start | bytes 36872 | tf_op jit(solution)/shard_map/ppermute | solution.py:677
  11.7 8.8 %pack_first.1 = f32[16,1024,128]{2,1,0:T(8,128)} custom-call(s32[2,16]{1,0:T(2,128)} %bitcast.2, f32[2,1,1536,768]{3,2,1,0:T(8,128)} %after_ref, f32[2,1,1536,768]{3,2,1,0:T(8,128)} %after_ref, f32[2,1,1536,768]{3,2,1,0:T(8,128)} %after_ref), custom_call_target="tpu_custom_call" | custom-call | flops 1000000 | bytes 20000000 | tf_op jit(solution)/shard_map/pack_first/pallas_call | solution.py:171
  20.5 0.0 collective-permute-done.left_ref
  20.5 0.0 copy-start.1
  20.5 0.0 collective-permute-done.1.right_ref
  20.6 0.6 copy-done.1
  21.1 0.0 copy-start.2
  21.1 0.6 copy-done.2
  21.7 1.6 insert_edges.1
  23.4 102.8 %all_to_all.10.msg.below_msg = f32[16,1024,128]{2,1,0:T(8,128)} all-to-all(f32[16,1024,128]{2,1,0:T(8,128)} %pack_first.1), channel_id=1, replica_groups=mesh['row'=16,'col'=8] {'row'}, dimensions={0} | all-to-all | bytes 16777216 | tf_op jit(solution)/shard_map/all_to_all | solution.py:682
  126.1 3.7 %all-to-all-start.1 = ((f32[16,208,128]{2,1,0:T(8,128)}), f32[16,208,128]{2,1,0:T(8,128)S(1)}, u32[]{:S(2)}, u32[]{:S(2)}) async-start(f32[16,208,128]{2,1,0:T(8,128)} %insert_edges.1), calls=%async_computation.1 | async-start | bytes 3407872 | tf_op jit(solution)/shard_map/all_to_all | solution.py:684
  129.9 22.7 %link_first.1 = (f32[2048,128]{1,0:T(8,128)}, f32[2,16,16,256]{3,2,1,0:T(8,128)}) custom-call(f32[16,1024,128]{2,1,0:T(8,128)} %all_to_all.10.msg.below_msg, f32[16,1024,128]{2,1,0:T(8,128)} %all_to_all.10.msg.below_msg, bf16[6,256,256]{2,1,0:T(8,128)(2,1)} %constant.4.clone.table), custom_call_target="tpu_custom_call" | custom-call | flops 1000000000 | bytes 10000000 | tf_op jit(solution)/shard_map/link_first/pallas_call | solution.py:611
  152.6 6.0 %all-to-all-done.1.msg = f32[16,208,128]{2,1,0:T(8,128)S(1)} async-done(((f32[16,208,128]{2,1,0:T(8,128)}), f32[16,208,128]{2,1,0:T(8,128)S(1)}, u32[]{:S(2)}, u32[]{:S(2)}) %all-to-all-start.1) | async-done | bytes 1703968 | tf_op jit(solution)/shard_map/all_to_all | solution.py:684
  158.6 0.0 copy-start
  158.6 1.2 copy-done
  159.8 7.5 %link_last.1 = f32[2,16,16,256]{3,2,1,0:T(8,128)} custom-call(f32[16,208,128]{2,1,0:T(8,128)} %copy-done, bf16[6,256,256]{2,1,0:T(8,128)(2,1)} %constant.4.clone.table, f32[16,128]{1,0:T(8,128)} %constant.5.clone.pool, f32[2048,128]{1,0:T(8,128)} %get-tuple-element.25.partial_hbm, f32[2,16,16,256]{3,2,1,0:T(8,128)} %get-tuple-element.26.done_hbm), custom_call_target="tpu_custom_call" | custom-call | flops 100000000 | bytes 10000000 | tf_op jit(solution)/shard_map/link_last/pallas_call | solution.py:638
Async XLA Ops:
  5.3 15.3 %collective-permute-start = (f32[2,1536]{1,0:T(2,128)}, f32[2,1536]{1,0:T(2,128)S(1)}, u32[]{:S(2)}, u32[]{:S(2)}) collective-permute-start(f32[2,1536]{1,0:T(2,128)} %get-tuple-element.18), channel_id=1, source_target_pairs={{0,1},{1,2},{2,3},{3,4},{4,5},{5,6},{6,7},{8,9},{9,10},{10,11},{11... | collective-permute-start | bytes 36872 | tf_op jit(solution)/shard_map/ppermute | solution.py:676
  9.8 10.8 %collective-permute-start.1 = (f32[2,1536]{1,0:T(2,128)}, f32[2,1536]{1,0:T(2,128)S(1)}, u32[]{:S(2)}, u32[]{:S(2)}) collective-permute-start(f32[2,1536]{1,0:T(2,128)} %get-tuple-element.19), channel_id=1, source_target_pairs={{1,0},{2,1},{3,2},{4,3},{5,4},{6,5},{7,6},{9,8},{10,9},{11,10},{12... | collective-permute-start | bytes 36872 | tf_op jit(solution)/shard_map/ppermute | solution.py:677
  20.5 0.6 copy-start.1
  21.1 0.6 copy-start.2
  126.1 32.5 %all-to-all-start.1 = ((f32[16,208,128]{2,1,0:T(8,128)}), f32[16,208,128]{2,1,0:T(8,128)S(1)}, u32[]{:S(2)}, u32[]{:S(2)}) async-start(f32[16,208,128]{2,1,0:T(8,128)} %insert_edges.1), calls=%async_computation.1 | async-start | bytes 3407872 | tf_op jit(solution)/shard_map/all_to_all | solution.py:684
  158.6 1.2 copy-start

commit v4 on v3

--- a/solution.py
+++ b/solution.py
@@ -21,11 +21,12 @@
 TILE_LANES = 192
 ROWS1 = 1024
 HALO1 = FIRST * TILE_LANES
+OWN_TILE = 1008
+OWN_ROW = 1010
 ROWS2 = 208
 HALO2 = TILE_LANES
-EDGE_ROW = 202
-GROUP1 = 4
-GROUP2 = 8
+WINDOW = TILE_ROWS + 5
+GROUP = 4
 
 
 def pair_groups():
@@ -44,7 +45,6 @@
 FIELDS = DATES + 2 * len(PAIRS)
 CHUNK = 512
 SIDE = 512
-VMEM_LIMIT = 56 * 1024 * 1024
 FEEDS = ((0, 2), (0,), (0,), (0, 1), (1, 2), (2,))
 
 
@@ -78,155 +78,81 @@
     return tables, pool.reshape(16, 128)
 
 
-def masked_rows(valid_ref, parts, step, span, rows_ref):
+def pack_kernel(valid_ref, before_ref, tile_ref, after_ref, out1_ref, out2_ref, rows_ref):
     me = lax.axis_index("row")
+    step = pl.program_id(0)
     low, high = valid_ref[0, me], valid_ref[1, me]
-    count_out = rows_ref.shape[1]
-    kept = []
-    for which, (start, count) in enumerate(((-8, 8), (0, span), (span, 8))):
+    span = GROUP * TILE_ROWS
+    for ref, start, count in ((before_ref, -8, 8), (tile_ref, 0, span), (after_ref, span, 8)):
         row = lax.broadcasted_iota(jnp.int32, (count, 128), 0) + (step * span + start)
         keep = (row >= low) & (row < high)
         left = lax.broadcasted_iota(jnp.int32, (count, 128), 1) < 64
         for part in range(2):
-            value = [jnp.where(keep, v, 0.0) for v in parts(which, part)]
-            if which == 1:
-                kept.append(value)
-            turned = [pltpu.roll(v, 64, 1) for v in value]
-            for lt in range(count_out):
+            turned = []
+            for lt in range(LANE_TILES):
+                value = ref[part, 0, :, lt * 128 : lt * 128 + 128]
+                turned.append(pltpu.roll(jnp.where(keep, value, 0.0), 64, 1))
+            for lt in range(LANE_TILES):
                 rows_ref[part, lt, pl.ds(start + 8, count), :] = jnp.where(
-                    left, turned[lt], turned[(lt + 1) % len(turned)]
+                    left, turned[lt], turned[(lt + 1) % LANE_TILES]
                 )
-    return kept
-
-
-def spread(out, tile, base, first_row, rows_ref, lt):
-    for part in range(2):
-        for phase in range(6):
-            for half in range(2):
-                at = first_row + part * 96 + phase * 16 + half * 8
-                out[tile, pl.ds(at, 8), :] = rows_ref[
-                    part, lt, pl.ds(base + 6 * half + phase, 8, stride=12), :
-                ]
-
-
-def pack_first_kernel(valid_ref, before_ref, tile_ref, after_ref, out_ref, rows_ref):
-    refs = (before_ref, tile_ref, after_ref)
-
-    def parts(which, part):
-        return [refs[which][part, 0, :, lt * 128 : lt * 128 + 128] for lt in range(LANE_TILES)]
-
-    masked_rows(valid_ref, parts, pl.program_id(0), GROUP1 * TILE_ROWS, rows_ref)
-    for tile in range(GROUP1):
+    lane = lax.broadcasted_iota(jnp.int32, (8, 128), 1)
+    row = lax.broadcasted_iota(jnp.int32, (8, 128), 0)
+    pick = jnp.where(((row == 0) & (lane == 64)) | ((row == 1) & (lane == 63)), 1.0, 0.0)
+    for tile in range(GROUP):
         base = 5 + tile * TILE_ROWS
-        out_ref[tile, pl.ds(ROWS1 - 16, 16), :] = jnp.zeros((16, 128), jnp.float32)
-        for lt in range(FIRST):
-            spread(out_ref, tile, base, lt * TILE_LANES, rows_ref, lt)
+        out1_ref[tile, pl.ds(ROWS1 - 16, 16), :] = jnp.zeros((16, 128), jnp.float32)
+        out2_ref[tile, pl.ds(ROWS2 - 16, 16), :] = jnp.zeros((16, 128), jnp.float32)
+        for part in range(2):
+            columns = lax.dot_general(
+                pick, rows_ref[part, LANE_TILES - 1, pl.ds(base, 128), :],
+                (((1,), (1,)), ((), ())),
+                precision=lax.Precision.HIGHEST, preferred_element_type=jnp.float32,
+            )
+            columns = jnp.where(lane < WINDOW + 1, columns, 0.0)
+            for side in range(2):
+                out1_ref[tile, pl.ds(OWN_ROW + 2 * side + part, 1), :] = columns[side : side + 1]
+        for lt in range(LANE_TILES):
+            out = out1_ref if lt < FIRST else out2_ref
+            top = lt * TILE_LANES if lt < FIRST else 0
+            below = HALO1 + lt * 10 if lt < FIRST else HALO2
             for part in range(2):
-                out_ref[tile, pl.ds(HALO1 + lt * 10 + 5 * part, 5), :] = rows_ref[
+                for phase in range(6):
+                    for half in range(2):
+                        at = top + part * 96 + phase * 16 + half * 8
+                        out[tile, pl.ds(at, 8), :] = rows_ref[
+                            part, lt, pl.ds(base + 6 * half + phase, 8, stride=12), :
+                        ]
+                out[tile, pl.ds(below + 5 * part, 5), :] = rows_ref[
                     part, lt, pl.ds(base + TILE_ROWS, 5), :
                 ]
 
 
-def pack_last_kernel(
-    valid_ref, l_before, l_tile, l_after, r_before, r_tile, r_after, out_ref, first_ref, last_ref,
-    rows_ref,
-):
-    refs = ((r_before, l_before), (r_tile, l_tile), (r_after, l_after))
-
-    def parts(which, part):
-        return [ref[part, 0] for ref in refs[which]]
-
-    kept = masked_rows(valid_ref, parts, pl.program_id(0), GROUP2 * TILE_ROWS, rows_ref)
-    lane = lax.broadcasted_iota(jnp.int32, (8, 128), 1)
-    for at, pick, out in ((1, 0, first_ref), (0, 127, last_ref)):
-        for part in range(2):
-            column = lax.dot_general(
-                jnp.where(lane == pick, 1.0, 0.0), kept[part][at], (((1,), (1,)), ((), ())),
-                precision=lax.Precision.HIGHEST, preferred_element_type=jnp.float32,
-            )
-            out[part : part + 1, :] = column[0:1, :]
-    for tile in range(GROUP2):
-        base = 5 + tile * TILE_ROWS
-        spread(out_ref, tile, base, 0, rows_ref, 0)
-        for part in range(2):
-            out_ref[tile, pl.ds(HALO2 + 5 * part, 5), :] = rows_ref[
-                part, 0, pl.ds(base + TILE_ROWS, 5), :
-            ]
-        out_ref[tile, pl.ds(EDGE_ROW, 6), :] = jnp.zeros((6, 128), jnp.float32)
-
-
-def row_specs(span, width, column):
+def pack(slc, valid):
+    span = GROUP * TILE_ROWS
     eight = span // 8
-    return [
-        pl.BlockSpec((2, 1, 8, width), lambda i: (0, 0, jnp.maximum(i * eight - 1, 0), column)),
-        pl.BlockSpec((2, 1, span, width), lambda i: (0, 0, i, column)),
-        pl.BlockSpec(
-            (2, 1, 8, width), lambda i: (0, 0, jnp.minimum(i * eight + eight, 191), column)
-        ),
-    ]
-
-
-def pack_first(slc, valid):
-    span = GROUP1 * TILE_ROWS
     return pl.pallas_call(
-        pack_first_kernel,
-        grid=(TILES // GROUP1,),
-        in_specs=[pl.BlockSpec(memory_space=pltpu.SMEM)] + row_specs(span, COLS, 0),
-        out_specs=pl.BlockSpec((GROUP1, ROWS1, 128), lambda i: (i, 0, 0)),
-        out_shape=jax.ShapeDtypeStruct((TILES, ROWS1, 128), jnp.float32),
-        scratch_shapes=[pltpu.VMEM((2, LANE_TILES, span + 16, 128), jnp.float32)],
-        compiler_params=pltpu.CompilerParams(vmem_limit_bytes=VMEM_LIMIT),
+        pack_kernel,
+        grid=(TILES // GROUP,),
+        in_specs=[
+            pl.BlockSpec(memory_space=pltpu.SMEM),
+            pl.BlockSpec((2, 1, 8, COLS), lambda i: (0, 0, jnp.maximum(i * eight - 1, 0), 0)),
+            pl.BlockSpec((2, 1, span, COLS), lambda i: (0, 0, i, 0)),
+            pl.BlockSpec((2, 1, 8, COLS), lambda i: (0, 0, jnp.minimum(i * eight + eight, 191), 0)),
+        ],
+        out_specs=[
+            pl.BlockSpec((GROUP, ROWS1, 128), lambda i: (i, 0, 0)),
+            pl.BlockSpec((GROUP, ROWS2, 128), lambda i: (i, 0, 0)),
+        ],
+        out_shape=[
+            jax.ShapeDtypeStruct((TILES, ROWS1, 128), jnp.float32),
+            jax.ShapeDtypeStruct((TILES, ROWS2, 128), jnp.float32),
+        ],
+        scratch_shapes=[pltpu.VMEM((2, LANE_TILES, span + 48, 128), jnp.float32)],
+        compiler_params=pltpu.CompilerParams(vmem_limit_bytes=20 * 1024 * 1024),
         cost_estimate=pl.CostEstimate(flops=10**6, bytes_accessed=2 * 10**7, transcendentals=0),
-        name="pack_first",
+        name="pack",
     )(valid, slc, slc, slc)
-
-
-def pack_last(slc, valid):
-    span = GROUP2 * TILE_ROWS
-    column = jax.ShapeDtypeStruct((2, 1536), jnp.float32)
-    return pl.pallas_call(
-        pack_last_kernel,
-        grid=(TILES // GROUP2,),
-        in_specs=[pl.BlockSpec(memory_space=pltpu.SMEM)]
-        + row_specs(span, 128, 0)
-        + row_specs(span, 128, LANE_TILES - 1),
-        out_specs=[
-            pl.BlockSpec((GROUP2, ROWS2, 128), lambda i: (i, 0, 0)),
-            pl.BlockSpec((2, span), lambda i: (0, i)),
-            pl.BlockSpec((2, span), lambda i: (0, i)),
-        ],
-        out_shape=[jax.ShapeDtypeStruct((TILES, ROWS2, 128), jnp.float32), column, column],
-        scratch_shapes=[pltpu.VMEM((2, 1, span + 16, 128), jnp.float32)],
-        compiler_params=pltpu.CompilerParams(vmem_limit_bytes=VMEM_LIMIT),
-        cost_estimate=pl.CostEstimate(flops=10**6, bytes_accessed=5 * 10**6, transcendentals=0),
-        name="pack_last",
-    )(valid, *([slc] * 6))
-
-
-def insert_kernel(left_ref, right_ref, in_ref, out_ref, wide_ref):
-    out_ref[...] = in_ref[...]
-    wide_ref[...] = jnp.zeros_like(wide_ref)
-    for side, ref in enumerate((left_ref, right_ref)):
-        wide_ref[2 * side : 2 * side + 2, 128 : 128 + 1536] = ref[...]
-    for tile in range(TILES):
-        start = 128 + tile * TILE_ROWS - 3
-        at = EDGE_ROW % 8
-        out_ref[tile, at : at + 4, :] = wide_ref[0:4, start : start + 128]
-
-
-def insert_edges(left, right, message):
-    spec = pl.BlockSpec((TILES, 8, 128), lambda i: (0, EDGE_ROW // 8, 0))
-    column = pl.BlockSpec((2, 1536), lambda i: (0, 0))
-    return pl.pallas_call(
-        insert_kernel,
-        grid=(1,),
-        in_specs=[column, column, spec],
-        out_specs=spec,
-        out_shape=jax.ShapeDtypeStruct(message.shape, message.dtype),
-        input_output_aliases={2: 0},
-        scratch_shapes=[pltpu.VMEM((8, 1920), jnp.float32)],
-        name="insert_edges",
-    )(left, right, message)
 
 
 def split(x):
@@ -441,7 +367,7 @@
 
 
 def last_kernel(
-    msg, table, pool, partial_hbm, done_hbm, out, sums, lhs, small, side_lhs, res, halo,
+    msg, left, right, table, pool, partial_hbm, done_hbm, out, sums, lhs, small, side_lhs, res, halo,
     pairs, edge, coh, vec, weight, rows, partial, done, sems,
 ):
     copies = [
@@ -452,8 +378,12 @@
         copy.start()
     fill_sums(msg, sums)
     for date in range(DATES):
-        for row in range(14):
+        for row in range(10):
             small[row, date : date + 1, :] = msg[date, HALO2 + row : HALO2 + row + 1, :]
+        for part in range(2):
+            own = OWN_ROW - OWN_TILE + part
+            small[10 + part, date : date + 1, :] = left[date, own + 2 : own + 3, :]
+            small[12 + part, date : date + 1, :] = right[date, own : own + 1, :]
     halo_products(small, side_lhs)
     high, low = split(side_lhs[...])
     halo[...] = dot(jnp.concatenate([high, low], axis=1), table[0])
@@ -628,18 +558,20 @@
         ]
         + SOLVE_SCRATCH
         + [pltpu.VMEM((2, DATES, 2, BLOCKS, 128), jnp.float32)],
-        compiler_params=pltpu.CompilerParams(vmem_limit_bytes=VMEM_LIMIT),
+        compiler_params=pltpu.CompilerParams(vmem_limit_bytes=40 * 1024 * 1024),
         cost_estimate=pl.CostEstimate(flops=10**9, bytes_accessed=10**7, transcendentals=0),
         name="link_first",
     )(message, message, tables)
 
 
-def link_last(message, tables, pool, partial, done):
+def link_last(message, left, right, tables, pool, partial, done):
     return pl.pallas_call(
         last_kernel,
         grid=(1,),
         in_specs=[
             whole(DATES, ROWS2, 128),
+            whole(DATES, 8, 128),
+            whole(DATES, 8, 128),
             pl.BlockSpec((1, 256, 128), lambda i: (FIRST, 0, 0)),
             whole(16, 128),
             pl.BlockSpec(memory_space=pl.ANY),
@@ -661,10 +593,10 @@
             pltpu.VMEM(LINKED, jnp.float32),
             pltpu.SemaphoreType.DMA((2,)),
         ],
-        compiler_params=pltpu.CompilerParams(vmem_limit_bytes=VMEM_LIMIT),
+        compiler_params=pltpu.CompilerParams(vmem_limit_bytes=24 * 1024 * 1024),
         cost_estimate=pl.CostEstimate(flops=10**8, bytes_accessed=10**7, transcendentals=0),
         name="link_last",
-    )(message, tables, pool, partial, done)
+    )(message, left, right, tables, pool, partial, done)
 
 
 def local(slc, valid_rows):
@@ -672,20 +604,17 @@
     up = [(i, i + 1) for i in range(size - 1)]
     down = [(i + 1, i) for i in range(size - 1)]
     valid = valid_rows.T
-    message2, first, last = pack_last(slc, valid)
-    left = lax.ppermute(last, "col", up)
-    right = lax.ppermute(first, "col", down)
-    slc, message2 = lax.optimization_barrier((slc, message2))
-    message1 = pack_first(slc, valid)
-    message2 = insert_edges(left, right, message2)
-    message1, message2 = lax.optimization_barrier((message1, message2))
+    message1, message2 = pack(slc, valid)
     received1 = lax.all_to_all(message1, "row", 0, 0, tiled=True)
     received1, message2 = lax.optimization_barrier((received1, message2))
     received2 = lax.all_to_all(message2, "row", 0, 0, tiled=True)
+    own = received1[:, OWN_TILE : OWN_TILE + 8]
+    left = lax.ppermute(own, "col", up)
+    right = lax.ppermute(own, "col", down)
     tables, pool = column_tables()
     tables = jnp.asarray(tables, jnp.bfloat16)
     partial, done = link_first(received1, tables)
-    return link_last(received2, tables, jnp.asarray(pool), partial, done)
+    return link_last(received2, left, right, tables, jnp.asarray(pool), partial, done)
 
 
 def solution(mesh):

time: 168 us -> 161 us (0.958)
  Pallas kernels: 45.9 us -> 32.8 us
  local copies, waits for them, and re-layouts: 2.4 us -> 13.4 us
  waiting for transfers between devices: 6.02 us -> 0.01 us
    unnamed x6 -> x24, local copies, waits for them, and re-layouts: 2.4 us -> 12.5 us
    pallas_call x3 -> x1, Pallas kernels: 15.7 us -> 6.12 us  [pack(): pl.pallas_call(pack_kernel, grid=(TILES // GROUP,), in_specs=[pl.BlockSpe...]
    all_to_all x1, waiting for transfers between devices: 6.01 us -> 0.01 us  [local(): received2 = lax.all_to_all(message2, 'row', 0, 0, tiled=True)]
    pallas_call x1, Pallas kernels: 22.7 us -> 20.6 us  [link_first(): pl.pallas_call(first_kernel, grid=(FIRST,), in_specs=[pl.BlockSpec((DATES...]
  transfers between devices with their start and end apart: 3 -> 3, of which waited for: 1 -> 0; matrix products, arithmetic and copies ran while one was open for 0% -> 1% of each run, Pallas kernels for 19% -> 13%
where the time goes in v4:
time: 161 us; the launch traced here: 160 us
  blocking collectives  104 us (65%)
  Pallas kernels  32.8 us (20%)
  local copies, waits for them, and re-layouts  13.4 us (8%)
  starting transfers between devices  10.6 us (7%)
    all_to_all x1, blocking collectives, local(): received1 = lax.all_to_all(message1, 'row', 0, 0, tiled=True)  104 us
    pallas_call x1, Pallas kernels, link_first(): pl.pallas_call(first_kernel, grid=(FIRST,), in_specs=[pl.BlockSpec((DATES...  20.6 us
    unnamed x24, local copies, waits for them, and re-layouts  12.5 us
    pallas_call x1, Pallas kernels, pack(): pl.pallas_call(pack_kernel, grid=(TILES // GROUP,), in_specs=[pl.BlockSpe...  6.12 us
    pallas_call x1, Pallas kernels, link_last(): pl.pallas_call(last_kernel, grid=(1,), in_specs=[whole(DATES, ROWS2, 128)...  6.09 us
    ppermute x1, starting transfers between devices, local(): right = lax.ppermute(own, 'col', down)  3.88 us
    all_to_all x1, starting transfers between devices, local(): received2 = lax.all_to_all(message2, 'row', 0, 0, tiled=True)  3.71 us
  transfers between devices with their start and end apart: 3, of which 0 were waited for; matrix products, arithmetic and copies ran while one was open for 1% of the time, Pallas kernels for 13%

profile of v4, /device:TPU:1, one launch (start us, length us, event | category | flops | bytes accessed | tf_op | source)
XLA Modules:
  0.0 160.4 jit_solution(2205036032461855282)
XLA Ops:
  0.0 0.0 copy-start
  0.0 3.7 %copy-done = f32[2,1,1536,768]{3,2,1,0:T(8,128)S(1)} copy-done((f32[2,1,1536,768]{3,2,1,0:T(8,128)S(1)}, f32[2,1,1536,768]{3,2,1,0:T(8,128)}, u32[]{:S(2)}) %copy-start) | copy-done | bytes 9437208
  3.7 0.0 copy-start.11
  3.7 0.7 copy-done.11
  4.4 6.1 %pack.1 = (f32[16,1024,128]{2,1,0:T(8,128)S(1)}, f32[16,208,128]{2,1,0:T(8,128)S(1)}) custom-call(s32[2,16]{1,0:T(2,128)S(1)} %bitcast.1, f32[2,1,1536,768]{3,2,1,0:T(8,128)S(1)} %copy-done, f32[2,1,1536,768]{3,2,1,0:T(8,128)S(1)} %copy-done, f32[2,1,1536,768]{3,2,1,0:T(8,128)S(1)} %copy-done), custom_call_target="tpu_custom_call" | custom-call | flops 1000000 | bytes 20000000 | tf_op jit(solution)/shard_map/pack/pallas_call | solution.py:134
  10.5 0.0 copy-start.3
  10.5 103.6 %all_to_all.10.msg.below_msg = f32[16,1024,128]{2,1,0:T(8,128)} all-to-all(f32[16,1024,128]{2,1,0:T(8,128)S(1)} %get-tuple-element.11), channel_id=1, replica_groups=mesh['row'=16,'col'=8] {'row'}, dimensions={0} | all-to-all | bytes 16777216 | tf_op jit(solution)/shard_map/all_to_all | solution.py:608
  114.0 0.0 copy-done.3
  114.0 3.7 %all-to-all-start.1 = ((f32[16,208,128]{2,1,0:T(8,128)}), f32[16,208,128]{2,1,0:T(8,128)S(1)}, u32[]{:S(2)}, u32[]{:S(2)}) async-start(f32[16,208,128]{2,1,0:T(8,128)} %copy-done.3), calls=%async_computation.1 | async-start | bytes 3407872 | tf_op jit(solution)/shard_map/all_to_all | solution.py:610
  117.8 0.0 copy-start.10
  117.8 0.9 slice.3
  118.6 3.9 %collective-permute-start.1 = (f32[16,8,128]{2,1,0:T(8,128)S(1)}, f32[16,8,128]{2,1,0:T(8,128)S(1)}, u32[]{:S(2)}, u32[]{:S(2)}) collective-permute-start(f32[16,8,128]{2,1,0:T(8,128)S(1)} %slice.3), channel_id=1, source_target_pairs={{1,0},{2,1},{3,2},{4,3},{5,4},{6,5},{7,6},{9,8},{10,9},{11,10},{12... | collective-permute-start | bytes 196616 | tf_op jit(solution)/shard_map/ppermute | solution.py:613
  122.5 3.0 %collective-permute-start = (f32[16,8,128]{2,1,0:T(8,128)S(1)}, f32[16,8,128]{2,1,0:T(8,128)S(1)}, u32[]{:S(2)}, u32[]{:S(2)}) collective-permute-start(f32[16,8,128]{2,1,0:T(8,128)S(1)} %slice.3), channel_id=1, source_target_pairs={{0,1},{1,2},{2,3},{3,4},{4,5},{5,6},{6,7},{8,9},{9,10},{10,11},{11... | collective-permute-start | bytes 196616 | tf_op jit(solution)/shard_map/ppermute | solution.py:612
  125.5 0.0 copy-done.2
  125.5 0.0 copy-start.1
  125.6 3.4 %copy-done.1 = f32[16,1024,128]{2,1,0:T(8,128)S(1)} copy-done((f32[16,1024,128]{2,1,0:T(8,128)S(1)}, f32[16,1024,128]{2,1,0:T(8,128)}, u32[]{:S(2)}) %copy-start.1) | copy-done | bytes 8388632
  128.9 20.6 %link_first.1 = (f32[2048,128]{1,0:T(8,128)S(1)}, f32[2,16,16,256]{3,2,1,0:T(8,128)S(1)}) custom-call(f32[16,1024,128]{2,1,0:T(8,128)S(1)} %copy-done.1, f32[16,1024,128]{2,1,0:T(8,128)S(1)} %copy-done.1, bf16[6,256,256]{2,1,0:T(8,128)(2,1)S(1)} %copy-done.2), custom_call_target="tpu_custom_call" | custom-call | flops 1000000000 | bytes 10000000 | tf_op jit(solution)/shard_map/link_first/pallas_call | solution.py:541
  149.5 0.0 copy-start.4
  149.5 0.8 copy-done.4
  150.3 0.0 collective-permute-done.1.right
  150.3 0.0 copy-start.6
  150.3 0.6 copy-done.6
  150.9 0.0 collective-permute-done.left
  150.9 0.0 copy-start.8
  150.9 0.6 copy-done.8
  151.6 0.0 all-to-all-done.1.msg
  151.6 0.0 copy-done.10
  151.6 0.0 copy-start.5
  151.6 1.0 copy-done.5
  152.6 0.8 copy-done.7
  153.5 0.8 copy-done.9
  154.3 6.1 %link_last.1 = f32[2,16,16,256]{3,2,1,0:T(8,128)} custom-call(f32[16,208,128]{2,1,0:T(8,128)S(1)} %all-to-all-done.1.msg, f32[16,8,128]{2,1,0:T(8,128)S(1)} %copy-done.9, f32[16,8,128]{2,1,0:T(8,128)S(1)} %copy-done.7, bf16[6,256,256]{2,1,0:T(8,128)(2,1)S(1)} %copy-done.2, f32[16,128]{1,0:T(8,128)S(1)} %copy-done.10, ...), custom_call_target="tpu_custom_call" | custom-call | flops 100000000 | bytes 10000000 | tf_op jit(solution)/shard_map/link_last/pallas_call | solution.py:568
  (3 shorter events, 0.0 us)
Async XLA Ops:
  0.0 3.7 %copy-start = (f32[2,1,1536,768]{3,2,1,0:T(8,128)S(1)}, f32[2,1,1536,768]{3,2,1,0:T(8,128)}, u32[]{:S(2)}) copy-start(f32[2,1,1536,768]{3,2,1,0:T(8,128)} %after_ref.1) | copy-start | bytes 28311556
  3.7 0.7 copy-start.11
  10.5 103.6 %copy-start.3 = (f32[16,208,128]{2,1,0:T(8,128)}, f32[16,208,128]{2,1,0:T(8,128)S(1)}, u32[]{:S(2)}) copy-start(f32[16,208,128]{2,1,0:T(8,128)S(1)} %get-tuple-element.13) | copy-start | bytes 5111812
  10.5 115.1 %copy-start.2 = (bf16[6,256,256]{2,1,0:T(8,128)(2,1)S(1)}, bf16[6,256,256]{2,1,0:T(8,128)(2,1)}, u32[]{:S(2)}) copy-start(bf16[6,256,256]{2,1,0:T(8,128)(2,1)} %constant.4.clone.table) | copy-start | bytes 2359300
  114.0 37.5 %all-to-all-start.1 = ((f32[16,208,128]{2,1,0:T(8,128)}), f32[16,208,128]{2,1,0:T(8,128)S(1)}, u32[]{:S(2)}, u32[]{:S(2)}) async-start(f32[16,208,128]{2,1,0:T(8,128)} %copy-done.3), calls=%async_computation.1 | async-start | bytes 3407872 | tf_op jit(solution)/shard_map/all_to_all | solution.py:610
  117.8 33.8 %copy-start.10 = (f32[16,128]{1,0:T(8,128)S(1)}, f32[16,128]{1,0:T(8,128)}, u32[]{:S(2)}) copy-start(f32[16,128]{1,0:T(8,128)} %constant.5.clone.pool) | copy-start | bytes 24580
  118.6 31.7 %collective-permute-start.1 = (f32[16,8,128]{2,1,0:T(8,128)S(1)}, f32[16,8,128]{2,1,0:T(8,128)S(1)}, u32[]{:S(2)}, u32[]{:S(2)}) collective-permute-start(f32[16,8,128]{2,1,0:T(8,128)S(1)} %slice.3), channel_id=1, source_target_pairs={{1,0},{2,1},{3,2},{4,3},{5,4},{6,5},{7,6},{9,8},{10,9},{11,10},{12... | collective-permute-start | bytes 196616 | tf_op jit(solution)/shard_map/ppermute | solution.py:613
  122.5 28.4 %collective-permute-start = (f32[16,8,128]{2,1,0:T(8,128)S(1)}, f32[16,8,128]{2,1,0:T(8,128)S(1)}, u32[]{:S(2)}, u32[]{:S(2)}) collective-permute-start(f32[16,8,128]{2,1,0:T(8,128)S(1)} %slice.3), channel_id=1, source_target_pairs={{0,1},{1,2},{2,3},{3,4},{4,5},{5,6},{6,7},{8,9},{9,10},{10,11},{11... | collective-permute-start | bytes 196616 | tf_op jit(solution)/shard_map/ppermute | solution.py:612
  125.5 3.4 %copy-start.1 = (f32[16,1024,128]{2,1,0:T(8,128)S(1)}, f32[16,1024,128]{2,1,0:T(8,128)}, u32[]{:S(2)}) copy-start(f32[16,1024,128]{2,1,0:T(8,128)} %all_to_all.10.msg.below_msg) | copy-start | bytes 25165828
  149.5 0.8 copy-start.4
  150.3 0.6 copy-start.6
  150.9 0.6 copy-start.8
  151.6 1.0 copy-start.5
  152.6 0.8 copy-start.7
  153.4 0.8 copy-start.9

commit v5 on v4

--- a/solution.py
+++ b/solution.py
@@ -26,7 +26,9 @@
 ROWS2 = 208
 HALO2 = TILE_LANES
 WINDOW = TILE_ROWS + 5
-GROUP = 4
+PIECES = 8
+PIECE_ROWS = 192
+GRANT = 60 * 1024 * 1024
 
 
 def pair_groups():
@@ -78,31 +80,44 @@
     return tables, pool.reshape(16, 128)
 
 
-def pack_kernel(valid_ref, before_ref, tile_ref, after_ref, out1_ref, out2_ref, rows_ref):
+def pack_kernel(valid_ref, slc, out1, out2, taken, rows_ref, stage1, stage2, in_sems, out_sems):
     me = lax.axis_index("row")
-    step = pl.program_id(0)
     low, high = valid_ref[0, me], valid_ref[1, me]
-    span = GROUP * TILE_ROWS
-    for ref, start, count in ((before_ref, -8, 8), (tile_ref, 0, span), (after_ref, span, 8)):
-        row = lax.broadcasted_iota(jnp.int32, (count, 128), 0) + (step * span + start)
-        keep = (row >= low) & (row < high)
+    lane = lax.broadcasted_iota(jnp.int32, (8, 128), 1)
+    row = lax.broadcasted_iota(jnp.int32, (8, 128), 0)
+    pick = jnp.where(((row == 0) & (lane == 64)) | ((row == 1) & (lane == 63)), 1.0, 0.0)
+    count = TILE_ROWS + 16
+
+    def piece(index):
+        return pltpu.make_async_copy(
+            slc.at[:, 0, pl.ds(index * PIECE_ROWS, PIECE_ROWS), :],
+            taken.at[:, pl.ds(index * PIECE_ROWS + 8, PIECE_ROWS), :],
+            in_sems.at[index],
+        )
+
+    def sends(tile):
+        return (
+            pltpu.make_async_copy(stage1.at[tile], out1.at[tile], out_sems.at[0, tile]),
+            pltpu.make_async_copy(stage2.at[tile], out2.at[tile], out_sems.at[1, tile]),
+        )
+
+    def one_tile(tile):
+        start = pl.multiple_of(tile * TILE_ROWS, 8)
+        at_row = lax.broadcasted_iota(jnp.int32, (count, 128), 0) + (start - 8)
+        keep = (at_row >= low) & (at_row < high)
         left = lax.broadcasted_iota(jnp.int32, (count, 128), 1) < 64
         for part in range(2):
             turned = []
             for lt in range(LANE_TILES):
-                value = ref[part, 0, :, lt * 128 : lt * 128 + 128]
+                value = taken[part, pl.ds(start, count), lt * 128 : lt * 128 + 128]
                 turned.append(pltpu.roll(jnp.where(keep, value, 0.0), 64, 1))
             for lt in range(LANE_TILES):
-                rows_ref[part, lt, pl.ds(start + 8, count), :] = jnp.where(
+                rows_ref[part, lt, 0:count, :] = jnp.where(
                     left, turned[lt], turned[(lt + 1) % LANE_TILES]
                 )
-    lane = lax.broadcasted_iota(jnp.int32, (8, 128), 1)
-    row = lax.broadcasted_iota(jnp.int32, (8, 128), 0)
-    pick = jnp.where(((row == 0) & (lane == 64)) | ((row == 1) & (lane == 63)), 1.0, 0.0)
-    for tile in range(GROUP):
-        base = 5 + tile * TILE_ROWS
-        out1_ref[tile, pl.ds(ROWS1 - 16, 16), :] = jnp.zeros((16, 128), jnp.float32)
-        out2_ref[tile, pl.ds(ROWS2 - 16, 16), :] = jnp.zeros((16, 128), jnp.float32)
+        base = 5
+        stage1[tile, pl.ds(ROWS1 - 16, 16), :] = jnp.zeros((16, 128), jnp.float32)
+        stage2[tile, pl.ds(ROWS2 - 16, 16), :] = jnp.zeros((16, 128), jnp.float32)
         for part in range(2):
             columns = lax.dot_general(
                 pick, rows_ref[part, LANE_TILES - 1, pl.ds(base, 128), :],
@@ -111,9 +126,9 @@
             )
             columns = jnp.where(lane < WINDOW + 1, columns, 0.0)
             for side in range(2):
-                out1_ref[tile, pl.ds(OWN_ROW + 2 * side + part, 1), :] = columns[side : side + 1]
+                stage1[tile, pl.ds(OWN_ROW + 2 * side + part, 1), :] = columns[side : side + 1]
         for lt in range(LANE_TILES):
-            out = out1_ref if lt < FIRST else out2_ref
+            out = stage1 if lt < FIRST else stage2
             top = lt * TILE_LANES if lt < FIRST else 0
             below = HALO1 + lt * 10 if lt < FIRST else HALO2
             for part in range(2):
@@ -126,33 +141,58 @@
                 out[tile, pl.ds(below + 5 * part, 5), :] = rows_ref[
                     part, lt, pl.ds(base + TILE_ROWS, 5), :
                 ]
+        for send in sends(tile):
+            send.start()
+
+    for index in range(PIECES):
+        piece(index).start()
+    rows_ref[:, :, pl.ds(count, 24), :] = jnp.zeros((2, LANE_TILES, 24, 128), jnp.float32)
+    piece(0).wait()
+
+    def step(index, carry):
+        one_tile(2 * index)
+
+        @pl.when(index < PIECES - 1)
+        def _():
+            piece(index + 1).wait()
+
+        one_tile(2 * index + 1)
+        return carry
+
+    lax.fori_loop(0, PIECES, step, 0)
+
+    def finish(tile, carry):
+        for send in sends(tile):
+            send.wait()
+        return carry
+
+    lax.fori_loop(0, TILES, finish, 0)
 
 
 def pack(slc, valid):
-    span = GROUP * TILE_ROWS
-    eight = span // 8
     return pl.pallas_call(
         pack_kernel,
-        grid=(TILES // GROUP,),
         in_specs=[
             pl.BlockSpec(memory_space=pltpu.SMEM),
-            pl.BlockSpec((2, 1, 8, COLS), lambda i: (0, 0, jnp.maximum(i * eight - 1, 0), 0)),
-            pl.BlockSpec((2, 1, span, COLS), lambda i: (0, 0, i, 0)),
-            pl.BlockSpec((2, 1, 8, COLS), lambda i: (0, 0, jnp.minimum(i * eight + eight, 191), 0)),
+            pl.BlockSpec(memory_space=pl.ANY),
         ],
-        out_specs=[
-            pl.BlockSpec((GROUP, ROWS1, 128), lambda i: (i, 0, 0)),
-            pl.BlockSpec((GROUP, ROWS2, 128), lambda i: (i, 0, 0)),
-        ],
+        out_specs=[pl.BlockSpec(memory_space=pl.ANY)] * 2,
         out_shape=[
             jax.ShapeDtypeStruct((TILES, ROWS1, 128), jnp.float32),
             jax.ShapeDtypeStruct((TILES, ROWS2, 128), jnp.float32),
         ],
-        scratch_shapes=[pltpu.VMEM((2, LANE_TILES, span + 48, 128), jnp.float32)],
-        compiler_params=pltpu.CompilerParams(vmem_limit_bytes=20 * 1024 * 1024),
+        scratch_shapes=[
+            pltpu.VMEM((2, 1536 + 16, COLS), jnp.float32),
+            pltpu.VMEM((2, LANE_TILES, TILE_ROWS + 40, 128), jnp.float32),
+            pltpu.VMEM((TILES, ROWS1, 128), jnp.float32),
+            pltpu.VMEM((TILES, ROWS2, 128), jnp.float32),
+            pltpu.SemaphoreType.DMA((PIECES,)),
+            pltpu.SemaphoreType.DMA((2, TILES)),
+        ],
+        compiler_params=pltpu.CompilerParams(vmem_limit_bytes=GRANT),
         cost_estimate=pl.CostEstimate(flops=10**6, bytes_accessed=2 * 10**7, transcendentals=0),
         name="pack",
-    )(valid, slc, slc, slc)
+    )(valid, slc)
 
 
 def split(x):
@@ -288,7 +328,7 @@
 
 def pool_side(side_lhs, table):
     high, low = split(side_lhs[...])
-    return dot(jnp.concatenate([high, low], axis=1), table[0])
+    return dot(jnp.concatenate([high, low], axis=1), table)
 
 
 def chunk_rows(chunk):
@@ -297,18 +337,19 @@
 
 def first_kernel(
     msg, below_msg, table, part_out, out, sums, lhs, small, side_lhs, res, halo, coh, vec, weight,
-    rows,
+    rows, weights,
 ):
     step = pl.program_id(0)
+    weights[...] = table[0].astype(jnp.bfloat16)
     fill_sums(msg, sums)
     for date in range(DATES):
         for row in range(10):
             small[row, date : date + 1, :] = below_msg[date, pl.ds(step * 10 + row, 1), :]
     halo_products(small, side_lhs)
-    halo[step] = pool_side(side_lhs, table)
+    halo[step] = pool_side(side_lhs, weights[...])
 
     def pooled(chunk):
-        res[step, chunk_rows(chunk), :] = dot(lhs[chunk_rows(chunk), :], table[0])
+        res[step, chunk_rows(chunk), :] = dot(lhs[chunk_rows(chunk), :], weights[...])
 
     main_products(msg, sums, lhs, pooled)
 
@@ -368,7 +409,7 @@
 
 def last_kernel(
     msg, left, right, table, pool, partial_hbm, done_hbm, out, sums, lhs, small, side_lhs, res, halo,
-    pairs, edge, coh, vec, weight, rows, partial, done, sems,
+    pairs, edge, coh, vec, weight, rows, weights, partial, done, sems,
 ):
     copies = [
         pltpu.make_async_copy(partial_hbm, partial, sems.at[0]),
@@ -385,8 +426,8 @@
             small[10 + part, date : date + 1, :] = left[date, own + 2 : own + 3, :]
             small[12 + part, date : date + 1, :] = right[date, own : own + 1, :]
     halo_products(small, side_lhs)
-    high, low = split(side_lhs[...])
-    halo[...] = dot(jnp.concatenate([high, low], axis=1), table[0])
+    weights[...] = table[0].astype(jnp.bfloat16)
+    halo[...] = pool_side(side_lhs, weights[...])
     for side in range(2):
         row = 10 + 2 * side
 
@@ -409,7 +450,7 @@
         edge[2 * group + 1] = jnp.where(lower, pltpu.roll(even_rows, 64, 1), odd_rows)
 
     def pooled(chunk):
-        res[chunk_rows(chunk), :] = dot(lhs[chunk_rows(chunk), :], table[0])
+        res[chunk_rows(chunk), :] = dot(lhs[chunk_rows(chunk), :], weights[...])
 
     main_products(msg, sums, lhs, pooled)
 
@@ -535,6 +576,22 @@
 ]
 LINKED = (2, DATES, BLOCKS, OUT_COLS)
 PARTIAL = (FIELDS * 8, 128)
+
+
+def cut_kernel(in_ref, out_ref):
+    out_ref[...] = in_ref[...]
+
+
+def cut_columns(message):
+    return pl.pallas_call(
+        cut_kernel,
+        grid=(1,),
+        in_specs=[pl.BlockSpec((DATES, 8, 128), lambda i: (0, OWN_TILE // 8, 0))],
+        out_specs=whole(DATES, 8, 128),
+        out_shape=jax.ShapeDtypeStruct((DATES, 8, 128), jnp.float32),
+        compiler_params=pltpu.CompilerParams(vmem_limit_bytes=GRANT),
+        name="cut_columns",
+    )(message)
 
 
 def link_first(message, tables):
@@ -557,8 +614,8 @@
             pltpu.VMEM((FIRST, SIDE, 256), jnp.float32),
         ]
         + SOLVE_SCRATCH
-        + [pltpu.VMEM((2, DATES, 2, BLOCKS, 128), jnp.float32)],
-        compiler_params=pltpu.CompilerParams(vmem_limit_bytes=40 * 1024 * 1024),
+        + [pltpu.VMEM((2, DATES, 2, BLOCKS, 128), jnp.float32), pltpu.VMEM((256, 256), jnp.bfloat16)],
+        compiler_params=pltpu.CompilerParams(vmem_limit_bytes=GRANT),
         cost_estimate=pl.CostEstimate(flops=10**9, bytes_accessed=10**7, transcendentals=0),
         name="link_first",
     )(message, message, tables)
@@ -589,11 +646,12 @@
         + SOLVE_SCRATCH
         + [
             pltpu.VMEM((2, DATES, 1, BLOCKS, 128), jnp.float32),
+            pltpu.VMEM((256, 128), jnp.bfloat16),
             pltpu.VMEM(PARTIAL, jnp.float32),
             pltpu.VMEM(LINKED, jnp.float32),
             pltpu.SemaphoreType.DMA((2,)),
         ],
-        compiler_params=pltpu.CompilerParams(vmem_limit_bytes=24 * 1024 * 1024),
+        compiler_params=pltpu.CompilerParams(vmem_limit_bytes=GRANT),
         cost_estimate=pl.CostEstimate(flops=10**8, bytes_accessed=10**7, transcendentals=0),
         name="link_last",
     )(message, left, right, tables, pool, partial, done)
@@ -608,11 +666,11 @@
     received1 = lax.all_to_all(message1, "row", 0, 0, tiled=True)
     received1, message2 = lax.optimization_barrier((received1, message2))
     received2 = lax.all_to_all(message2, "row", 0, 0, tiled=True)
-    own = received1[:, OWN_TILE : OWN_TILE + 8]
+    own = cut_columns(received1)
     left = lax.ppermute(own, "col", up)
     right = lax.ppermute(own, "col", down)
     tables, pool = column_tables()
-    tables = jnp.asarray(tables, jnp.bfloat16)
+    tables = jnp.asarray(tables)
     partial, done = link_first(received1, tables)
     return link_last(received2, left, right, tables, jnp.asarray(pool), partial, done)
 

time: 161 us -> 158 us (0.981)
  local copies, waits for them, and re-layouts: 13.4 us -> 1.22 us
  Pallas kernels: 32.8 us -> 42.7 us
    unnamed x24 -> x6, local copies, waits for them, and re-layouts: 12.5 us -> 1.22 us
    pallas_call x1 -> x2, Pallas kernels: 6.12 us -> 12.2 us  [the longest x1 10.7 us: pack(): pl.pallas_call(pack_kernel, in_specs=[pl.BlockSpec(memory_space=pltpu.SME...]
    pallas_call x1, Pallas kernels: 20.6 us -> 22.9 us  [link_first(): pl.pallas_call(first_kernel, grid=(FIRST,), in_specs=[pl.BlockSpec((DATES...]
  transfers between devices with their start and end apart: 3 -> 3, of which waited for: 0 -> 0; matrix products, arithmetic and copies ran while one was open for 1% -> 0% of each run, Pallas kernels for 13% -> 15%
where the time goes in v5:
time: 158 us
  blocking collectives  103 us (65%)
  Pallas kernels  42.7 us (27%)
  starting transfers between devices  10.6 us (7%)
    all_to_all x1, blocking collectives, local(): received1 = lax.all_to_all(message1, 'row', 0, 0, tiled=True)  103 us
    pallas_call x1, Pallas kernels, link_first(): pl.pallas_call(first_kernel, grid=(FIRST,), in_specs=[pl.BlockSpec((DATES...  22.9 us
    pallas_call x1, Pallas kernels, pack(): pl.pallas_call(pack_kernel, in_specs=[pl.BlockSpec(memory_space=pltpu.SME...  10.7 us
    pallas_call x1, Pallas kernels, link_last(): pl.pallas_call(last_kernel, grid=(1,), in_specs=[whole(DATES, ROWS2, 128)...  7.55 us
    ppermute x1, starting transfers between devices, local(): right = lax.ppermute(own, 'col', down)  3.87 us
    all_to_all x1, starting transfers between devices, local(): received2 = lax.all_to_all(message2, 'row', 0, 0, tiled=True)  3.71 us
  transfers between devices with their start and end apart: 3, of which 0 were waited for; matrix products, arithmetic and copies ran while one was open for 0% of the time, Pallas kernels for 15%

profile of v5, /device:TPU:1, one launch (start us, length us, event | category | flops | bytes accessed | tf_op | source)
XLA Modules:
  0.0 158.0 jit_solution(6147062584373421500)
XLA Ops:
  0.0 10.7 %pack.1 = (f32[16,1024,128]{2,1,0:T(8,128)}, f32[16,208,128]{2,1,0:T(8,128)}) custom-call(s32[2,16]{1,0:T(2,128)} %bitcast.1, f32[2,1,1536,768]{3,2,1,0:T(8,128)} %slc.1), custom_call_target="tpu_custom_call" | custom-call | flops 1000000 | bytes 20000000 | tf_op jit(solution)/shard_map/pack/pallas_call | solution.py:173
  10.7 103.5 %all_to_all.10.in_ref.msg.below_msg = f32[16,1024,128]{2,1,0:T(8,128)} all-to-all(f32[16,1024,128]{2,1,0:T(8,128)} %get-tuple-element.11), channel_id=1, replica_groups=mesh['row'=16,'col'=8] {'row'}, dimensions={0} | all-to-all | bytes 16777216 | tf_op jit(solution)/shard_map/all_to_all | solution.py:666
  114.2 3.7 %all-to-all-start.1 = ((f32[16,208,128]{2,1,0:T(8,128)}), f32[16,208,128]{2,1,0:T(8,128)S(1)}, u32[]{:S(2)}, u32[]{:S(2)}) async-start(f32[16,208,128]{2,1,0:T(8,128)} %get-tuple-element.13), calls=%async_computation.1 | async-start | bytes 3407872 | tf_op jit(solution)/shard_map/all_to_all | solution.py:668
  118.0 1.5 cut_columns.1
  119.4 3.9 %collective-permute-start.1 = (f32[16,8,128]{2,1,0:T(8,128)}, f32[16,8,128]{2,1,0:T(8,128)S(1)}, u32[]{:S(2)}, u32[]{:S(2)}) collective-permute-start(f32[16,8,128]{2,1,0:T(8,128)} %cut_columns.1), channel_id=1, source_target_pairs={{1,0},{2,1},{3,2},{4,3},{5,4},{6,5},{7,6},{9,8},{10,9},{11,10},{12... | collective-permute-start | bytes 196616 | tf_op jit(solution)/shard_map/ppermute | solution.py:671
  123.3 3.0 %collective-permute-start = (f32[16,8,128]{2,1,0:T(8,128)}, f32[16,8,128]{2,1,0:T(8,128)S(1)}, u32[]{:S(2)}, u32[]{:S(2)}) collective-permute-start(f32[16,8,128]{2,1,0:T(8,128)} %cut_columns.1), channel_id=1, source_target_pairs={{0,1},{1,2},{2,3},{3,4},{4,5},{5,6},{6,7},{8,9},{9,10},{10,11},{11... | collective-permute-start | bytes 196616 | tf_op jit(solution)/shard_map/ppermute | solution.py:670
  126.3 22.9 %link_first.1 = (f32[2048,128]{1,0:T(8,128)}, f32[2,16,16,256]{3,2,1,0:T(8,128)}) custom-call(f32[16,1024,128]{2,1,0:T(8,128)} %all_to_all.10.in_ref.msg.below_msg, f32[16,1024,128]{2,1,0:T(8,128)} %all_to_all.10.in_ref.msg.below_msg, f32[6,256,256]{2,1,0:T(8,128)} %constant.4.clone.table), custom_call_target="tpu_custom_call" | custom-call | flops 1000000000 | bytes 10000000 | tf_op jit(solution)/shard_map/link_first/pallas_call | solution.py:598
  149.2 0.0 collective-permute-done.1.right
  149.2 0.0 copy-start.1
  149.2 0.0 collective-permute-done.left
  149.2 0.0 copy-start.2
  149.3 0.0 all-to-all-done.1.msg
  149.3 0.0 copy-start
  149.3 0.6 copy-done.1
  149.9 0.0 copy-done.2
  149.9 0.6 copy-done
  150.5 7.5 %link_last.1 = f32[2,16,16,256]{3,2,1,0:T(8,128)} custom-call(f32[16,208,128]{2,1,0:T(8,128)} %copy-done, f32[16,8,128]{2,1,0:T(8,128)} %copy-done.2, f32[16,8,128]{2,1,0:T(8,128)} %copy-done.1, f32[6,256,256]{2,1,0:T(8,128)} %constant.4.clone.table, f32[16,128]{1,0:T(8,128)} %constant.5.clone.pool, f32[2048,128]{1,0:T(8,128)} %get-tuple-element.15.partial_hbm, ...), custom_call_target="tpu_custom_call" | custom-call | flops 100000000 | bytes 10000000 | tf_op jit(solution)/shard_map/link_last/pallas_call | solution.py:625
Async XLA Ops:
  114.2 35.0 %all-to-all-start.1 = ((f32[16,208,128]{2,1,0:T(8,128)}), f32[16,208,128]{2,1,0:T(8,128)S(1)}, u32[]{:S(2)}, u32[]{:S(2)}) async-start(f32[16,208,128]{2,1,0:T(8,128)} %get-tuple-element.13), calls=%async_computation.1 | async-start | bytes 3407872 | tf_op jit(solution)/shard_map/all_to_all | solution.py:668
  119.4 29.8 %collective-permute-start.1 = (f32[16,8,128]{2,1,0:T(8,128)}, f32[16,8,128]{2,1,0:T(8,128)S(1)}, u32[]{:S(2)}, u32[]{:S(2)}) collective-permute-start(f32[16,8,128]{2,1,0:T(8,128)} %cut_columns.1), channel_id=1, source_target_pairs={{1,0},{2,1},{3,2},{4,3},{5,4},{6,5},{7,6},{9,8},{10,9},{11,10},{12... | collective-permute-start | bytes 196616 | tf_op jit(solution)/shard_map/ppermute | solution.py:671
  123.3 25.9 %collective-permute-start = (f32[16,8,128]{2,1,0:T(8,128)}, f32[16,8,128]{2,1,0:T(8,128)S(1)}, u32[]{:S(2)}, u32[]{:S(2)}) collective-permute-start(f32[16,8,128]{2,1,0:T(8,128)} %cut_columns.1), channel_id=1, source_target_pairs={{0,1},{1,2},{2,3},{3,4},{4,5},{5,6},{6,7},{8,9},{9,10},{10,11},{11... | collective-permute-start | bytes 196616 | tf_op jit(solution)/shard_map/ppermute | solution.py:670
  149.2 0.6 copy-start.1
  149.2 0.6 copy-start.2
  149.3 1.2 copy-start

commit v6 on v5

--- a/solution.py
+++ b/solution.py
@@ -101,7 +101,7 @@
             pltpu.make_async_copy(stage2.at[tile], out2.at[tile], out_sems.at[1, tile]),
         )
 
-    def one_tile(tile):
+    def mask_rows(tile, slot):
         start = pl.multiple_of(tile * TILE_ROWS, 8)
         at_row = lax.broadcasted_iota(jnp.int32, (count, 128), 0) + (start - 8)
         keep = (at_row >= low) & (at_row < high)
@@ -112,21 +112,36 @@
                 value = taken[part, pl.ds(start, count), lt * 128 : lt * 128 + 128]
                 turned.append(pltpu.roll(jnp.where(keep, value, 0.0), 64, 1))
             for lt in range(LANE_TILES):
-                rows_ref[part, lt, 0:count, :] = jnp.where(
+                rows_ref[slot, part, lt, 0:count, :] = jnp.where(
                     left, turned[lt], turned[(lt + 1) % LANE_TILES]
                 )
+
+    def own_columns(tiles):
+        blocks = [
+            rows_ref[slot, part, LANE_TILES - 1, pl.ds(5, 128), :]
+            for slot in range(2)
+            for part in range(2)
+        ]
+        rest = jnp.concatenate(blocks, axis=0)
+        columns = None
+        for _ in range(3):
+            piece_of = rest.astype(jnp.bfloat16)
+            rest = rest - piece_of.astype(jnp.float32)
+            term = lax.dot_general(
+                pick.astype(jnp.bfloat16), piece_of, (((1,), (1,)), ((), ())),
+                preferred_element_type=jnp.float32,
+            )
+            columns = term if columns is None else columns + term
+        for slot, tile in enumerate(tiles):
+            for part in range(2):
+                at = (2 * slot + part) * 128
+                value = jnp.where(lane < WINDOW + 1, columns[:, at : at + 128], 0.0)
+                for side in range(2):
+                    row_at = pl.ds(OWN_ROW + 2 * side + part, 1)
+                    stage1[tile, row_at, :] = value[side : side + 1]
+
+    def spread(tile, slot):
         base = 5
-        stage1[tile, pl.ds(ROWS1 - 16, 16), :] = jnp.zeros((16, 128), jnp.float32)
-        stage2[tile, pl.ds(ROWS2 - 16, 16), :] = jnp.zeros((16, 128), jnp.float32)
-        for part in range(2):
-            columns = lax.dot_general(
-                pick, rows_ref[part, LANE_TILES - 1, pl.ds(base, 128), :],
-                (((1,), (1,)), ((), ())),
-                precision=lax.Precision.HIGHEST, preferred_element_type=jnp.float32,
-            )
-            columns = jnp.where(lane < WINDOW + 1, columns, 0.0)
-            for side in range(2):
-                stage1[tile, pl.ds(OWN_ROW + 2 * side + part, 1), :] = columns[side : side + 1]
         for lt in range(LANE_TILES):
             out = stage1 if lt < FIRST else stage2
             top = lt * TILE_LANES if lt < FIRST else 0
@@ -136,30 +151,38 @@
                     for half in range(2):
                         at = top + part * 96 + phase * 16 + half * 8
                         out[tile, pl.ds(at, 8), :] = rows_ref[
-                            part, lt, pl.ds(base + 6 * half + phase, 8, stride=12), :
+                            slot, part, lt, pl.ds(base + 6 * half + phase, 8, stride=12), :
                         ]
                 out[tile, pl.ds(below + 5 * part, 5), :] = rows_ref[
-                    part, lt, pl.ds(base + TILE_ROWS, 5), :
+                    slot, part, lt, pl.ds(base + TILE_ROWS, 5), :
                 ]
-        for send in sends(tile):
-            send.start()
+
+    def two_tiles(index):
+        tiles = (2 * index, 2 * index + 1)
+        for slot, tile in enumerate(tiles):
+            mask_rows(tile, slot)
+        for tile in tiles:
+            stage1[tile, pl.ds(ROWS1 - 16, 16), :] = jnp.zeros((16, 128), jnp.float32)
+            stage2[tile, pl.ds(ROWS2 - 16, 16), :] = jnp.zeros((16, 128), jnp.float32)
+        own_columns(tiles)
+        for slot, tile in enumerate(tiles):
+            spread(tile, slot)
+        for tile in tiles:
+            for send in sends(tile):
+                send.start()
 
     for index in range(PIECES):
         piece(index).start()
-    rows_ref[:, :, pl.ds(count, 24), :] = jnp.zeros((2, LANE_TILES, 24, 128), jnp.float32)
+    rows_ref[:, :, :, pl.ds(count, 24), :] = jnp.zeros((2, 2, LANE_TILES, 24, 128), jnp.float32)
     piece(0).wait()
 
     def step(index, carry):
-        one_tile(2 * index)
-
-        @pl.when(index < PIECES - 1)
-        def _():
-            piece(index + 1).wait()
-
-        one_tile(2 * index + 1)
+        piece(index + 1).wait()
+        two_tiles(index)
         return carry
 
-    lax.fori_loop(0, PIECES, step, 0)
+    lax.fori_loop(0, PIECES - 1, step, 0)
+    two_tiles(PIECES - 1)
 
     def finish(tile, carry):
         for send in sends(tile):
@@ -183,7 +206,7 @@
         ],
         scratch_shapes=[
             pltpu.VMEM((2, 1536 + 16, COLS), jnp.float32),
-            pltpu.VMEM((2, LANE_TILES, TILE_ROWS + 40, 128), jnp.float32),
+            pltpu.VMEM((2, 2, LANE_TILES, TILE_ROWS + 40, 128), jnp.float32),
             pltpu.VMEM((TILES, ROWS1, 128), jnp.float32),
             pltpu.VMEM((TILES, ROWS2, 128), jnp.float32),
             pltpu.SemaphoreType.DMA((PIECES,)),
@@ -408,7 +431,7 @@
 
 
 def last_kernel(
-    msg, left, right, table, pool, partial_hbm, done_hbm, out, sums, lhs, small, side_lhs, res, halo,
+    msg, beside_msg, table, pool, partial_hbm, done_hbm, out, sums, lhs, small, side_lhs, res, halo,
     pairs, edge, coh, vec, weight, rows, weights, partial, done, sems,
 ):
     copies = [
@@ -417,14 +440,18 @@
     ]
     for copy in copies:
         copy.start()
+    col = lax.axis_index("col")
+    cols = beside_msg.shape[0]
     fill_sums(msg, sums)
     for date in range(DATES):
         for row in range(10):
             small[row, date : date + 1, :] = msg[date, HALO2 + row : HALO2 + row + 1, :]
         for part in range(2):
             own = OWN_ROW - OWN_TILE + part
-            small[10 + part, date : date + 1, :] = left[date, own + 2 : own + 3, :]
-            small[12 + part, date : date + 1, :] = right[date, own : own + 1, :]
+            before = beside_msg[jnp.maximum(col - 1, 0), date, own + 2 : own + 3, :]
+            after = beside_msg[jnp.minimum(col + 1, cols - 1), date, own : own + 1, :]
+            small[10 + part, date : date + 1, :] = jnp.where(col > 0, before, 0.0)
+            small[12 + part, date : date + 1, :] = jnp.where(col < cols - 1, after, 0.0)
     halo_products(small, side_lhs)
     weights[...] = table[0].astype(jnp.bfloat16)
     halo[...] = pool_side(side_lhs, weights[...])
@@ -495,6 +522,8 @@
         root = lax.rsqrt(jnp.maximum(diag, FLOOR))
         inv.append(root)
         weight[t] = diag * (root * root) + 1.0
+    row_real = [weight[t] for t in range(DATES)]
+    row_imag = [None] * DATES
     for i, (t, u) in enumerate(PAIRS):
         factor = inv[t] * inv[u]
         real = cov(t, u, 0) * factor
@@ -502,10 +531,15 @@
         coh[i, 0] = real
         coh[i, 1] = real + imag
         coh[i, 2] = imag - real
+        row_real[t] = row_real[t] + real
+        row_real[u] = row_real[u] + real
+        row_imag[t] = imag if row_imag[t] is None else row_imag[t] + imag
+        row_imag[u] = -imag if row_imag[u] is None else row_imag[u] - imag
     for t in range(DATES):
-        vec[0, t] = jnp.full((8, 128), 0.25, jnp.float32)
-        vec[1, t] = jnp.zeros((8, 128), jnp.float32)
-        vec[2, t] = jnp.full((8, 128), 0.25, jnp.float32)
+        real, imag = 0.25 * row_real[t], 0.25 * row_imag[t]
+        vec[0, t] = real
+        vec[1, t] = imag
+        vec[2, t] = real + imag
 
     def iterate(_, carry):
         scale = inverse_norm(vec)
@@ -549,7 +583,7 @@
             vec[2, t] = real + imag
         return carry
 
-    lax.fori_loop(0, ITERS, iterate, 0)
+    lax.fori_loop(0, ITERS - 1, iterate, 0)
     scale = inverse_norm(vec)
     for t in range(DATES):
         for part in range(2):
@@ -621,14 +655,13 @@
     )(message, message, tables)
 
 
-def link_last(message, left, right, tables, pool, partial, done):
+def link_last(message, beside, tables, pool, partial, done):
     return pl.pallas_call(
         last_kernel,
         grid=(1,),
         in_specs=[
             whole(DATES, ROWS2, 128),
-            whole(DATES, 8, 128),
-            whole(DATES, 8, 128),
+            whole(*beside.shape),
             pl.BlockSpec((1, 256, 128), lambda i: (FIRST, 0, 0)),
             whole(16, 128),
             pl.BlockSpec(memory_space=pl.ANY),
@@ -654,25 +687,21 @@
         compiler_params=pltpu.CompilerParams(vmem_limit_bytes=GRANT),
         cost_estimate=pl.CostEstimate(flops=10**8, bytes_accessed=10**7, transcendentals=0),
         name="link_last",
-    )(message, left, right, tables, pool, partial, done)
+    )(message, beside, tables, pool, partial, done)
 
 
 def local(slc, valid_rows):
-    size = lax.axis_size("col")
-    up = [(i, i + 1) for i in range(size - 1)]
-    down = [(i + 1, i) for i in range(size - 1)]
     valid = valid_rows.T
     message1, message2 = pack(slc, valid)
     received1 = lax.all_to_all(message1, "row", 0, 0, tiled=True)
     received1, message2 = lax.optimization_barrier((received1, message2))
     received2 = lax.all_to_all(message2, "row", 0, 0, tiled=True)
     own = cut_columns(received1)
-    left = lax.ppermute(own, "col", up)
-    right = lax.ppermute(own, "col", down)
+    beside = lax.all_gather(own, "col")
     tables, pool = column_tables()
     tables = jnp.asarray(tables)
     partial, done = link_first(received1, tables)
-    return link_last(received2, left, right, tables, jnp.asarray(pool), partial, done)
+    return link_last(received2, beside, tables, jnp.asarray(pool), partial, done)
 
 
 def solution(mesh):

time: 158 us -> 165 us (1.044)
  blocking collectives: 103 us -> 120 us
  starting transfers between devices: 10.6 us -> 3.71 us
  Pallas kernels: 42.7 us -> 39.6 us
    all_gather x0 -> x1, blocking collectives: none -> 16.3 us  [local(): beside = lax.all_gather(own, 'col')]
    ppermute x2 -> x0, starting transfers between devices: 6.89 us -> none  [the longest x1 3.87 us: local(): right = lax.ppermute(own, 'col', down)]
    pallas_call x1, Pallas kernels: 10.7 us -> 8.39 us  [pack(): pl.pallas_call(pack_kernel, in_specs=[pl.BlockSpec(memory_space=pltpu.SME...]
  transfers between devices with their start and end apart: 3 -> 1, of which waited for: 0 -> 0; matrix products, arithmetic and copies ran while one was open for 0% -> 0% of each run, Pallas kernels for 15% -> 14%
where the time goes in v6:
time: 165 us; the launch traced here: 164 us
  blocking collectives  120 us (73%)
  Pallas kernels  39.6 us (24%)
  starting transfers between devices  3.71 us (2%)
    all_to_all x1, blocking collectives, local(): received1 = lax.all_to_all(message1, 'row', 0, 0, tiled=True)  103 us
    pallas_call x1, Pallas kernels, link_first(): pl.pallas_call(first_kernel, grid=(FIRST,), in_specs=[pl.BlockSpec((DATES...  22.3 us
    all_gather x1, blocking collectives, local(): beside = lax.all_gather(own, 'col')  16.3 us
    pallas_call x1, Pallas kernels, pack(): pl.pallas_call(pack_kernel, in_specs=[pl.BlockSpec(memory_space=pltpu.SME...  8.39 us
    pallas_call x1, Pallas kernels, link_last(): pl.pallas_call(last_kernel, grid=(1,), in_specs=[whole(DATES, ROWS2, 128)...  7.43 us
    all_to_all x1, starting transfers between devices, local(): received2 = lax.all_to_all(message2, 'row', 0, 0, tiled=True)  3.71 us
  transfers between devices with their start and end apart: 1, of which 0 were waited for; matrix products, arithmetic and copies ran while one was open for 0% of the time, Pallas kernels for 14%

profile of v6, /device:TPU:1, one launch (start us, length us, event | category | flops | bytes accessed | tf_op | source)
XLA Modules:
  0.0 164.4 jit_solution(10144900925221214053)
XLA Ops:
  0.0 8.4 %pack.1 = (f32[16,1024,128]{2,1,0:T(8,128)}, f32[16,208,128]{2,1,0:T(8,128)}) custom-call(s32[2,16]{1,0:T(2,128)} %bitcast.3, f32[2,1,1536,768]{3,2,1,0:T(8,128)} %slc.1), custom_call_target="tpu_custom_call" | custom-call | flops 1000000 | bytes 20000000 | tf_op jit(solution)/shard_map/pack/pallas_call | solution.py:196
  8.4 103.5 %all_to_all.10.in_ref.msg.below_msg = f32[16,1024,128]{2,1,0:T(8,128)} all-to-all(f32[16,1024,128]{2,1,0:T(8,128)} %get-tuple-element.11), channel_id=1, replica_groups=mesh['row'=16,'col'=8] {'row'}, dimensions={0} | all-to-all | bytes 16777216 | tf_op jit(solution)/shard_map/all_to_all | solution.py:696
  111.9 3.7 %all-to-all-start.1 = ((f32[16,208,128]{2,1,0:T(8,128)}), f32[16,208,128]{2,1,0:T(8,128)S(1)}, u32[]{:S(2)}, u32[]{:S(2)}) async-start(f32[16,208,128]{2,1,0:T(8,128)} %get-tuple-element.13), calls=%async_computation.1 | async-start | bytes 3407872 | tf_op jit(solution)/shard_map/all_to_all | solution.py:698
  115.6 1.5 cut_columns.1
  117.1 0.0 copy-start.1
  117.1 22.3 %link_first.1 = (f32[2048,128]{1,0:T(8,128)}, f32[2,16,16,256]{3,2,1,0:T(8,128)}) custom-call(f32[16,1024,128]{2,1,0:T(8,128)} %all_to_all.10.in_ref.msg.below_msg, f32[16,1024,128]{2,1,0:T(8,128)} %all_to_all.10.in_ref.msg.below_msg, f32[6,256,256]{2,1,0:T(8,128)} %constant.4.clone.table), custom_call_target="tpu_custom_call" | custom-call | flops 1000000000 | bytes 10000000 | tf_op jit(solution)/shard_map/link_first/pallas_call | solution.py:632
  139.4 0.0 copy-done.1
  139.4 16.3 %all-gather = f32[128,8,128]{2,1,0:T(8,128)} all-gather(f32[16,8,128]{2,1,0:T(8,128)S(1)} %copy-done.1), channel_id=2, replica_groups=mesh['row'=16,'col'=8] {'col'}, dimensions={0}, use_global_device_ids=true | all-gather | bytes 589824 | tf_op jit(solution)/shard_map/all_gather | solution.py:700
  155.8 0.0 all-to-all-done.1.msg
  155.8 0.0 copy-start
  155.8 1.2 copy-done
  157.0 7.4 %link_last.1 = f32[2,16,16,256]{3,2,1,0:T(8,128)} custom-call(f32[16,208,128]{2,1,0:T(8,128)} %copy-done, f32[8,16,8,128]{3,2,1,0:T(8,128)} %bitcast.2, f32[6,256,256]{2,1,0:T(8,128)} %constant.4.clone.table, f32[16,128]{1,0:T(8,128)} %constant.5.clone.pool, f32[2048,128]{1,0:T(8,128)} %get-tuple-element.15.partial_hbm, ...), custom_call_target="tpu_custom_call" | custom-call | flops 100000000 | bytes 10000000 | tf_op jit(solution)/shard_map/link_last/pallas_call | solution.py:659
Async XLA Ops:
  111.9 43.9 %all-to-all-start.1 = ((f32[16,208,128]{2,1,0:T(8,128)}), f32[16,208,128]{2,1,0:T(8,128)S(1)}, u32[]{:S(2)}, u32[]{:S(2)}) async-start(f32[16,208,128]{2,1,0:T(8,128)} %get-tuple-element.13), calls=%async_computation.1 | async-start | bytes 3407872 | tf_op jit(solution)/shard_map/all_to_all | solution.py:698
  117.1 22.3 %copy-start.1 = (f32[16,8,128]{2,1,0:T(8,128)S(1)}, f32[16,8,128]{2,1,0:T(8,128)}, u32[]{:S(2)}) copy-start(f32[16,8,128]{2,1,0:T(8,128)} %cut_columns.1) | copy-start | bytes 196612
  155.8 1.2 copy-start

commit v7 on v6

--- a/solution.py
+++ b/solution.py
@@ -338,7 +338,8 @@
         sums[date, pl.ds(96, 96), :] = a - b
         return carry
 
-    lax.fori_loop(0, DATES, fill, 0, unroll=2)
+    for date in range(DATES):
+        fill(date, 0)
 
 
 def halo_products(small, side_lhs):
@@ -358,8 +359,12 @@
     return pl.ds(chunk * CHUNK, CHUNK)
 
 
+def done_rows(part, date, mt):
+    return pl.ds(FIELDS * 8 + ((part * DATES + date) * 2 + mt) * BLOCKS, BLOCKS)
+
+
 def first_kernel(
-    msg, below_msg, table, part_out, out, sums, lhs, small, side_lhs, res, halo, coh, vec, weight,
+    msg, below_msg, table, part_out, sums, lhs, small, side_lhs, res, halo, coh, vec, weight,
     rows, weights,
 ):
     step = pl.program_id(0)
@@ -368,13 +373,13 @@
     for date in range(DATES):
         for row in range(10):
             small[row, date : date + 1, :] = below_msg[date, pl.ds(step * 10 + row, 1), :]
+
+    def pooled(chunk):
+        res[step, chunk_rows(chunk), :] = dot(lhs[chunk_rows(chunk), :], weights[...])
+
+    main_products(msg, sums, lhs, pooled)
     halo_products(small, side_lhs)
     halo[step] = pool_side(side_lhs, weights[...])
-
-    def pooled(chunk):
-        res[step, chunk_rows(chunk), :] = dot(lhs[chunk_rows(chunk), :], weights[...])
-
-    main_products(msg, sums, lhs, pooled)
 
     @pl.when(step == FIRST - 1)
     def _():
@@ -425,33 +430,28 @@
                 value = vec[part, date]
                 rows[part, date, 1, pl.ds(0, 8, stride=2), :] = value
                 rows[part, date, 1, pl.ds(1, 8, stride=2), :] = pltpu.roll(value, 64, 1)
-        out[:, :, :, 0:128] = rows[:, :, 0]
-        left = lax.broadcasted_iota(jnp.int32, (2, DATES, BLOCKS, 128), 3) < 32
-        out[:, :, :, 128:256] = jnp.where(left, rows[:, :, 0], rows[:, :, 1])
+        left = lax.broadcasted_iota(jnp.int32, (BLOCKS, 128), 1) < 32
+        for part in range(2):
+            for date in range(DATES):
+                one, two = rows[part, date, 0], rows[part, date, 1]
+                part_out[done_rows(part, date, 0), :] = one
+                part_out[done_rows(part, date, 1), :] = jnp.where(left, one, two)
 
 
 def last_kernel(
-    msg, beside_msg, table, pool, partial_hbm, done_hbm, out, sums, lhs, small, side_lhs, res, halo,
-    pairs, edge, coh, vec, weight, rows, weights, partial, done, sems,
+    msg, left, right, table, pool, partial_hbm, out, sums, lhs, small, side_lhs, res, halo,
+    pairs, edge, coh, vec, weight, rows, weights, partial, sem,
 ):
-    copies = [
-        pltpu.make_async_copy(partial_hbm, partial, sems.at[0]),
-        pltpu.make_async_copy(done_hbm, done, sems.at[1]),
-    ]
-    for copy in copies:
-        copy.start()
-    col = lax.axis_index("col")
-    cols = beside_msg.shape[0]
+    copy = pltpu.make_async_copy(partial_hbm, partial, sem)
+    copy.start()
     fill_sums(msg, sums)
     for date in range(DATES):
         for row in range(10):
             small[row, date : date + 1, :] = msg[date, HALO2 + row : HALO2 + row + 1, :]
         for part in range(2):
             own = OWN_ROW - OWN_TILE + part
-            before = beside_msg[jnp.maximum(col - 1, 0), date, own + 2 : own + 3, :]
-            after = beside_msg[jnp.minimum(col + 1, cols - 1), date, own : own + 1, :]
-            small[10 + part, date : date + 1, :] = jnp.where(col > 0, before, 0.0)
-            small[12 + part, date : date + 1, :] = jnp.where(col < cols - 1, after, 0.0)
+            small[10 + part, date : date + 1, :] = left[date, own + 2 : own + 3, :]
+            small[12 + part, date : date + 1, :] = right[date, own : own + 1, :]
     halo_products(small, side_lhs)
     weights[...] = table[0].astype(jnp.bfloat16)
     halo[...] = pool_side(side_lhs, weights[...])
@@ -485,8 +485,7 @@
     last = lax.broadcasted_iota(jnp.int32, (8, 128), 0) == 7
     even = (lane < 32) | (lane >= 96)
     beside = (lane == 0) | (lane == 127) | (lane == 63) | (lane == 64)
-    for copy in copies:
-        copy.wait()
+    copy.wait()
 
     def cov(t, u, part):
         field = field_of(t, u) + part
@@ -503,9 +502,14 @@
             value = vec[part, date]
             rows[part, date, 0, pl.ds(0, 8, stride=2), :] = value
             rows[part, date, 0, pl.ds(1, 8, stride=2), :] = pltpu.roll(value, 64, 1)
-    place = lax.broadcasted_iota(jnp.int32, (2, DATES, BLOCKS, 128), 3)
-    out[:, :, :, 0:128] = jnp.where(place < 32, rows[:, :, 0], done[:, :, :, 0:128])
-    out[:, :, :, 128:256] = jnp.where(place >= 96, rows[:, :, 0], done[:, :, :, 128:256])
+    place = lax.broadcasted_iota(jnp.int32, (BLOCKS, 128), 1)
+    for part in range(2):
+        for date in range(DATES):
+            own = rows[part, date, 0]
+            for mt, mine in ((0, place < 32), (1, place >= 96)):
+                out[part, date, :, mt * 128 : mt * 128 + 128] = jnp.where(
+                    mine, own, partial[done_rows(part, date, mt), :]
+                )
 
 
 def inverse_norm(vec):
@@ -583,7 +587,7 @@
             vec[2, t] = real + imag
         return carry
 
-    lax.fori_loop(0, ITERS - 1, iterate, 0)
+    lax.fori_loop(0, ITERS - 1, iterate, 0, unroll=3)
     scale = inverse_norm(vec)
     for t in range(DATES):
         for part in range(2):
@@ -609,7 +613,7 @@
     pltpu.VMEM((DATES, 8, 128), jnp.float32),
 ]
 LINKED = (2, DATES, BLOCKS, OUT_COLS)
-PARTIAL = (FIELDS * 8, 128)
+PARTIAL = (FIELDS * 8 + 2 * DATES * 2 * BLOCKS, 128)
 
 
 def cut_kernel(in_ref, out_ref):
@@ -637,11 +641,8 @@
             pl.BlockSpec((DATES, 64, 128), lambda i: (0, HALO1 // 64, 0)),
             pl.BlockSpec((1, 256, 256), lambda i: (i, 0, 0)),
         ],
-        out_specs=[whole(*PARTIAL), whole(*LINKED)],
-        out_shape=[
-            jax.ShapeDtypeStruct(PARTIAL, jnp.float32),
-            jax.ShapeDtypeStruct(LINKED, jnp.float32),
-        ],
+        out_specs=whole(*PARTIAL),
+        out_shape=jax.ShapeDtypeStruct(PARTIAL, jnp.float32),
         scratch_shapes=common_scratch(10)
         + [
             pltpu.VMEM((FIRST, FIELDS * 16, 256), jnp.float32),
@@ -655,16 +656,16 @@
     )(message, message, tables)
 
 
-def link_last(message, beside, tables, pool, partial, done):
+def link_last(message, left, right, tables, pool, partial):
     return pl.pallas_call(
         last_kernel,
         grid=(1,),
         in_specs=[
             whole(DATES, ROWS2, 128),
-            whole(*beside.shape),
-            pl.BlockSpec((1, 256, 128), lambda i: (FIRST, 0, 0)),
+            whole(DATES, 8, 128),
+            whole(DATES, 8, 128),
+            whole(1, 256, 128),
             whole(16, 128),
-            pl.BlockSpec(memory_space=pl.ANY),
             pl.BlockSpec(memory_space=pl.ANY),
         ],
         out_specs=whole(*LINKED),
@@ -681,27 +682,30 @@
             pltpu.VMEM((2, DATES, 1, BLOCKS, 128), jnp.float32),
             pltpu.VMEM((256, 128), jnp.bfloat16),
             pltpu.VMEM(PARTIAL, jnp.float32),
-            pltpu.VMEM(LINKED, jnp.float32),
-            pltpu.SemaphoreType.DMA((2,)),
+            pltpu.SemaphoreType.DMA,
         ],
-        compiler_params=pltpu.CompilerParams(vmem_limit_bytes=GRANT),
+        compiler_params=pltpu.CompilerParams(vmem_limit_bytes=24 * 1024 * 1024),
         cost_estimate=pl.CostEstimate(flops=10**8, bytes_accessed=10**7, transcendentals=0),
         name="link_last",
-    )(message, beside, tables, pool, partial, done)
+    )(message, left, right, tables, pool, partial)
 
 
 def local(slc, valid_rows):
     valid = valid_rows.T
+    size = lax.axis_size("col")
+    up = [(i, i + 1) for i in range(size - 1)]
+    down = [(i + 1, i) for i in range(size - 1)]
     message1, message2 = pack(slc, valid)
     received1 = lax.all_to_all(message1, "row", 0, 0, tiled=True)
     received1, message2 = lax.optimization_barrier((received1, message2))
     received2 = lax.all_to_all(message2, "row", 0, 0, tiled=True)
     own = cut_columns(received1)
-    beside = lax.all_gather(own, "col")
+    left = lax.ppermute(own, "col", up)
+    right = lax.ppermute(own, "col", down)
     tables, pool = column_tables()
-    tables = jnp.asarray(tables)
-    partial, done = link_first(received1, tables)
-    return link_last(received2, beside, tables, jnp.asarray(pool), partial, done)
+    last_table = jnp.asarray(tables[FIRST:, :, 0:128])
+    partial = link_first(received1, jnp.asarray(tables))
+    return link_last(received2, left, right, last_table, jnp.asarray(pool), partial)
 
 
 def solution(mesh):

time: 165 us -> 153 us (0.927)
  blocking collectives: 120 us -> 103 us
  starting transfers between devices: 3.71 us -> 10.7 us
  Pallas kernels: 39.6 us -> 37.3 us
    all_gather x1 -> x0, blocking collectives: 16.3 us -> none  [local(): beside = lax.all_gather(own, 'col')]
    ppermute x0 -> x2, starting transfers between devices: none -> 7.02 us  [the longest x1 4.01 us: local(): right = lax.ppermute(own, 'col', down)]
    pallas_call x1, Pallas kernels: 7.43 us -> 5.75 us  [link_last(): pl.pallas_call(last_kernel, grid=(1,), in_specs=[whole(DATES, ROWS2, 128)...]
  transfers between devices with their start and end apart: 1 -> 3, of which waited for: 0 -> 0; matrix products, arithmetic and copies ran while one was open for 0% -> 0% of each run, Pallas kernels for 14% -> 15%
where the time goes in v7:
time: 153 us
  blocking collectives  103 us (67%)
  Pallas kernels  37.3 us (24%)
  starting transfers between devices  10.7 us (7%)
    all_to_all x1, blocking collectives, local(): received1 = lax.all_to_all(message1, 'row', 0, 0, tiled=True)  103 us
    pallas_call x1, Pallas kernels, link_first(): pl.pallas_call(first_kernel, grid=(FIRST,), in_specs=[pl.BlockSpec((DATES...  21.7 us
    pallas_call x1, Pallas kernels, pack(): pl.pallas_call(pack_kernel, in_specs=[pl.BlockSpec(memory_space=pltpu.SME...  8.38 us
    pallas_call x1, Pallas kernels, link_last(): pl.pallas_call(last_kernel, grid=(1,), in_specs=[whole(DATES, ROWS2, 128)...  5.75 us
    ppermute x1, starting transfers between devices, local(): right = lax.ppermute(own, 'col', down)  4.01 us
    all_to_all x1, starting transfers between devices, local(): received2 = lax.all_to_all(message2, 'row', 0, 0, tiled=True)  3.71 us
  transfers between devices with their start and end apart: 3, of which 0 were waited for; matrix products, arithmetic and copies ran while one was open for 0% of the time, Pallas kernels for 15%

profile of v7, /device:TPU:1, one launch (start us, length us, event | category | flops | bytes accessed | tf_op | source)
XLA Modules:
  0.0 153.0 jit_solution(8557396446191826673)
XLA Ops:
  0.0 8.4 %pack.1 = (f32[16,1024,128]{2,1,0:T(8,128)}, f32[16,208,128]{2,1,0:T(8,128)}) custom-call(s32[2,16]{1,0:T(2,128)} %bitcast.1, f32[2,1,1536,768]{3,2,1,0:T(8,128)} %slc.1), custom_call_target="tpu_custom_call" | custom-call | flops 1000000 | bytes 20000000 | tf_op jit(solution)/shard_map/pack/pallas_call | solution.py:196
  8.4 103.5 %all_to_all.10.in_ref.msg.below_msg = f32[16,1024,128]{2,1,0:T(8,128)} all-to-all(f32[16,1024,128]{2,1,0:T(8,128)} %get-tuple-element.9), channel_id=1, replica_groups=mesh['row'=16,'col'=8] {'row'}, dimensions={0} | all-to-all | bytes 16777216 | tf_op jit(solution)/shard_map/all_to_all | solution.py:699
  111.9 3.7 %all-to-all-start.1 = ((f32[16,208,128]{2,1,0:T(8,128)}), f32[16,208,128]{2,1,0:T(8,128)S(1)}, u32[]{:S(2)}, u32[]{:S(2)}) async-start(f32[16,208,128]{2,1,0:T(8,128)} %get-tuple-element.11), calls=%async_computation.1 | async-start | bytes 3407872 | tf_op jit(solution)/shard_map/all_to_all | solution.py:701
  115.6 1.5 cut_columns.1
  117.1 0.0 copy-start.1
  117.1 0.0 copy-start.2
  117.1 4.0 %collective-permute-start.1 = (f32[16,8,128]{2,1,0:T(8,128)}, f32[16,8,128]{2,1,0:T(8,128)S(1)}, u32[]{:S(2)}, u32[]{:S(2)}) collective-permute-start(f32[16,8,128]{2,1,0:T(8,128)} %cut_columns.1), channel_id=1, source_target_pairs={{1,0},{2,1},{3,2},{4,3},{5,4},{6,5},{7,6},{9,8},{10,9},{11,10},{12... | collective-permute-start | bytes 196616 | tf_op jit(solution)/shard_map/ppermute | solution.py:704
  121.1 3.0 %collective-permute-start = (f32[16,8,128]{2,1,0:T(8,128)}, f32[16,8,128]{2,1,0:T(8,128)S(1)}, u32[]{:S(2)}, u32[]{:S(2)}) collective-permute-start(f32[16,8,128]{2,1,0:T(8,128)} %cut_columns.1), channel_id=1, source_target_pairs={{0,1},{1,2},{2,3},{3,4},{4,5},{5,6},{6,7},{8,9},{9,10},{10,11},{11... | collective-permute-start | bytes 196616 | tf_op jit(solution)/shard_map/ppermute | solution.py:703
  124.1 21.7 %link_first.1.partial_hbm = f32[3072,128]{1,0:T(8,128)} custom-call(f32[16,1024,128]{2,1,0:T(8,128)} %all_to_all.10.in_ref.msg.below_msg, f32[16,1024,128]{2,1,0:T(8,128)} %all_to_all.10.in_ref.msg.below_msg, f32[6,256,256]{2,1,0:T(8,128)} %constant.7.clone.table), custom_call_target="tpu_custom_call" | custom-call | flops 1000000000 | bytes 10000000 | tf_op jit(solution)/shard_map/link_first/pallas_call | solution.py:636
  145.8 0.0 collective-permute-done.1.right
  145.8 0.0 collective-permute-done.left
  145.8 0.0 all-to-all-done.1.msg
  145.8 0.0 copy-done.1
  145.8 0.0 copy-done.2
  145.8 0.0 copy-start
  145.9 1.4 copy-done
  147.3 5.8 %link_last.1 = f32[2,16,16,256]{3,2,1,0:T(8,128)} custom-call(f32[16,208,128]{2,1,0:T(8,128)S(1)} %all-to-all-done.1.msg, f32[16,8,128]{2,1,0:T(8,128)S(1)} %collective-permute-done.left, f32[16,8,128]{2,1,0:T(8,128)S(1)} %collective-permute-done.1.right, f32[1,256,128]{2,1,0:T(8,128)S(1)} %copy-done.1, f32[16,128]{1,0:T(8,128)S(1)} %copy-done.2, ...), custom_call_target="tpu_custom_call" | custom-call | flops 100000000 | bytes 10000000 | tf_op jit(solution)/shard_map/link_last/pallas_call | solution.py:660
Async XLA Ops:
  111.9 33.9 %all-to-all-start.1 = ((f32[16,208,128]{2,1,0:T(8,128)}), f32[16,208,128]{2,1,0:T(8,128)S(1)}, u32[]{:S(2)}, u32[]{:S(2)}) async-start(f32[16,208,128]{2,1,0:T(8,128)} %get-tuple-element.11), calls=%async_computation.1 | async-start | bytes 3407872 | tf_op jit(solution)/shard_map/all_to_all | solution.py:701
  117.1 28.8 %copy-start.1 = (f32[1,256,128]{2,1,0:T(8,128)S(1)}, f32[1,256,128]{2,1,0:T(8,128)}, u32[]{:S(2)}) copy-start(f32[1,256,128]{2,1,0:T(8,128)} %constant.6.clone.table) | copy-start | bytes 393220
  117.1 28.8 %copy-start.2 = (f32[16,128]{1,0:T(8,128)S(1)}, f32[16,128]{1,0:T(8,128)}, u32[]{:S(2)}) copy-start(f32[16,128]{1,0:T(8,128)} %constant.8.clone.pool) | copy-start | bytes 24580
  117.1 28.7 %collective-permute-start.1 = (f32[16,8,128]{2,1,0:T(8,128)}, f32[16,8,128]{2,1,0:T(8,128)S(1)}, u32[]{:S(2)}, u32[]{:S(2)}) collective-permute-start(f32[16,8,128]{2,1,0:T(8,128)} %cut_columns.1), channel_id=1, source_target_pairs={{1,0},{2,1},{3,2},{4,3},{5,4},{6,5},{7,6},{9,8},{10,9},{11,10},{12... | collective-permute-start | bytes 196616 | tf_op jit(solution)/shard_map/ppermute | solution.py:704
  121.1 24.7 %collective-permute-start = (f32[16,8,128]{2,1,0:T(8,128)}, f32[16,8,128]{2,1,0:T(8,128)S(1)}, u32[]{:S(2)}, u32[]{:S(2)}) collective-permute-start(f32[16,8,128]{2,1,0:T(8,128)} %cut_columns.1), channel_id=1, source_target_pairs={{0,1},{1,2},{2,3},{3,4},{4,5},{5,6},{6,7},{8,9},{9,10},{10,11},{11... | collective-permute-start | bytes 196616 | tf_op jit(solution)/shard_map/ppermute | solution.py:703
  145.8 1.4 copy-start

commit v8 on v7

--- a/solution.py
+++ b/solution.py
@@ -212,7 +212,7 @@
             pltpu.SemaphoreType.DMA((PIECES,)),
             pltpu.SemaphoreType.DMA((2, TILES)),
         ],
-        compiler_params=pltpu.CompilerParams(vmem_limit_bytes=GRANT),
+        compiler_params=pltpu.CompilerParams(vmem_limit_bytes=42 * 1024 * 1024),
         cost_estimate=pl.CostEstimate(flops=10**6, bytes_accessed=2 * 10**7, transcendentals=0),
         name="pack",
     )(valid, slc)
@@ -616,17 +616,19 @@
 PARTIAL = (FIELDS * 8 + 2 * DATES * 2 * BLOCKS, 128)
 
 
-def cut_kernel(in_ref, out_ref):
-    out_ref[...] = in_ref[...]
+def cut_kernel(in_ref, out_ref, sem):
+    copy = pltpu.make_async_copy(in_ref.at[:, pl.ds(OWN_TILE, 8), :], out_ref, sem)
+    copy.start()
+    copy.wait()
 
 
 def cut_columns(message):
     return pl.pallas_call(
         cut_kernel,
-        grid=(1,),
-        in_specs=[pl.BlockSpec((DATES, 8, 128), lambda i: (0, OWN_TILE // 8, 0))],
-        out_specs=whole(DATES, 8, 128),
+        in_specs=[pl.BlockSpec(memory_space=pl.ANY)],
+        out_specs=pl.BlockSpec(memory_space=pl.ANY),
         out_shape=jax.ShapeDtypeStruct((DATES, 8, 128), jnp.float32),
+        scratch_shapes=[pltpu.SemaphoreType.DMA],
         compiler_params=pltpu.CompilerParams(vmem_limit_bytes=GRANT),
         name="cut_columns",
     )(message)

time: 153 us -> 155 us (1.013)
    pallas_call x1, Pallas kernels: 1.47 us -> 3.1 us  [cut_columns(): pl.pallas_call(cut_kernel, in_specs=[pl.BlockSpec(memory_space=pl.ANY)],...]
  transfers between devices with their start and end apart: 3 -> 3, of which waited for: 0 -> 0; matrix products, arithmetic and copies ran while one was open for 0% -> 0% of each run, Pallas kernels for 15% -> 16%
where the time goes in v8:
time: 155 us
  blocking collectives  103 us (66%)
  Pallas kernels  38.6 us (25%)
  starting transfers between devices  10.7 us (7%)
  local copies, waits for them, and re-layouts  2.09 us (1%)
    all_to_all x1, blocking collectives, local(): received1 = lax.all_to_all(message1, 'row', 0, 0, tiled=True)  103 us
    pallas_call x1, Pallas kernels, link_first(): pl.pallas_call(first_kernel, grid=(FIRST,), in_specs=[pl.BlockSpec((DATES...  21.7 us
    pallas_call x1, Pallas kernels, pack(): pl.pallas_call(pack_kernel, in_specs=[pl.BlockSpec(memory_space=pltpu.SME...  8.02 us
    pallas_call x1, Pallas kernels, link_last(): pl.pallas_call(last_kernel, grid=(1,), in_specs=[whole(DATES, ROWS2, 128)...  5.75 us
    ppermute x1, starting transfers between devices, local(): right = lax.ppermute(own, 'col', down)  4.02 us
    all_to_all x1, starting transfers between devices, local(): received2 = lax.all_to_all(message2, 'row', 0, 0, tiled=True)  3.71 us
  transfers between devices with their start and end apart: 3, of which 0 were waited for; matrix products, arithmetic and copies ran while one was open for 0% of the time, Pallas kernels for 16%

profile of v8, /device:TPU:1, one launch (start us, length us, event | category | flops | bytes accessed | tf_op | source)
XLA Modules:
  0.0 154.8 jit_solution(10441750295120655224)
XLA Ops:
  0.0 0.0 copy-start.3
  0.0 0.7 copy-done.3
  0.7 8.0 %pack.1 = (f32[16,1024,128]{2,1,0:T(8,128)S(1)}, f32[16,208,128]{2,1,0:T(8,128)}) custom-call(s32[2,16]{1,0:T(2,128)S(1)} %bitcast.1, f32[2,1,1536,768]{3,2,1,0:T(8,128)} %slc.1), custom_call_target="tpu_custom_call" | custom-call | flops 1000000 | bytes 20000000 | tf_op jit(solution)/shard_map/pack/pallas_call | solution.py:196
  8.7 103.3 %all_to_all.10.in_ref.msg.below_msg = f32[16,1024,128]{2,1,0:T(8,128)} all-to-all(f32[16,1024,128]{2,1,0:T(8,128)S(1)} %get-tuple-element.9), channel_id=1, replica_groups=mesh['row'=16,'col'=8] {'row'}, dimensions={0} | all-to-all | bytes 16777216 | tf_op jit(solution)/shard_map/all_to_all | solution.py:701
  112.0 3.7 %all-to-all-start.1 = ((f32[16,208,128]{2,1,0:T(8,128)}), f32[16,208,128]{2,1,0:T(8,128)S(1)}, u32[]{:S(2)}, u32[]{:S(2)}) async-start(f32[16,208,128]{2,1,0:T(8,128)} %get-tuple-element.11), calls=%async_computation.1 | async-start | bytes 3407872 | tf_op jit(solution)/shard_map/all_to_all | solution.py:703
  115.7 3.1 %cut_columns.1 = f32[16,8,128]{2,1,0:T(8,128)} custom-call(f32[16,1024,128]{2,1,0:T(8,128)} %all_to_all.10.in_ref.msg.below_msg), custom_call_target="tpu_custom_call" | custom-call | tf_op jit(solution)/shard_map/cut_columns/pallas_call | solution.py:626
  118.8 0.0 copy-start.1
  118.8 0.0 copy-start.2
  118.8 4.0 %collective-permute-start.1 = (f32[16,8,128]{2,1,0:T(8,128)}, f32[16,8,128]{2,1,0:T(8,128)S(1)}, u32[]{:S(2)}, u32[]{:S(2)}) collective-permute-start(f32[16,8,128]{2,1,0:T(8,128)} %cut_columns.1), channel_id=1, source_target_pairs={{1,0},{2,1},{3,2},{4,3},{5,4},{6,5},{7,6},{9,8},{10,9},{11,10},{12... | collective-permute-start | bytes 196616 | tf_op jit(solution)/shard_map/ppermute | solution.py:706
  122.9 3.0 %collective-permute-start = (f32[16,8,128]{2,1,0:T(8,128)}, f32[16,8,128]{2,1,0:T(8,128)S(1)}, u32[]{:S(2)}, u32[]{:S(2)}) collective-permute-start(f32[16,8,128]{2,1,0:T(8,128)} %cut_columns.1), channel_id=1, source_target_pairs={{0,1},{1,2},{2,3},{3,4},{4,5},{5,6},{6,7},{8,9},{9,10},{10,11},{11... | collective-permute-start | bytes 196616 | tf_op jit(solution)/shard_map/ppermute | solution.py:705
  125.9 21.7 %link_first.1.partial_hbm = f32[3072,128]{1,0:T(8,128)} custom-call(f32[16,1024,128]{2,1,0:T(8,128)} %all_to_all.10.in_ref.msg.below_msg, f32[16,1024,128]{2,1,0:T(8,128)} %all_to_all.10.in_ref.msg.below_msg, f32[6,256,256]{2,1,0:T(8,128)} %constant.7.clone.table), custom_call_target="tpu_custom_call" | custom-call | flops 1000000000 | bytes 10000000 | tf_op jit(solution)/shard_map/link_first/pallas_call | solution.py:638
  147.6 0.0 collective-permute-done.1.right
  147.6 0.0 collective-permute-done.left
  147.6 0.0 all-to-all-done.1.msg
  147.6 0.0 copy-done.1
  147.6 0.0 copy-done.2
  147.6 0.0 copy-start
  147.6 1.4 copy-done
  149.0 5.8 %link_last.1 = f32[2,16,16,256]{3,2,1,0:T(8,128)} custom-call(f32[16,208,128]{2,1,0:T(8,128)S(1)} %all-to-all-done.1.msg, f32[16,8,128]{2,1,0:T(8,128)S(1)} %collective-permute-done.left, f32[16,8,128]{2,1,0:T(8,128)S(1)} %collective-permute-done.1.right, f32[1,256,128]{2,1,0:T(8,128)S(1)} %copy-done.1, f32[16,128]{1,0:T(8,128)S(1)} %copy-done.2, ...), custom_call_target="tpu_custom_call" | custom-call | flops 100000000 | bytes 10000000 | tf_op jit(solution)/shard_map/link_last/pallas_call | solution.py:662
Async XLA Ops:
  0.0 0.7 copy-start.3
  112.0 35.6 %all-to-all-start.1 = ((f32[16,208,128]{2,1,0:T(8,128)}), f32[16,208,128]{2,1,0:T(8,128)S(1)}, u32[]{:S(2)}, u32[]{:S(2)}) async-start(f32[16,208,128]{2,1,0:T(8,128)} %get-tuple-element.11), calls=%async_computation.1 | async-start | bytes 3407872 | tf_op jit(solution)/shard_map/all_to_all | solution.py:703
  118.8 28.8 %copy-start.1 = (f32[1,256,128]{2,1,0:T(8,128)S(1)}, f32[1,256,128]{2,1,0:T(8,128)}, u32[]{:S(2)}) copy-start(f32[1,256,128]{2,1,0:T(8,128)} %constant.6.clone.table) | copy-start | bytes 393220
  118.8 28.8 %copy-start.2 = (f32[16,128]{1,0:T(8,128)S(1)}, f32[16,128]{1,0:T(8,128)}, u32[]{:S(2)}) copy-start(f32[16,128]{1,0:T(8,128)} %constant.8.clone.pool) | copy-start | bytes 24580
  118.8 28.7 %collective-permute-start.1 = (f32[16,8,128]{2,1,0:T(8,128)}, f32[16,8,128]{2,1,0:T(8,128)S(1)}, u32[]{:S(2)}, u32[]{:S(2)}) collective-permute-start(f32[16,8,128]{2,1,0:T(8,128)} %cut_columns.1), channel_id=1, source_target_pairs={{1,0},{2,1},{3,2},{4,3},{5,4},{6,5},{7,6},{9,8},{10,9},{11,10},{12... | collective-permute-start | bytes 196616 | tf_op jit(solution)/shard_map/ppermute | solution.py:706
  122.9 24.7 %collective-permute-start = (f32[16,8,128]{2,1,0:T(8,128)}, f32[16,8,128]{2,1,0:T(8,128)S(1)}, u32[]{:S(2)}, u32[]{:S(2)}) collective-permute-start(f32[16,8,128]{2,1,0:T(8,128)} %cut_columns.1), channel_id=1, source_target_pairs={{0,1},{1,2},{2,3},{3,4},{4,5},{5,6},{6,7},{8,9},{9,10},{10,11},{11... | collective-permute-start | bytes 196616 | tf_op jit(solution)/shard_map/ppermute | solution.py:705
  147.6 1.4 copy-start

commit v9 on v7

--- a/solution.py
+++ b/solution.py
@@ -684,7 +684,7 @@
             pltpu.VMEM(PARTIAL, jnp.float32),
             pltpu.SemaphoreType.DMA,
         ],
-        compiler_params=pltpu.CompilerParams(vmem_limit_bytes=24 * 1024 * 1024),
+        compiler_params=pltpu.CompilerParams(vmem_limit_bytes=49 * 1024 * 1024),
         cost_estimate=pl.CostEstimate(flops=10**8, bytes_accessed=10**7, transcendentals=0),
         name="link_last",
     )(message, left, right, tables, pool, partial)

time: 153 us -> 153 us (level)
  no operation moved by 1% of the time
where the time goes in v9:
time: 153 us
  blocking collectives  103 us (67%)
  Pallas kernels  37.3 us (24%)
  starting transfers between devices  10.7 us (7%)
    all_to_all x1, blocking collectives, local(): received1 = lax.all_to_all(message1, 'row', 0, 0, tiled=True)  103 us
    pallas_call x1, Pallas kernels, link_first(): pl.pallas_call(first_kernel, grid=(FIRST,), in_specs=[pl.BlockSpec((DATES...  21.7 us
    pallas_call x1, Pallas kernels, pack(): pl.pallas_call(pack_kernel, in_specs=[pl.BlockSpec(memory_space=pltpu.SME...  8.38 us
    pallas_call x1, Pallas kernels, link_last(): pl.pallas_call(last_kernel, grid=(1,), in_specs=[whole(DATES, ROWS2, 128)...  5.75 us
    ppermute x1, starting transfers between devices, local(): right = lax.ppermute(own, 'col', down)  4.01 us
    all_to_all x1, starting transfers between devices, local(): received2 = lax.all_to_all(message2, 'row', 0, 0, tiled=True)  3.71 us
  transfers between devices with their start and end apart: 3, of which 0 were waited for; matrix products, arithmetic and copies ran while one was open for 0% of the time, Pallas kernels for 15%

profile of v9, /device:TPU:1, one launch (start us, length us, event | category | flops | bytes accessed | tf_op | source)
XLA Modules:
  0.0 153.0 jit_solution(8308496309531828987)
XLA Ops:
  0.0 8.4 %pack.1 = (f32[16,1024,128]{2,1,0:T(8,128)}, f32[16,208,128]{2,1,0:T(8,128)}) custom-call(s32[2,16]{1,0:T(2,128)} %bitcast.1, f32[2,1,1536,768]{3,2,1,0:T(8,128)} %slc.1), custom_call_target="tpu_custom_call" | custom-call | flops 1000000 | bytes 20000000 | tf_op jit(solution)/shard_map/pack/pallas_call | solution.py:196
  8.4 103.5 %all_to_all.10.in_ref.msg.below_msg = f32[16,1024,128]{2,1,0:T(8,128)} all-to-all(f32[16,1024,128]{2,1,0:T(8,128)} %get-tuple-element.9), channel_id=1, replica_groups=mesh['row'=16,'col'=8] {'row'}, dimensions={0} | all-to-all | bytes 16777216 | tf_op jit(solution)/shard_map/all_to_all | solution.py:699
  111.9 3.7 %all-to-all-start.1 = ((f32[16,208,128]{2,1,0:T(8,128)}), f32[16,208,128]{2,1,0:T(8,128)S(1)}, u32[]{:S(2)}, u32[]{:S(2)}) async-start(f32[16,208,128]{2,1,0:T(8,128)} %get-tuple-element.11), calls=%async_computation.1 | async-start | bytes 3407872 | tf_op jit(solution)/shard_map/all_to_all | solution.py:701
  115.6 1.5 cut_columns.1
  117.1 0.0 copy-start.1
  117.1 0.0 copy-start.2
  117.1 4.0 %collective-permute-start.1 = (f32[16,8,128]{2,1,0:T(8,128)}, f32[16,8,128]{2,1,0:T(8,128)S(1)}, u32[]{:S(2)}, u32[]{:S(2)}) collective-permute-start(f32[16,8,128]{2,1,0:T(8,128)} %cut_columns.1), channel_id=1, source_target_pairs={{1,0},{2,1},{3,2},{4,3},{5,4},{6,5},{7,6},{9,8},{10,9},{11,10},{12... | collective-permute-start | bytes 196616 | tf_op jit(solution)/shard_map/ppermute | solution.py:704
  121.1 3.0 %collective-permute-start = (f32[16,8,128]{2,1,0:T(8,128)}, f32[16,8,128]{2,1,0:T(8,128)S(1)}, u32[]{:S(2)}, u32[]{:S(2)}) collective-permute-start(f32[16,8,128]{2,1,0:T(8,128)} %cut_columns.1), channel_id=1, source_target_pairs={{0,1},{1,2},{2,3},{3,4},{4,5},{5,6},{6,7},{8,9},{9,10},{10,11},{11... | collective-permute-start | bytes 196616 | tf_op jit(solution)/shard_map/ppermute | solution.py:703
  124.1 21.7 %link_first.1.partial_hbm = f32[3072,128]{1,0:T(8,128)} custom-call(f32[16,1024,128]{2,1,0:T(8,128)} %all_to_all.10.in_ref.msg.below_msg, f32[16,1024,128]{2,1,0:T(8,128)} %all_to_all.10.in_ref.msg.below_msg, f32[6,256,256]{2,1,0:T(8,128)} %constant.7.clone.table), custom_call_target="tpu_custom_call" | custom-call | flops 1000000000 | bytes 10000000 | tf_op jit(solution)/shard_map/link_first/pallas_call | solution.py:636
  145.8 0.0 collective-permute-done.1.right
  145.8 0.0 collective-permute-done.left
  145.8 0.0 all-to-all-done.1.msg
  145.8 0.0 copy-done.1
  145.8 0.0 copy-done.2
  145.8 0.0 copy-start
  145.9 1.4 copy-done
  147.3 5.8 %link_last.1 = f32[2,16,16,256]{3,2,1,0:T(8,128)} custom-call(f32[16,208,128]{2,1,0:T(8,128)S(1)} %all-to-all-done.1.msg, f32[16,8,128]{2,1,0:T(8,128)S(1)} %collective-permute-done.left, f32[16,8,128]{2,1,0:T(8,128)S(1)} %collective-permute-done.1.right, f32[1,256,128]{2,1,0:T(8,128)S(1)} %copy-done.1, f32[16,128]{1,0:T(8,128)S(1)} %copy-done.2, ...), custom_call_target="tpu_custom_call" | custom-call | flops 100000000 | bytes 10000000 | tf_op jit(solution)/shard_map/link_last/pallas_call | solution.py:660
Async XLA Ops:
  111.9 33.9 %all-to-all-start.1 = ((f32[16,208,128]{2,1,0:T(8,128)}), f32[16,208,128]{2,1,0:T(8,128)S(1)}, u32[]{:S(2)}, u32[]{:S(2)}) async-start(f32[16,208,128]{2,1,0:T(8,128)} %get-tuple-element.11), calls=%async_computation.1 | async-start | bytes 3407872 | tf_op jit(solution)/shard_map/all_to_all | solution.py:701
  117.1 28.8 %copy-start.1 = (f32[1,256,128]{2,1,0:T(8,128)S(1)}, f32[1,256,128]{2,1,0:T(8,128)}, u32[]{:S(2)}) copy-start(f32[1,256,128]{2,1,0:T(8,128)} %constant.6.clone.table) | copy-start | bytes 393220
  117.1 28.8 %copy-start.2 = (f32[16,128]{1,0:T(8,128)S(1)}, f32[16,128]{1,0:T(8,128)}, u32[]{:S(2)}) copy-start(f32[16,128]{1,0:T(8,128)} %constant.8.clone.pool) | copy-start | bytes 24580
  117.1 28.7 %collective-permute-start.1 = (f32[16,8,128]{2,1,0:T(8,128)}, f32[16,8,128]{2,1,0:T(8,128)S(1)}, u32[]{:S(2)}, u32[]{:S(2)}) collective-permute-start(f32[16,8,128]{2,1,0:T(8,128)} %cut_columns.1), channel_id=1, source_target_pairs={{1,0},{2,1},{3,2},{4,3},{5,4},{6,5},{7,6},{9,8},{10,9},{11,10},{12... | collective-permute-start | bytes 196616 | tf_op jit(solution)/shard_map/ppermute | solution.py:704
  121.1 24.7 %collective-permute-start = (f32[16,8,128]{2,1,0:T(8,128)}, f32[16,8,128]{2,1,0:T(8,128)S(1)}, u32[]{:S(2)}, u32[]{:S(2)}) collective-permute-start(f32[16,8,128]{2,1,0:T(8,128)} %cut_columns.1), channel_id=1, source_target_pairs={{0,1},{1,2},{2,3},{3,4},{4,5},{5,6},{6,7},{8,9},{9,10},{10,11},{11... | collective-permute-start | bytes 196616 | tf_op jit(solution)/shard_map/ppermute | solution.py:703
  145.8 1.4 copy-start
